TPU v7x, 128 devices: a whole 4x4x4 slice. The times are simulated.
128 devices in a mesh: freq: 16 (over y, x_lo, core), panel: 8 (over x_hi, z).
Axes of the slice: x: 4 (x_hi: 2, x_lo: 2; x = x_hi * 2 + x_lo), y: 4, z: 4, core: 2. Of those that a mesh axis runs over, the one named last changes fastest.
Arguments:
- reflection: bfloat16 [2, 128, 2048, 2048], P(None, 'freq', None, 'panel'), may hold values from -0.1875 to 0.1875
- focus_init: float32 [512, 48, 2048], P('freq', None, 'panel'), may hold values from -6 to 6
- onsets: int32 [48, 2048], P(None, 'panel'), may hold values from 64 to 191
Outputs:
- focusing: float32 [512, 48, 2048], P('freq', None, 'panel')
- upgoing: float32 [512, 48, 2048], P('freq', None, 'panel')
All inputs are finite; a program needn't handle non-finite values.
Results may differ from a plain program's by a relative error of at most 0.023.
Values may be sent and summed in bfloat16 or wider, within the bound.
No kernel may reach another device: no remote copies, remote signals or barrier semaphores. Data moves between devices by JAX's collectives and lax.ppermute only.
A program may use at most 128 MiB of HBM per device.

v0:
```python
import math

import jax
import jax.numpy as jnp
from jax import lax
from jax.sharding import PartitionSpec as P

NT = 512
ITERS = 2


def band_tables(freq_count, time_count):
    harmonic = jnp.arange(1, freq_count + 1, dtype=jnp.int32)
    samples = jnp.arange(time_count, dtype=jnp.int32)
    phases = harmonic[:, None] * samples[None, :] % time_count
    angles = phases.astype(jnp.float32) * jnp.float32(2.0 * math.pi / time_count)
    factor = 1.0 / math.sqrt(time_count)
    cosines = jnp.stack([jnp.cos(angles), -jnp.sin(angles)], axis=1).reshape(
        2 * freq_count, time_count
    )
    forward = cosines * jnp.float32(factor)
    inverse = jnp.transpose(cosines) * jnp.float32(2.0 * factor)
    return (forward, inverse)


def local(reflection, focus_init, onsets):
    local_freqs = reflection.shape[1]
    freq_groups = lax.axis_size("freq")
    freq_count = local_freqs * freq_groups
    forward, inverse = band_tables(freq_count, NT)

    def transform(traces):
        spectra = jnp.dot(
            forward,
            traces.reshape(NT, -1),
            precision=lax.Precision.HIGHEST,
            preferred_element_type=jnp.float32,
        )
        return spectra.reshape(freq_count, 2, traces.shape[1], traces.shape[2])

    def synthesize(spectra):
        traces = jnp.dot(
            inverse,
            spectra.reshape(2 * freq_count, -1),
            precision=lax.Precision.HIGHEST,
            preferred_element_type=jnp.float32,
        )
        return traces.reshape(NT, spectra.shape[2], spectra.shape[3])

    def to_frequency(traces):
        spectra = transform(
            lax.all_to_all(
                traces.astype(jnp.bfloat16), "freq", split_axis=1, concat_axis=0, tiled=True
            ).astype(traces.dtype)
        )
        return lax.all_to_all(
            spectra.astype(jnp.bfloat16), "freq", split_axis=0, concat_axis=2, tiled=True
        )

    def to_samples(spectra):
        traces = synthesize(
            lax.all_to_all(
                spectra.astype(jnp.bfloat16), "freq", split_axis=2, concat_axis=0, tiled=True
            ).astype(spectra.dtype)
        )
        traces = lax.all_to_all(
            traces.astype(jnp.bfloat16), "freq", split_axis=0, concat_axis=1, tiled=True
        ).astype(traces.dtype)
        return traces

    time_share = NT // freq_groups
    samples = lax.axis_index("freq") * time_share + jnp.arange(time_share, dtype=jnp.int32)
    kept_mask = (samples[:, None, None] < onsets[None]) | (
        samples[:, None, None] > NT - onsets[None]
    )
    focusing = focus_init
    upgoing = focus_init
    for iteration in range(ITERS):
        focus_bands = to_frequency(focusing)
        image_products = jnp.einsum(
            "cjrs,jdvs->jcdvr", reflection, focus_bands, preferred_element_type=jnp.float32
        )
        image_real_part = image_products[:, 0, 0] - image_products[:, 1, 1]
        image_imag_part = image_products[:, 0, 1] + image_products[:, 1, 0]
        images = lax.psum_scatter(
            jnp.stack([image_real_part, image_imag_part], axis=1).astype(jnp.bfloat16),
            "panel",
            scatter_dimension=3,
            tiled=True,
        ).astype(jnp.float32)
        upgoing = jnp.where(kept_mask, to_samples(images), 0.0)
        upgoing_bands = to_frequency(upgoing)
        products = jnp.einsum(
            "cjrs,jdvr->jcdvs",
            reflection,
            lax.all_gather(upgoing_bands, "panel", axis=3, tiled=True),
            preferred_element_type=jnp.float32,
        )
        real_part = products[:, 0, 0] + products[:, 1, 1]
        imag_part = products[:, 0, 1] - products[:, 1, 0]
        returns = jnp.stack([real_part, imag_part], axis=1)
        focusing = focus_init + jnp.where(kept_mask, to_samples(returns), 0.0)
    return (focusing, upgoing)


def solution(mesh):
    placed = (P(None, "freq", None, "panel"), P("freq", None, "panel"), P(None, "panel"))
    return jax.shard_map(
        local,
        mesh=mesh,
        in_specs=placed,
        out_specs=(P("freq", None, "panel"), P("freq", None, "panel")),
        check_vma=False,
    )
```

profile of v0, /device:TPU:1, one launch (start us, length us, event | category | flops | bytes accessed | tf_op | source)
XLA Modules:
  0.0 646.7 jit_solution(398860679760530750)
XLA Ops:
  7.2 3.1 copy.365
  10.3 6.9 %all-to-all-start = ((bf16[32,48,256]{2,0,1:T(8,128)(2,1)}), bf16[32,48,256]{2,0,1:T(8,128)(2,1)S(1)}, u32[]{:S(2)}, u32[]{:S(2)}) async-start(bf16[32,48,256]{2,0,1:T(8,128)(2,1)} %copy.365), calls=%async_computation | async-start | bytes 1572864 | tf_op jit(solution)/shard_map/all_to_all | solution.py:52
  17.3 1.1 fusion.72
  18.4 11.8 %all-to-all-done = bf16[32,48,256]{2,0,1:T(8,128)(2,1)S(1)} async-done(((bf16[32,48,256]{2,0,1:T(8,128)(2,1)}), bf16[32,48,256]{2,0,1:T(8,128)(2,1)S(1)}, u32[]{:S(2)}, u32[]{:S(2)}) %all-to-all-start) | async-done | bytes 786464 | tf_op jit(solution)/shard_map/all_to_all | solution.py:52
  30.2 0.7 copy.217
  31.3 0.8 convolution_convert_fusion.7
  32.6 11.8 %all_to_all.228 = bf16[128,2,3,256]{3,1,2,0:T(2,128)(2,1)S(1)} all-to-all(bf16[128,2,3,256]{3,1,2,0:T(2,128)(2,1)S(1)} %copy.219), channel_id=1, replica_groups=mesh['freq'=16,'panel'=8] {'freq'}, dimensions={0} | all-to-all | bytes 786432 | tf_op jit(solution)/shard_map/all_to_all | solution.py:56
  44.4 11.3 %fusion.8 = f32[8,2,2,48,2048]{4,3,1,2,0:T(8,128)} fusion(bf16[8,2,48,256,1]{3,0,2,1,4:T(8,128)(2,1)S(1)} %bitcast.307, bf16[2,8,2048,256]{3,2,1,0:T(8,128)(2,1)} %param.3), kind=kOutput, calls=%fused_computation.8 | convolution fusion | flops 1610612736 | bytes 29753344 | tf_op jit(solution)/shard_map/cjrs,jdvs->jcdvr/dot_general | solution.py:80
  55.8 3.3 fusion.23
  59.0 3.3 fusion.22
  62.3 1.9 pad_maximum_fusion
  64.3 78.7 %reduce-scatter.3.cloned.1.call-done = bf16[8,2,48,256]{3,2,0,1:T(8,128)(2,1)} async-done(((bf16[8,2,48,2048]{3,2,0,1:T(8,128)(2,1)}), bf16[8,2,48,256]{3,2,0,1:T(8,128)(2,1)}) %reduce-scatter.3.cloned.1.call-update) | async-done | bytes 393232 | tf_op jit(solution)/shard_map/reduce_scatter | solution.py:85
  143.0 1.9 copy.226
  144.9 6.1 all-to-all-start.2
  151.8 7.6 %all-to-all-done.2 = bf16[8,2,48,256]{3,0,1,2:T(8,128)(2,1)S(1)} async-done(((bf16[8,2,48,256]{3,0,1,2:T(8,128)(2,1)}), bf16[8,2,48,256]{3,0,1,2:T(8,128)(2,1)S(1)}, u32[]{:S(2)}, u32[]{:S(2)}) %all-to-all-start.2) | async-done | bytes 393248 | tf_op jit(solution)/shard_map/all_to_all | solution.py:62
  159.9 1.5 convolution_convert_fusion.3
  161.4 1.6 copy.231
  163.0 5.1 all-to-all-start.3
  168.2 15.8 %all-to-all-done.3 = bf16[512,3,256]{2,1,0:T(4,128)(2,1)S(1)} async-done(((bf16[512,3,256]{2,1,0:T(4,128)(2,1)}), bf16[512,3,256]{2,1,0:T(4,128)(2,1)S(1)}, u32[]{:S(2)}, u32[]{:S(2)}) %all-to-all-start.3) | async-done | bytes 786464 | tf_op jit(solution)/shard_map/all_to_all | solution.py:66
  184.7 16.1 %all_to_all.229 = bf16[32,48,256]{2,0,1:T(8,128)(2,1)S(1)} all-to-all(bf16[32,48,256]{2,0,1:T(8,128)(2,1)S(1)} %fusion.29), channel_id=1, replica_groups=mesh['freq'=16,'panel'=8] {'freq'}, dimensions={1} | all-to-all | bytes 1572864 | tf_op jit(solution)/shard_map/all_to_all | solution.py:52
  200.8 0.7 copy.234
  202.0 0.8 convolution_convert_fusion.6
  203.2 11.9 %all_to_all.230 = bf16[128,2,3,256]{3,1,2,0:T(2,128)(2,1)S(1)} all-to-all(bf16[128,2,3,256]{3,1,2,0:T(2,128)(2,1)S(1)} %copy.236), channel_id=1, replica_groups=mesh['freq'=16,'panel'=8] {'freq'}, dimensions={0} | all-to-all | bytes 786432 | tf_op jit(solution)/shard_map/all_to_all | solution.py:56
  215.2 0.8 copy.239
  216.1 61.7 %all-gather.3.cloned.1.call-done = bf16[8,2,48,2048]{3,2,1,0:T(8,128)(2,1)} async-done(((bf16[8,2,48,256]{3,2,1,0:T(8,128)(2,1)}), bf16[8,2,48,2048]{3,2,1,0:T(8,128)(2,1)}) %all-gather.3.cloned.1.call-update) | async-done | bytes 3145744 | tf_op jit(solution)/shard_map/all_gather | solution.py:96
  277.8 8.2 %fusion.30 = f32[8,2,2,48,256]{4,3,1,2,0:T(8,128)S(1)} fusion(bf16[8,2,48,2048]{3,2,1,0:T(8,128)(2,1)} %all-gather.3.cloned.1.call-done, bf16[2,8,2048,256]{3,2,1,0:T(8,128)(2,1)} %param.3), kind=kOutput, calls=%fused_computation.43 | convolution fusion | flops 1610612736 | bytes 21495808 | tf_op jit(solution)/shard_map/cjrs,jdvr->jcdvs/dot_general | solution.py:93
  286.3 13.6 %all_to_all.231 = bf16[8,2,48,256]{3,0,1,2:T(8,128)(2,1)S(1)} all-to-all(bf16[8,2,48,256]{3,0,1,2:T(8,128)(2,1)S(1)} %copy.243), channel_id=1, replica_groups=mesh['freq'=16,'panel'=8] {'freq'}, dimensions={2} | all-to-all | bytes 786432 | tf_op jit(solution)/shard_map/all_to_all | solution.py:62
  300.4 1.5 convolution_convert_fusion.2
  301.9 0.7 copy.248
  302.6 19.1 %all_to_all.232 = bf16[512,3,256]{2,1,0:T(4,128)(2,1)S(1)} all-to-all(bf16[512,3,256]{2,1,0:T(4,128)(2,1)S(1)} %copy.248), channel_id=1, replica_groups=mesh['freq'=16,'panel'=8] {'freq'}, dimensions={0} | all-to-all | bytes 1572864 | tf_op jit(solution)/shard_map/all_to_all | solution.py:66
  322.2 1.2 copy-done
  323.4 1.3 fusion.28
  324.6 16.6 %all_to_all.233 = bf16[32,48,256]{2,0,1:T(8,128)(2,1)S(1)} all-to-all(bf16[32,48,256]{2,0,1:T(8,128)(2,1)S(1)} %fusion.28), channel_id=1, replica_groups=mesh['freq'=16,'panel'=8] {'freq'}, dimensions={1} | all-to-all | bytes 1572864 | tf_op jit(solution)/shard_map/all_to_all | solution.py:52
  341.3 0.7 copy.252
  342.1 1.2 copy.253
  343.3 2.0 convolution_convert_fusion.5
  345.7 11.9 %all_to_all.234 = bf16[128,2,3,256]{3,1,2,0:T(2,128)(2,1)S(1)} all-to-all(bf16[128,2,3,256]{3,1,2,0:T(2,128)(2,1)S(1)} %copy.254), channel_id=1, replica_groups=mesh['freq'=16,'panel'=8] {'freq'}, dimensions={0} | all-to-all | bytes 786432 | tf_op jit(solution)/shard_map/all_to_all | solution.py:56
  357.6 11.3 %fusion.11 = f32[8,2,2,48,2048]{4,3,1,2,0:T(8,128)} fusion(bf16[8,2,48,256,1]{3,0,2,1,4:T(8,128)(2,1)S(1)} %bitcast.308, bf16[2,8,2048,256]{3,2,1,0:T(8,128)(2,1)} %param.3), kind=kOutput, calls=%fused_computation.9 | convolution fusion | flops 1610612736 | bytes 29753344 | tf_op jit(solution)/shard_map/cjrs,jdvs->jcdvr/dot_general | solution.py:80
  369.0 3.3 fusion.25
  372.2 3.3 fusion.24
  375.5 1.9 pad_maximum_fusion.1
  377.5 75.4 %reduce-scatter.5.cloned.1.call-done = bf16[8,2,48,256]{3,2,0,1:T(8,128)(2,1)} async-done(((bf16[8,2,48,2048]{3,2,0,1:T(8,128)(2,1)}), bf16[8,2,48,256]{3,2,0,1:T(8,128)(2,1)}) %reduce-scatter.5.cloned.1.call-update) | async-done | bytes 393232 | tf_op jit(solution)/shard_map/reduce_scatter | solution.py:85
  452.9 1.1 copy.261
  454.0 14.3 %all_to_all.235 = bf16[8,2,48,256]{3,0,1,2:T(8,128)(2,1)S(1)} all-to-all(bf16[8,2,48,256]{3,0,1,2:T(8,128)(2,1)S(1)} %copy.261), channel_id=1, replica_groups=mesh['freq'=16,'panel'=8] {'freq'}, dimensions={2} | all-to-all | bytes 786432 | tf_op jit(solution)/shard_map/all_to_all | solution.py:62
  468.9 1.5 convolution_convert_fusion.1
  471.0 19.1 %all_to_all.236 = bf16[512,3,256]{2,1,0:T(4,128)(2,1)S(1)} all-to-all(bf16[512,3,256]{2,1,0:T(4,128)(2,1)S(1)} %copy.266), channel_id=1, replica_groups=mesh['freq'=16,'panel'=8] {'freq'}, dimensions={0} | all-to-all | bytes 1572864 | tf_op jit(solution)/shard_map/all_to_all | solution.py:66
  490.5 1.6 fusion.81
  492.1 16.6 %all_to_all.237 = bf16[32,48,256]{2,0,1:T(8,128)(2,1)S(1)} all-to-all(bf16[32,48,256]{2,0,1:T(8,128)(2,1)S(1)} %get-tuple-element.10), channel_id=1, replica_groups=mesh['freq'=16,'panel'=8] {'freq'}, dimensions={1} | all-to-all | bytes 1572864 | tf_op jit(solution)/shard_map/all_to_all | solution.py:52
  508.8 0.7 copy.269
  509.6 1.2 copy.270
  510.8 2.0 convolution_convert_fusion.4
  513.2 11.9 %all_to_all.238 = bf16[128,2,3,256]{3,1,2,0:T(2,128)(2,1)S(1)} all-to-all(bf16[128,2,3,256]{3,1,2,0:T(2,128)(2,1)S(1)} %copy.271), channel_id=1, replica_groups=mesh['freq'=16,'panel'=8] {'freq'}, dimensions={0} | all-to-all | bytes 786432 | tf_op jit(solution)/shard_map/all_to_all | solution.py:56
  525.2 0.8 copy.274
  526.0 61.8 %all-gather.5.cloned.1.call-done = bf16[8,2,48,2048]{3,2,1,0:T(8,128)(2,1)} async-done(((bf16[8,2,48,256]{3,2,1,0:T(8,128)(2,1)}), bf16[8,2,48,2048]{3,2,1,0:T(8,128)(2,1)}) %all-gather.5.cloned.1.call-update) | async-done | bytes 3145744 | tf_op jit(solution)/shard_map/all_gather | solution.py:96
  587.8 8.2 %fusion.35 = f32[8,2,2,48,256]{4,3,1,2,0:T(8,128)S(1)} fusion(bf16[8,2,48,2048]{3,2,1,0:T(8,128)(2,1)} %all-gather.5.cloned.1.call-done, bf16[2,8,2048,256]{3,2,1,0:T(8,128)(2,1)} %param.3), kind=kOutput, calls=%fused_computation.44 | convolution fusion | flops 1610612736 | bytes 21495808 | tf_op jit(solution)/shard_map/cjrs,jdvr->jcdvs/dot_general | solution.py:93
  596.3 13.6 %all_to_all.239 = bf16[8,2,48,256]{3,0,1,2:T(8,128)(2,1)S(1)} all-to-all(bf16[8,2,48,256]{3,0,1,2:T(8,128)(2,1)S(1)} %copy.278), channel_id=1, replica_groups=mesh['freq'=16,'panel'=8] {'freq'}, dimensions={2} | all-to-all | bytes 786432 | tf_op jit(solution)/shard_map/all_to_all | solution.py:62
  610.4 1.5 convolution_convert_fusion
  611.9 1.6 copy.283
  613.5 5.2 all-to-all-start.15
  618.8 2.1 copy.288
  620.9 14.0 %all-to-all-done.15 = bf16[512,3,256]{2,1,0:T(4,128)(2,1)} async-done(((bf16[512,3,256]{2,1,0:T(4,128)(2,1)}), bf16[512,3,256]{2,1,0:T(4,128)(2,1)}, u32[]{:S(2)}, u32[]{:S(2)}) %all-to-all-start.15) | async-done | bytes 786464 | tf_op jit(solution)/shard_map/all_to_all | solution.py:66
  634.8 1.3 copy.284
  636.5 1.3 fusion.26
  637.8 2.1 copy.287
  (69 shorter events, 9.3 us)
Async XLA Ops:
  10.3 19.9 %all-to-all-start = ((bf16[32,48,256]{2,0,1:T(8,128)(2,1)}), bf16[32,48,256]{2,0,1:T(8,128)(2,1)S(1)}, u32[]{:S(2)}, u32[]{:S(2)}) async-start(bf16[32,48,256]{2,0,1:T(8,128)(2,1)} %copy.365), calls=%async_computation | async-start | bytes 1572864 | tf_op jit(solution)/shard_map/all_to_all | solution.py:52
  17.2 125.8 %reduce-scatter.3.cloned.1.call-start = ((), (), s32[]{:S(2)}) async-start(), calls=%async_computation.18 | async-start | bytes 3538944 | tf_op jit(solution)/shard_map/reduce_scatter | solution.py:85
  144.9 14.5 %all-to-all-start.2 = ((bf16[8,2,48,256]{3,0,1,2:T(8,128)(2,1)}), bf16[8,2,48,256]{3,0,1,2:T(8,128)(2,1)S(1)}, u32[]{:S(2)}, u32[]{:S(2)}) async-start(bf16[8,2,48,256]{3,0,1,2:T(8,128)(2,1)} %copy.226), calls=%async_computation.3 | async-start | bytes 786432 | tf_op jit(solution)/shard_map/all_to_all | solution.py:62
  161.4 6.8 %copy-start.2 = (s32[48,256]{1,0:T(8,128)S(1)}, s32[48,256]{1,0:T(8,128)}, u32[]{:S(2)}) copy-start(s32[48,256]{1,0:T(8,128)} %param.5) | copy-start | bytes 147460
  163.0 21.0 %all-to-all-start.3 = ((bf16[512,3,256]{2,1,0:T(4,128)(2,1)}), bf16[512,3,256]{2,1,0:T(4,128)(2,1)S(1)}, u32[]{:S(2)}, u32[]{:S(2)}) async-start(bf16[512,3,256]{2,1,0:T(4,128)(2,1)} %copy.231), calls=%async_computation.4 | async-start | bytes 2097152 | tf_op jit(solution)/shard_map/all_to_all | solution.py:66
  168.1 109.7 %all-gather.3.cloned.1.call-start = ((), (), s32[]{:S(2)}) async-start(), calls=%async_computation.19 | async-start | bytes 3538944 | tf_op jit(solution)/shard_map/all_gather | solution.py:96
  216.1 236.8 %reduce-scatter.5.cloned.1.call-start = ((), (), s32[]{:S(2)}) async-start(), calls=%async_computation.20 | async-start | bytes 3538944 | tf_op jit(solution)/shard_map/reduce_scatter | solution.py:85
  322.0 1.4 copy-start
  377.5 210.4 %all-gather.5.cloned.1.call-start = ((), (), s32[]{:S(2)}) async-start(), calls=%async_computation.21 | async-start | bytes 3538944 | tf_op jit(solution)/shard_map/all_gather | solution.py:96
  611.9 6.9 %copy-start.1 = (f32[32,48,256]{2,0,1:T(8,128)S(1)}, f32[32,48,256]{2,0,1:T(8,128)}, u32[]{:S(2)}) copy-start(f32[32,48,256]{2,0,1:T(8,128)} %get-tuple-element.11) | copy-start | bytes 4718596
  613.5 21.3 %all-to-all-start.15 = ((bf16[512,3,256]{2,1,0:T(4,128)(2,1)}), bf16[512,3,256]{2,1,0:T(4,128)(2,1)}, u32[]{:S(2)}, u32[]{:S(2)}) async-start(bf16[512,3,256]{2,1,0:T(4,128)(2,1)} %copy.283), calls=%async_computation.17 | async-start | bytes 2097152 | tf_op jit(solution)/shard_map/all_to_all | solution.py:66
Sparse Core Ops, SparseCore 0:
  64.4 78.5 reduce-scatter.2
  216.2 61.5 all-gather.2
  377.6 75.2 reduce-scatter.4
  526.1 61.6 all-gather.4
where the time goes:
time: 656 us; the launch traced here: 647 us
  waiting for transfers between devices  327 us (50%)
  blocking collectives  177 us (27%)
  matrix products  50.4 us (8%)
  local copies, waits for them, and re-layouts  31.1 us (5%)
  starting transfers between devices  23.5 us (4%)
  other arithmetic  23.5 us (4%)
  between operations  14.6 us (2%)
    reduce_scatter x2, waiting for transfers between devices, local(): lax.psum_scatter(jnp.stack([image_real_part, image_imag_part], axis=1).as...  154 us
    all_gather x2, waiting for transfers between devices, local(): lax.all_gather(upgoing_bands, 'panel', axis=3, tiled=True)  124 us
    all_to_all x3, blocking collectives, to_frequency(): lax.all_to_all(traces.astype(jnp.bfloat16), 'freq', split_axis=1, concat_...  49.4 us
    all_to_all x4, blocking collectives, to_frequency(): lax.all_to_all(spectra.astype(jnp.bfloat16), 'freq', split_axis=0, concat...  47.5 us
    all_to_all x3, blocking collectives, to_samples(): lax.all_to_all(spectra.astype(jnp.bfloat16), 'freq', split_axis=2, concat...  41.5 us
    all_to_all x2, blocking collectives, to_samples(): lax.all_to_all(traces.astype(jnp.bfloat16), 'freq', split_axis=0, concat_...  38.2 us
    all_to_all x2, waiting for transfers between devices, to_samples(): lax.all_to_all(traces.astype(jnp.bfloat16), 'freq', split_axis=0, concat_...  29.8 us
    dot_general x2, matrix products, local(): jnp.einsum('cjrs,jdvs->jcdvr', reflection, focus_bands, preferred_element...  22.6 us
  transfers between devices with their start and end apart: 8, of which 8 were waited for; matrix products, arithmetic and copies ran while one was open for 1% of the time, Pallas kernels for 0%

commit v1 on v0

v1 whole, which is shorter than its diff:
```python
import math

import jax
import jax.numpy as jnp
import ml_dtypes
import numpy as np
from jax import lax
from jax.experimental import pallas as pl
from jax.experimental.pallas import tpu as pltpu
from jax.sharding import PartitionSpec as P

NT = 512
ITERS = 2
LIMIT = 40 * 1024 * 1024


def split_table(table):
    high = table.astype(ml_dtypes.bfloat16)
    low = (table - high.astype(np.float32)).astype(ml_dtypes.bfloat16)
    return high, low


def band_tables(freq_count, time_count):
    harmonic = np.arange(1, freq_count + 1)
    phases = harmonic[:, None] * np.arange(time_count)[None, :] % time_count
    angles = phases * (2.0 * math.pi / time_count)
    factor = 1.0 / math.sqrt(time_count)
    cosines = np.stack([np.cos(angles), -np.sin(angles)], axis=1).reshape(2 * freq_count, time_count)
    forward = (cosines * factor).astype(np.float32)
    inverse = (cosines.T * (2.0 * factor)).astype(np.float32)
    return split_table(forward), split_table(inverse)


def dot(a, b):
    return jnp.dot(a, b, preferred_element_type=jnp.float32)


def dot_nt(a, b):
    return lax.dot_general(a, b, (((1,), (1,)), ((), ())), preferred_element_type=jnp.float32)


def halves(x):
    high = x.astype(jnp.bfloat16)
    return high, (x - high.astype(jnp.float32)).astype(jnp.bfloat16)


def table_times(high_ref, low_ref, x):
    if x.dtype == jnp.bfloat16:
        return dot(high_ref[...], x) + dot(low_ref[...], x)
    high, low = halves(x)
    return dot(high_ref[...], high) + dot(low_ref[...], high) + dot(high_ref[...], low)


def pick(rows_ref, row, step, count):
    return jnp.concatenate(
        [rows_ref[h, pl.ds(row, count, stride=step), :] for h in range(rows_ref.shape[0])], axis=1
    )


def place(rows_ref, row, step, value):
    for h in range(rows_ref.shape[0]):
        rows_ref[h, pl.ds(row, value.shape[0], stride=step), :] = value[:, h * 128 : (h + 1) * 128]


def fill(rows_ref, blocks):
    flat = blocks.reshape(rows_ref.shape[1], -1).astype(jnp.float32)
    for h in range(rows_ref.shape[0]):
        rows_ref[h] = flat[:, h * 128 : (h + 1) * 128]


def emptied(rows_ref, out_ref):
    flat = jnp.concatenate([rows_ref[h].astype(jnp.bfloat16) for h in range(rows_ref.shape[0])], axis=1)
    out_ref[...] = flat.reshape(out_ref.shape)


def image_kernel(step, bands_ref, refl_ref, out_ref, rows, bands):
    count = rows.shape[1] // step
    freqs = step // 2

    @pl.when(pl.program_id(0) == 0)
    def _():
        fill(rows, bands_ref[...])
        for j in range(freqs):
            for c in range(2):
                bands[j, c * count : (c + 1) * count, :] = pick(rows, 2 * j + c, step, count).astype(jnp.bfloat16)

    for j in range(freqs):
        a = dot_nt(bands[j], refl_ref[0, j])
        b = dot_nt(bands[j], refl_ref[1, j])
        place(rows, 2 * j, step, a[:count] - b[count:])
        place(rows, 2 * j + 1, step, b[:count] + a[count:])
    emptied(rows, out_ref)


def image_blocks(bands, reflection, panels):
    groups, height, width = bands.shape
    _, freqs, receivers, sources = reflection.shape
    block = receivers // panels
    step = 2 * freqs
    return pl.pallas_call(
        lambda *refs: image_kernel(step, *refs),
        grid=(panels,),
        in_specs=[
            pl.BlockSpec((groups, height, width), lambda p: (0, 0, 0)),
            pl.BlockSpec((2, freqs, block, sources), lambda p: (0, 0, p, 0)),
        ],
        out_specs=pl.BlockSpec((groups, 1, height, block), lambda p: (0, p, 0, 0)),
        out_shape=jax.ShapeDtypeStruct((groups, panels, height, block), jnp.bfloat16),
        scratch_shapes=[
            pltpu.VMEM((width // 128, groups * height, 128), jnp.float32),
            pltpu.VMEM((freqs, 2 * groups * height // step, width), jnp.bfloat16),
        ],
        compiler_params=pltpu.CompilerParams(vmem_limit_bytes=LIMIT),
        name="image_blocks",
    )(bands, reflection)


def return_kernel(step, bands_ref, refl_ref, out_ref, rows, total):
    count = rows.shape[1] // step
    freqs = step // 2
    panel = pl.program_id(0)

    @pl.when(panel == 0)
    def _():
        total[...] = jnp.zeros_like(total)

    fill(rows, bands_ref[...])
    for j in range(freqs):
        both = jnp.concatenate([pick(rows, 2 * j, step, count), pick(rows, 2 * j + 1, step, count)], axis=0)
        both = both.astype(jnp.bfloat16)
        a = dot(both, refl_ref[0, j])
        b = dot(both, refl_ref[1, j])
        total[j, 0] += a[:count] + b[count:]
        total[j, 1] += a[count:] - b[:count]

    @pl.when(panel == pl.num_programs(0) - 1)
    def _():
        for j in range(freqs):
            for c in range(2):
                place(rows, 2 * j + c, step, total[j, c])
        emptied(rows, out_ref)


def return_blocks(bands, reflection):
    groups, panels, height, width = bands.shape
    _, freqs, _, sources = reflection.shape
    step = 2 * freqs
    return pl.pallas_call(
        lambda *refs: return_kernel(step, *refs),
        grid=(panels,),
        in_specs=[
            pl.BlockSpec((groups, 1, height, width), lambda p: (0, p, 0, 0)),
            pl.BlockSpec((2, freqs, width, sources), lambda p: (0, 0, p, 0)),
        ],
        out_specs=pl.BlockSpec((groups, height, sources), lambda p: (0, 0, 0)),
        out_shape=jax.ShapeDtypeStruct((groups, height, sources), jnp.bfloat16),
        scratch_shapes=[
            pltpu.VMEM((width // 128, groups * height, 128), jnp.float32),
            pltpu.VMEM((freqs, 2, groups * height // step, sources), jnp.float32),
        ],
        compiler_params=pltpu.CompilerParams(vmem_limit_bytes=LIMIT),
        name="return_blocks",
    )(bands, reflection)


def windowed(traces, onsets_ref):
    samples = lax.broadcasted_iota(jnp.int32, traces.shape, 0)
    onsets = onsets_ref[0]
    return jnp.where((samples < onsets) | (samples > NT - onsets), traces, 0.0)


def table_specs(tables):
    return [pl.BlockSpec(t.shape, lambda v: (0, 0)) for pair in tables for t in pair]


def flat_tables(tables):
    return [jnp.asarray(t) for pair in tables for t in pair]


def start_kernel(high, low, traces_ref, first_ref, out_ref):
    spectra = table_times(high, low, traces_ref[...].reshape(NT, -1))
    first_ref[0] = spectra
    out_ref[...] = spectra.astype(jnp.bfloat16).reshape(out_ref.shape)


def start_bands(traces, forward, rows):
    blocks, count, share, width = traces.shape
    height = blocks * rows
    return pl.pallas_call(
        start_kernel,
        grid=(count,),
        in_specs=table_specs([forward])
        + [pl.BlockSpec((blocks, 1, share, width), lambda v: (0, v, 0, 0))],
        out_specs=[
            pl.BlockSpec((1, height, width), lambda v: (v, 0, 0)),
            pl.BlockSpec((blocks, rows, width), lambda v: (0, v, 0)),
        ],
        out_shape=[
            jax.ShapeDtypeStruct((count, height, width), jnp.float32),
            jax.ShapeDtypeStruct((blocks, count * rows, width), jnp.bfloat16),
        ],
        compiler_params=pltpu.CompilerParams(vmem_limit_bytes=LIMIT),
        name="start_bands",
    )(*flat_tables([forward]), traces)


def upgoing_kernel(with_traces, ih, il, fh, fl, onsets_ref, parts_ref, *outs):
    groups, panels, rows, width = parts_ref.shape
    images = parts_ref[:, 0].astype(jnp.float32)
    for p in range(1, panels):
        images = images + parts_ref[:, p].astype(jnp.float32)
    traces = windowed(table_times(ih, il, images.reshape(groups * rows, width)), onsets_ref)
    spectra = table_times(fh, fl, traces).astype(jnp.bfloat16).reshape(groups, rows, width)
    for p in range(panels):
        outs[0][:, p] = spectra
    if with_traces:
        outs[1][...] = traces.astype(jnp.bfloat16).reshape(outs[1].shape)


def upgoing_blocks(parts, onsets, tables, rows, with_traces):
    groups, panels, height, width = parts.shape
    count = height // rows
    share = NT // groups
    block = pl.BlockSpec((groups, panels, rows, width), lambda v: (0, 0, v, 0))
    out_specs = [block]
    out_shape = [jax.ShapeDtypeStruct(parts.shape, jnp.bfloat16)]
    if with_traces:
        out_specs.append(pl.BlockSpec((groups, 1, share, width), lambda v: (0, v, 0, 0)))
        out_shape.append(jax.ShapeDtypeStruct((groups, count, share, width), jnp.bfloat16))
    return pl.pallas_call(
        lambda *refs: upgoing_kernel(with_traces, *refs),
        grid=(count,),
        in_specs=table_specs(tables) + [pl.BlockSpec((1, 1, width), lambda v: (v, 0, 0)), block],
        out_specs=out_specs,
        out_shape=out_shape,
        compiler_params=pltpu.CompilerParams(vmem_limit_bytes=LIMIT),
        name="upgoing_blocks",
    )(*flat_tables(tables), onsets, parts)


def focus_kernel(ih, il, fh, fl, onsets_ref, first_ref, returns_ref, out_ref):
    groups, rows, width = returns_ref.shape
    traces = windowed(table_times(ih, il, returns_ref[...].reshape(groups * rows, width)), onsets_ref)
    spectra = first_ref[0] + table_times(fh, fl, traces)
    out_ref[...] = spectra.astype(jnp.bfloat16).reshape(out_ref.shape)


def focus_blocks(returns, first, onsets, tables, rows):
    groups, height, width = returns.shape
    block = pl.BlockSpec((groups, rows, width), lambda v: (0, v, 0))
    return pl.pallas_call(
        focus_kernel,
        grid=(height // rows,),
        in_specs=table_specs(tables)
        + [
            pl.BlockSpec((1, 1, width), lambda v: (v, 0, 0)),
            pl.BlockSpec((1, groups * rows, width), lambda v: (v, 0, 0)),
            block,
        ],
        out_specs=block,
        out_shape=jax.ShapeDtypeStruct(returns.shape, jnp.bfloat16),
        compiler_params=pltpu.CompilerParams(vmem_limit_bytes=LIMIT),
        name="focus_blocks",
    )(*flat_tables(tables), onsets, first, returns)


def trace_kernel(ih, il, onsets_ref, returns_ref, out_ref):
    groups, rows, width = returns_ref.shape
    traces = windowed(table_times(ih, il, returns_ref[...].reshape(groups * rows, width)), onsets_ref)
    out_ref[...] = traces.astype(jnp.bfloat16).reshape(out_ref.shape)


def trace_blocks(returns, onsets, inverse, rows):
    groups, height, width = returns.shape
    count = height // rows
    share = NT // groups
    return pl.pallas_call(
        trace_kernel,
        grid=(count,),
        in_specs=table_specs([inverse])
        + [
            pl.BlockSpec((1, 1, width), lambda v: (v, 0, 0)),
            pl.BlockSpec((groups, rows, width), lambda v: (0, v, 0)),
        ],
        out_specs=pl.BlockSpec((groups, 1, share, width), lambda v: (0, v, 0, 0)),
        out_shape=jax.ShapeDtypeStruct((groups, count, share, width), jnp.bfloat16),
        compiler_params=pltpu.CompilerParams(vmem_limit_bytes=LIMIT),
        name="trace_blocks",
    )(*flat_tables([inverse]), onsets, returns)


def exchange(blocks, axis):
    return lax.all_to_all(blocks, axis, split_axis=0, concat_axis=0, tiled=True)


def local(reflection, focus_init, onsets):
    groups = lax.axis_size("freq")
    panels = lax.axis_size("panel")
    _, freqs, _, _ = reflection.shape
    share, sources, width = focus_init.shape
    count = sources // groups
    rows = 2 * freqs
    forward, inverse = band_tables(freqs * groups, NT)
    tables = [inverse, forward]
    own_onsets = lax.dynamic_slice_in_dim(onsets, lax.axis_index("freq") * count, count, 0)
    own_onsets = own_onsets.reshape(count, 1, width)

    def to_all(blocks):
        flat = blocks.reshape((groups * panels,) + blocks.shape[2:])
        return exchange(flat, ("freq", "panel")).reshape(blocks.shape)

    def to_time(blocks):
        samples = exchange(blocks, "freq")
        return jnp.transpose(samples, (2, 0, 1, 3)).reshape(share, sources, width).astype(jnp.float32)

    sent = focus_init.astype(jnp.bfloat16).reshape(share, groups, count, width).transpose(1, 2, 0, 3)
    first, blocks = start_bands(exchange(sent, "freq"), forward, rows)
    for iteration in range(ITERS):
        last = iteration == ITERS - 1
        bands = exchange(blocks, "freq")
        parts = to_all(image_blocks(bands, reflection, panels))
        outs = upgoing_blocks(parts, own_onsets, tables, rows, last)
        returns = exchange(return_blocks(to_all(outs[0]), reflection), "freq")
        if last:
            upgoing = to_time(outs[1])
            focusing = focus_init + to_time(trace_blocks(returns, own_onsets, inverse, rows))
        else:
            blocks = focus_blocks(returns, first, own_onsets, tables, rows)
    return (focusing, upgoing)


def solution(mesh):
    placed = (P(None, "freq", None, "panel"), P("freq", None, "panel"), P(None, "panel"))
    return jax.shard_map(
        local,
        mesh=mesh,
        in_specs=placed,
        out_specs=(P("freq", None, "panel"), P("freq", None, "panel")),
        check_vma=False,
    )
```

time: 656 us -> 359 us (0.55); the launches traced: 647 us -> 357 us
  waiting for transfers between devices: 327 us -> 61.9 us
  Pallas kernels: 0 us -> 60.5 us
  matrix products: 50.4 us -> 0 us
  blocking collectives: 177 us -> 207 us
  local copies, waits for them, and re-layouts: 31.1 us -> 6.08 us
  other arithmetic: 23.5 us -> 4 us
  between operations: 14.6 us -> 0.82 us
    reduce_scatter x2 -> x0, waiting for transfers between devices: 154 us -> none  [local(): lax.psum_scatter(jnp.stack([image_real_part, image_imag_part], axis=1).as...]
    all_gather x2 -> x0, waiting for transfers between devices: 124 us -> none  [local(): lax.all_gather(upgoing_bands, 'panel', axis=3, tiled=True)]
    pallas_call x0 -> x9, Pallas kernels: none -> 60.5 us  [the longest x2 24.7 us: image_blocks(): pl.pallas_call(lambda *refs: image_kernel(step, *refs), grid=(panels,), i...]
    dot_general x12 -> x0, matrix products: 50.4 us -> none  [the longest x2 22.6 us: local(): jnp.einsum('cjrs,jdvs->jcdvr', reflection, focus_bands, preferred_element...]
    all_to_all x12 -> x8, blocking collectives: 177 us -> 207 us  [exchange(): return lax.all_to_all(blocks, axis, split_axis=0, concat_axis=0, tiled=True)]
    all_to_all x4 -> x3, waiting for transfers between devices: 49.2 us -> 61.9 us  [exchange(): return lax.all_to_all(blocks, axis, split_axis=0, concat_axis=0, tiled=True)]
    all_to_all x22 -> x0, local copies, waits for them, and re-layouts: 7.4 us -> none  [the longest x4 2.73 us: to_frequency(): lax.all_to_all(traces.astype(jnp.bfloat16), 'freq', split_axis=1, concat_...]
    sub x5 -> x0, other arithmetic: 6.68 us -> none  [the longest x2 6.58 us: local(): image_real_part = image_products[:, 0, 0] - image_products[:, 1, 1]]
  transfers between devices with their start and end apart: 8 -> 3, of which waited for: 8 -> 3; matrix products, arithmetic and copies ran while one was open for 1% -> 1% of each run, Pallas kernels for 0% -> 1%
where the time goes in v1:
time: 359 us; the launch traced here: 357 us
  blocking collectives  207 us (58%)
  waiting for transfers between devices  61.9 us (17%)
  Pallas kernels  60.5 us (17%)
  starting transfers between devices  17.3 us (5%)
  local copies, waits for them, and re-layouts  6.08 us (2%)
  other arithmetic  4 us (1%)
    all_to_all x8, blocking collectives, exchange(): return lax.all_to_all(blocks, axis, split_axis=0, concat_axis=0, tiled=True)  207 us
    all_to_all x3, waiting for transfers between devices, exchange(): return lax.all_to_all(blocks, axis, split_axis=0, concat_axis=0, tiled=True)  61.9 us
    pallas_call x2, Pallas kernels, image_blocks(): pl.pallas_call(lambda *refs: image_kernel(step, *refs), grid=(panels,), i...  24.7 us
    pallas_call x2, Pallas kernels, return_blocks(): pl.pallas_call(lambda *refs: return_kernel(step, *refs), grid=(panels,),...  21.4 us
    all_to_all x3, starting transfers between devices, exchange(): return lax.all_to_all(blocks, axis, split_axis=0, concat_axis=0, tiled=True)  17.3 us
    pallas_call x2, Pallas kernels, upgoing_blocks(): pl.pallas_call(lambda *refs: upgoing_kernel(with_traces, *refs), grid=(co...  8.53 us
  transfers between devices with their start and end apart: 3, of which 3 were waited for; matrix products, arithmetic and copies ran while one was open for 1% of the time, Pallas kernels for 1%

profile of v1, /device:TPU:1, one launch (start us, length us, event | category | flops | bytes accessed | tf_op | source)
XLA Modules:
  0.0 357.5 jit_solution(2016262035633329796)
XLA Ops:
  0.6 0.0 copy-start
  0.6 0.0 copy-start.1
  0.7 0.0 copy-start.2
  0.7 1.5 convert_element_type.21
  2.2 0.2 copy.9
  2.5 19.5 %all_to_all.55.traces_ref = bf16[16,3,32,256]{3,2,1,0:T(8,128)(2,1)S(1)} all-to-all(bf16[16,3,32,256]{3,2,1,0:T(8,128)(2,1)S(1)} %bitcast.26), channel_id=1, replica_groups=mesh['freq'=16,'panel'=8] {'freq'}, dimensions={0} | all-to-all | bytes 1572864 | tf_op jit(solution)/shard_map/all_to_all | solution.py:293
  22.0 0.0 copy-done.1
  22.0 0.0 copy-done.2
  22.0 1.0 start_bands.1
  23.0 0.0 copy-start.9
  23.0 0.9 copy-done.9
  23.9 11.9 %all_to_all.56.refs_0_ = bf16[16,48,256]{2,1,0:T(8,128)(2,1)S(1)} all-to-all(bf16[16,48,256]{2,1,0:T(8,128)(2,1)S(1)} %get-tuple-element.7), channel_id=1, replica_groups=mesh['freq'=16,'panel'=8] {'freq'}, dimensions={0} | all-to-all | bytes 786432 | tf_op jit(solution)/shard_map/all_to_all | solution.py:293
  35.8 12.9 %image_blocks.2 = bf16[16,8,48,256]{3,2,1,0:T(8,128)(2,1)} custom-call(bf16[16,48,256]{2,1,0:T(8,128)(2,1)S(1)} %all_to_all.56.refs_0_, bf16[2,8,2048,256]{3,2,1,0:T(8,128)(2,1)} %refs_1_.9), custom_call_target="tpu_custom_call" | custom-call | tf_op jit(solution)/shard_map/image_blocks/pallas_call | solution.py:100
  48.7 8.5 %all-to-all-start.2 = ((bf16[128,48,256]{2,1,0:T(8,128)(2,1)}), bf16[128,48,256]{2,1,0:T(8,128)(2,1)S(1)}, u32[]{:S(2)}, u32[]{:S(2)}) async-start(bf16[128,48,256]{2,1,0:T(8,128)(2,1)} %bitcast.2), calls=%async_computation.2 | async-start | bytes 6291456 | tf_op jit(solution)/shard_map/all_to_all | solution.py:293
  57.2 0.0 copy-done
  57.2 40.1 %all-to-all-done.2 = bf16[128,48,256]{2,1,0:T(8,128)(2,1)S(1)} async-done(((bf16[128,48,256]{2,1,0:T(8,128)(2,1)}), bf16[128,48,256]{2,1,0:T(8,128)(2,1)S(1)}, u32[]{:S(2)}, u32[]{:S(2)}) %all-to-all-start.2) | async-done | bytes 3145760 | tf_op jit(solution)/shard_map/all_to_all | solution.py:293
  97.3 0.0 copy-start.3
  97.4 0.9 copy-done.3
  98.3 0.0 copy-start.5
  98.3 0.9 copy-done.5
  99.2 0.0 copy-start.7
  99.3 0.9 copy-done.7
  100.2 3.9 %upgoing_blocks.2 = bf16[16,8,48,256]{3,2,1,0:T(8,128)(2,1)S(1)} custom-call(bf16[512,256]{1,0:T(8,128)(2,1)S(1)} %copy-done.7, bf16[512,256]{1,0:T(8,128)(2,1)S(1)} %copy-done.5, bf16[256,512]{1,0:T(8,128)(2,1)S(1)} %copy-done.3, bf16[256,512]{1,0:T(8,128)(2,1)S(1)} %copy-done.1, s32[3,1,256]{2,1,0:T(1,128)S(1)} %reshape.40.refs_4_.onsets_ref, ...), custom_call_target="tpu_custom_call" | custom-call | tf_op jit(solution)/shard_map/upgoing_blocks/pallas_call | solution.py:230
  104.1 46.1 %all_to_all.57 = bf16[128,48,256]{2,1,0:T(8,128)(2,1)S(1)} all-to-all(bf16[128,48,256]{2,1,0:T(8,128)(2,1)S(1)} %bitcast.22), channel_id=1, replica_groups=mesh['freq'=16,'panel'=8] {'freq','panel'}, dimensions={0} | all-to-all | bytes 6291456 | tf_op jit(solution)/shard_map/all_to_all | solution.py:293
  150.2 0.0 copy-start.4
  150.2 0.0 copy-start.6
  150.2 0.0 copy-start.8
  150.2 0.0 copy-start.10
  150.3 10.8 %return_blocks.2 = bf16[16,48,256]{2,1,0:T(8,128)(2,1)S(1)} custom-call(bf16[16,8,48,256]{3,2,1,0:T(8,128)(2,1)S(1)} %bitcast.17, bf16[2,8,2048,256]{3,2,1,0:T(8,128)(2,1)} %refs_1_.9), custom_call_target="tpu_custom_call" | custom-call | tf_op jit(solution)/shard_map/return_blocks/pallas_call | solution.py:148
  161.0 13.2 %all_to_all.58.returns_ref = bf16[16,48,256]{2,1,0:T(8,128)(2,1)S(1)} all-to-all(bf16[16,48,256]{2,1,0:T(8,128)(2,1)S(1)} %return_blocks.2), channel_id=1, replica_groups=mesh['freq'=16,'panel'=8] {'freq'}, dimensions={0} | all-to-all | bytes 786432 | tf_op jit(solution)/shard_map/all_to_all | solution.py:293
  174.2 0.0 copy-done.4
  174.2 0.0 copy-done.6
  174.2 0.0 copy-done.8
  174.2 0.0 copy-done.10
  174.2 2.9 focus_blocks.1
  177.1 12.1 %all_to_all.59.refs_0_ = bf16[16,48,256]{2,1,0:T(8,128)(2,1)S(1)} all-to-all(bf16[16,48,256]{2,1,0:T(8,128)(2,1)S(1)} %focus_blocks.1), channel_id=1, replica_groups=mesh['freq'=16,'panel'=8] {'freq'}, dimensions={0} | all-to-all | bytes 786432 | tf_op jit(solution)/shard_map/all_to_all | solution.py:293
  189.1 11.8 %image_blocks.3 = bf16[16,8,48,256]{3,2,1,0:T(8,128)(2,1)S(1)} custom-call(bf16[16,48,256]{2,1,0:T(8,128)(2,1)S(1)} %all_to_all.59.refs_0_, bf16[2,8,2048,256]{3,2,1,0:T(8,128)(2,1)} %refs_1_.9), custom_call_target="tpu_custom_call" | custom-call | tf_op jit(solution)/shard_map/image_blocks/pallas_call | solution.py:100
  200.9 44.7 %all_to_all.60 = bf16[128,48,256]{2,1,0:T(8,128)(2,1)S(1)} all-to-all(bf16[128,48,256]{2,1,0:T(8,128)(2,1)S(1)} %bitcast.18), channel_id=1, replica_groups=mesh['freq'=16,'panel'=8] {'freq','panel'}, dimensions={0} | all-to-all | bytes 6291456 | tf_op jit(solution)/shard_map/all_to_all | solution.py:293
  245.6 4.6 %upgoing_blocks.3 = (bf16[16,8,48,256]{3,2,1,0:T(8,128)(2,1)S(1)}, bf16[16,3,32,256]{3,2,1,0:T(8,128)(2,1)}) custom-call(bf16[512,256]{1,0:T(8,128)(2,1)S(1)} %copy-done.8, bf16[512,256]{1,0:T(8,128)(2,1)S(1)} %copy-done.6, bf16[256,512]{1,0:T(8,128)(2,1)S(1)} %copy-done.4, bf16[256,512]{1,0:T(8,128)(2,1)S(1)} %copy-done.1, ...), custom_call_target="tpu_custom_call" | custom-call | tf_op jit(solution)/shard_map/upgoing_blocks/pallas_call | solution.py:230
  250.2 46.1 %all_to_all.61 = bf16[128,48,256]{2,1,0:T(8,128)(2,1)S(1)} all-to-all(bf16[128,48,256]{2,1,0:T(8,128)(2,1)S(1)} %bitcast.23), channel_id=1, replica_groups=mesh['freq'=16,'panel'=8] {'freq','panel'}, dimensions={0} | all-to-all | bytes 6291456 | tf_op jit(solution)/shard_map/all_to_all | solution.py:293
  296.4 10.6 %return_blocks.3 = bf16[16,48,256]{2,1,0:T(8,128)(2,1)S(1)} custom-call(bf16[16,8,48,256]{3,2,1,0:T(8,128)(2,1)S(1)} %bitcast.19, bf16[2,8,2048,256]{3,2,1,0:T(8,128)(2,1)} %refs_1_.9), custom_call_target="tpu_custom_call" | custom-call | tf_op jit(solution)/shard_map/return_blocks/pallas_call | solution.py:148
  307.0 13.2 %all_to_all.62.returns_ref = bf16[16,48,256]{2,1,0:T(8,128)(2,1)S(1)} all-to-all(bf16[16,48,256]{2,1,0:T(8,128)(2,1)S(1)} %return_blocks.3), channel_id=1, replica_groups=mesh['freq'=16,'panel'=8] {'freq'}, dimensions={0} | all-to-all | bytes 786432 | tf_op jit(solution)/shard_map/all_to_all | solution.py:293
  320.2 4.6 %all-to-all-start.10 = ((bf16[16,3,32,256]{3,2,1,0:T(8,128)(2,1)}), bf16[16,3,32,256]{3,2,1,0:T(8,128)(2,1)S(1)}, u32[]{:S(2)}, u32[]{:S(2)}) async-start(bf16[16,3,32,256]{3,2,1,0:T(8,128)(2,1)} %get-tuple-element.9), calls=%async_computation.10 | async-start | bytes 1572864 | tf_op jit(solution)/shard_map/all_to_all | solution.py:293
  324.7 2.0 trace_blocks.1
  326.8 11.0 %all-to-all-done.10 = bf16[16,3,32,256]{3,2,1,0:T(8,128)(2,1)S(1)} async-done(((bf16[16,3,32,256]{3,2,1,0:T(8,128)(2,1)}), bf16[16,3,32,256]{3,2,1,0:T(8,128)(2,1)S(1)}, u32[]{:S(2)}, u32[]{:S(2)}) %all-to-all-start.10) | async-done | bytes 786464 | tf_op jit(solution)/shard_map/all_to_all | solution.py:293
  337.8 4.3 %all-to-all-start.9 = ((bf16[16,3,32,256]{3,2,1,0:T(8,128)(2,1)}), bf16[16,3,32,256]{3,2,1,0:T(8,128)(2,1)S(1)}, u32[]{:S(2)}, u32[]{:S(2)}) async-start(bf16[16,3,32,256]{3,2,1,0:T(8,128)(2,1)} %trace_blocks.1), calls=%async_computation.9 | async-start | bytes 1572864 | tf_op jit(solution)/shard_map/all_to_all | solution.py:293
  342.1 0.2 convert_element_type.31
  342.3 0.0 copy-start.11
  342.3 2.1 copy.11
  344.3 10.8 %all-to-all-done.9 = bf16[16,3,32,256]{3,2,1,0:T(8,128)(2,1)S(1)} async-done(((bf16[16,3,32,256]{3,2,1,0:T(8,128)(2,1)}), bf16[16,3,32,256]{3,2,1,0:T(8,128)(2,1)S(1)}, u32[]{:S(2)}, u32[]{:S(2)}) %all-to-all-start.9) | async-done | bytes 786464 | tf_op jit(solution)/shard_map/all_to_all | solution.py:293
  355.1 0.2 convert_element_type.30
  355.3 0.0 copy-done.11
  355.3 2.1 copy_add_fusion
  (2 shorter events, 0.0 us)
Async XLA Ops:
  0.6 56.6 %copy-start = (s32[48,256]{1,0:T(8,128)S(1)}, s32[48,256]{1,0:T(8,128)}, u32[]{:S(2)}) copy-start(s32[48,256]{1,0:T(8,128)} %param.9) | copy-start | bytes 147460
  0.6 21.3 %copy-start.1 = (bf16[256,512]{1,0:T(8,128)(2,1)S(1)}, bf16[256,512]{1,0:T(8,128)(2,1)}, u32[]{:S(2)}) copy-start(bf16[256,512]{1,0:T(8,128)(2,1)} %constant.21.clone.low.refs_3_.fl) | copy-start | bytes 786436
  0.7 21.3 %copy-start.2 = (bf16[256,512]{1,0:T(8,128)(2,1)S(1)}, bf16[256,512]{1,0:T(8,128)(2,1)}, u32[]{:S(2)}) copy-start(bf16[256,512]{1,0:T(8,128)(2,1)} %constant.20.clone.high.refs_2_.fh) | copy-start | bytes 786436
  23.0 0.9 copy-start.9
  48.7 48.7 %all-to-all-start.2 = ((bf16[128,48,256]{2,1,0:T(8,128)(2,1)}), bf16[128,48,256]{2,1,0:T(8,128)(2,1)S(1)}, u32[]{:S(2)}, u32[]{:S(2)}) async-start(bf16[128,48,256]{2,1,0:T(8,128)(2,1)} %bitcast.2), calls=%async_computation.2 | async-start | bytes 6291456 | tf_op jit(solution)/shard_map/all_to_all | solution.py:293
  97.3 1.0 copy-start.3
  98.3 0.9 copy-start.5
  99.2 0.9 copy-start.7
  150.2 23.9 %copy-start.4 = (bf16[256,512]{1,0:T(8,128)(2,1)S(1)}, bf16[256,512]{1,0:T(8,128)(2,1)}, u32[]{:S(2)}) copy-start(bf16[256,512]{1,0:T(8,128)(2,1)} %constant.20.clone.high.refs_2_.fh) | copy-start | bytes 786436
  150.2 23.9 %copy-start.6 = (bf16[512,256]{1,0:T(8,128)(2,1)S(1)}, bf16[512,256]{1,0:T(8,128)(2,1)}, u32[]{:S(2)}) copy-start(bf16[512,256]{1,0:T(8,128)(2,1)} %constant.23.clone.refs_1_.il) | copy-start | bytes 786436
  150.2 23.9 %copy-start.8 = (bf16[512,256]{1,0:T(8,128)(2,1)S(1)}, bf16[512,256]{1,0:T(8,128)(2,1)}, u32[]{:S(2)}) copy-start(bf16[512,256]{1,0:T(8,128)(2,1)} %constant.22.clone.refs_0_.ih) | copy-start | bytes 786436
  150.2 23.9 %copy-start.10 = (f32[3,256,256]{2,1,0:T(8,128)S(1)}, f32[3,256,256]{2,1,0:T(8,128)}, u32[]{:S(2)}) copy-start(f32[3,256,256]{2,1,0:T(8,128)} %copy-done.9) | copy-start | bytes 2359300
  320.2 17.6 %all-to-all-start.10 = ((bf16[16,3,32,256]{3,2,1,0:T(8,128)(2,1)}), bf16[16,3,32,256]{3,2,1,0:T(8,128)(2,1)S(1)}, u32[]{:S(2)}, u32[]{:S(2)}) async-start(bf16[16,3,32,256]{3,2,1,0:T(8,128)(2,1)} %get-tuple-element.9), calls=%async_computation.10 | async-start | bytes 1572864 | tf_op jit(solution)/shard_map/all_to_all | solution.py:293
  337.8 17.3 %all-to-all-start.9 = ((bf16[16,3,32,256]{3,2,1,0:T(8,128)(2,1)}), bf16[16,3,32,256]{3,2,1,0:T(8,128)(2,1)S(1)}, u32[]{:S(2)}, u32[]{:S(2)}) async-start(bf16[16,3,32,256]{3,2,1,0:T(8,128)(2,1)} %trace_blocks.1), calls=%async_computation.9 | async-start | bytes 1572864 | tf_op jit(solution)/shard_map/all_to_all | solution.py:293
  342.3 13.1 %copy-start.11 = (f32[32,48,256]{2,1,0:T(8,128)S(1)}, f32[32,48,256]{2,1,0:T(8,128)}, u32[]{:S(2)}) copy-start(f32[32,48,256]{2,1,0:T(8,128)} %param.8) | copy-start | bytes 4718596

commit v2 on v0

v2 whole, which is shorter than its diff:
```python
import math

import jax
import jax.numpy as jnp
import ml_dtypes
import numpy as np
from jax import lax
from jax.experimental import pallas as pl
from jax.experimental.pallas import tpu as pltpu
from jax.sharding import PartitionSpec as P

NT = 512
ITERS = 2
MIB = 1024 * 1024


def split_table(table):
    high = table.astype(ml_dtypes.bfloat16)
    low = (table - high.astype(np.float32)).astype(ml_dtypes.bfloat16)
    return high, low


def band_tables(freq_count, time_count):
    harmonic = np.arange(1, freq_count + 1)
    phases = harmonic[:, None] * np.arange(time_count)[None, :] % time_count
    angles = phases * (2.0 * math.pi / time_count)
    factor = 1.0 / math.sqrt(time_count)
    cosines = np.stack([np.cos(angles), -np.sin(angles)], axis=1).reshape(2 * freq_count, time_count)
    forward = (cosines * factor).astype(np.float32)
    inverse = (cosines.T * (2.0 * factor)).astype(np.float32)
    return split_table(forward), split_table(inverse)


def dot(a, b):
    return jnp.dot(a, b, preferred_element_type=jnp.float32)


def dot_nt(a, b):
    return lax.dot_general(a, b, (((1,), (1,)), ((), ())), preferred_element_type=jnp.float32)


def halves(x):
    high = x.astype(jnp.bfloat16)
    return high, (x - high.astype(jnp.float32)).astype(jnp.bfloat16)


def table_times(high_ref, low_ref, x):
    if x.dtype == jnp.bfloat16:
        return dot(high_ref[...], x) + dot(low_ref[...], x)
    high, low = halves(x)
    return dot(high_ref[...], high) + dot(low_ref[...], high) + dot(high_ref[...], low)


def pick(rows_ref, row, step, count):
    return jnp.concatenate(
        [rows_ref[h, pl.ds(row, count, stride=step), :] for h in range(rows_ref.shape[0])], axis=1
    )


def place(rows_ref, row, step, value):
    for h in range(rows_ref.shape[0]):
        rows_ref[h, pl.ds(row, value.shape[0], stride=step), :] = value[:, h * 128 : (h + 1) * 128]


def fill(rows_ref, blocks):
    flat = blocks.reshape(rows_ref.shape[1], -1).astype(jnp.float32)
    for h in range(rows_ref.shape[0]):
        rows_ref[h] = flat[:, h * 128 : (h + 1) * 128]


def emptied(rows_ref, out_ref):
    flat = jnp.concatenate([rows_ref[h].astype(jnp.bfloat16) for h in range(rows_ref.shape[0])], axis=1)
    out_ref[...] = flat.reshape(out_ref.shape)


def image_kernel(first, bands_ref, refl_ref, out_ref, *more):
    held_ref = more[0] if first else refl_ref
    rows, direct, crossed = more[first : first + 3]
    _, freqs, height, width = refl_ref.shape
    step = 2 * freqs
    count = rows.shape[1] // step
    groups, panels, block, share = out_ref.shape

    copies = []
    if first:
        for p in range(panels):
            part = (slice(None), slice(None), pl.ds(p * share, share))
            copies.append(pltpu.make_async_copy(refl_ref.at[part], held_ref.at[part], more[-1].at[p]))
            copies[-1].start()

    fill(rows, bands_ref[...])
    for j in range(freqs):
        real, imag = pick(rows, 2 * j, step, count), pick(rows, 2 * j + 1, step, count)
        direct[j] = jnp.concatenate([real, imag], axis=0).astype(jnp.bfloat16)
        crossed[j] = jnp.concatenate([-imag, real], axis=0).astype(jnp.bfloat16)

    for p in range(panels):
        if first:
            copies[p].wait()
        at = slice(p * share, (p + 1) * share)
        images = [
            dot_nt(direct[j], held_ref[0, j, at]) + dot_nt(crossed[j], held_ref[1, j, at]) for j in range(freqs)
        ]
        images = jnp.stack(images).reshape(step, count, share)
        out_ref[:, p] = jnp.swapaxes(images, 0, 1).astype(jnp.bfloat16).reshape(groups, block, share)


IN_VMEM = pl.BlockSpec(memory_space=pltpu.VMEM)


def call(kernel, name, out_shape, args, scratch=(), specs=None, flops=0):
    size = sum(a.size * a.dtype.itemsize for a in args)
    return pl.pallas_call(
        kernel,
        in_specs=specs or [IN_VMEM] * len(args),
        out_specs=jax.tree.map(lambda _: IN_VMEM, out_shape),
        out_shape=out_shape,
        scratch_shapes=list(scratch),
        compiler_params=pltpu.CompilerParams(vmem_limit_bytes=16 * MIB),
        cost_estimate=pl.CostEstimate(flops=flops, bytes_accessed=2 * size, transcendentals=0),
        name=name,
    )(*args)


def image_blocks(bands, reflection, panels, first):
    groups, height, width = bands.shape
    _, freqs, receivers, _ = reflection.shape
    count = groups * height // (2 * freqs)
    out_shape = [jax.ShapeDtypeStruct((groups, panels, height, receivers // panels), jnp.bfloat16)]
    scratch = [
        pltpu.VMEM((width // 128, groups * height, 128), jnp.float32),
        pltpu.VMEM((freqs, 2 * count, width), jnp.bfloat16),
        pltpu.VMEM((freqs, 2 * count, width), jnp.bfloat16),
    ]
    specs = None
    if first:
        out_shape.append(pltpu.VMEM(reflection.shape, reflection.dtype))
        scratch.append(pltpu.SemaphoreType.DMA((panels,)))
        specs = [IN_VMEM, pl.BlockSpec(memory_space=pltpu.HBM)]
        reflection = pltpu.with_memory_space_constraint(reflection, pltpu.HBM)
    return call(
        lambda *refs: image_kernel(int(first), *refs),
        "image_blocks",
        out_shape,
        (bands, reflection),
        scratch,
        specs,
        flops=4 * reflection.size * count,
    )


def return_kernel(bands_ref, refl_ref, *more):
    out_ref, rows, results = more[-3:]
    groups, panels, block, width = bands_ref.shape
    freqs = refl_ref.shape[1]
    step = 2 * freqs
    count = groups * block // step
    lanes = width // 128

    for p in range(panels):
        flat = bands_ref[:, p].reshape(groups * block, width).astype(jnp.float32)
        for h in range(lanes):
            rows[p * lanes + h] = flat[:, h * 128 : (h + 1) * 128]

    for j in range(freqs):
        total = None
        for p in range(panels):
            of_panel = rows.at[pl.ds(p * lanes, lanes)]
            real = pick(of_panel, 2 * j, step, count)
            imag = pick(of_panel, 2 * j + 1, step, count)
            direct = jnp.concatenate([real, imag], axis=0).astype(jnp.bfloat16)
            crossed = jnp.concatenate([imag, -real], axis=0).astype(jnp.bfloat16)
            at = slice(p * width, (p + 1) * width)
            part = dot(direct, refl_ref[0, j, at]) + dot(crossed, refl_ref[1, j, at])
            total = part if total is None else total + part
        place(results, 2 * j, step, total[:count])
        place(results, 2 * j + 1, step, total[count:])
    emptied(results, out_ref.at[:, :block])
    if len(more) > 3:
        out_ref[:, block:] = more[0][...].reshape(groups, -1, width)


def return_blocks(bands, reflection, traces=()):
    groups, panels, height, width = bands.shape
    _, freqs, _, sources = reflection.shape
    more = sum(t.size // (groups * width) for t in traces)
    return call(
        return_kernel,
        "return_blocks",
        jax.ShapeDtypeStruct((groups, height + more, sources), jnp.bfloat16),
        (bands, reflection, *traces),
        [
            pltpu.VMEM((panels * width // 128, groups * height, 128), jnp.float32),
            pltpu.VMEM((sources // 128, groups * height, 128), jnp.float32),
        ],
        flops=4 * reflection.size * groups * height // (2 * freqs),
    )


def windowed(traces, onsets_ref, v):
    count = onsets_ref.shape[0] // lax.axis_size("freq")
    onsets = onsets_ref[pl.ds(lax.axis_index("freq") * count + v, 1), :]
    samples = lax.broadcasted_iota(jnp.int32, traces.shape, 0)
    return jnp.where((samples < onsets) | (samples > NT - onsets), traces, 0.0)


def start_kernel(high, low, traces_ref, first_ref, out_ref):
    blocks, count, share, width = traces_ref.shape
    rows = out_ref.shape[1] // count
    for v in range(count):
        spectra = table_times(high, low, traces_ref[:, v].reshape(blocks * share, width))
        first_ref[v] = spectra
        out_ref[:, v * rows : (v + 1) * rows] = spectra.astype(jnp.bfloat16).reshape(blocks, rows, width)


def start_bands(traces, forward, rows):
    blocks, count, _, width = traces.shape
    return call(
        start_kernel,
        "start_bands",
        [
            pltpu.VMEM((count, blocks * rows, width), jnp.float32),
            jax.ShapeDtypeStruct((blocks, count * rows, width), jnp.bfloat16),
        ],
        (*forward, traces),
    )


def upgoing_kernel(rows, ih, il, fh, fl, onsets_ref, parts_ref, out_ref, *traces_ref):
    groups, panels, height, width = parts_ref.shape
    for v in range(height // rows):
        at = slice(v * rows, (v + 1) * rows)
        images = parts_ref[:, 0, at].astype(jnp.float32)
        for p in range(1, panels):
            images = images + parts_ref[:, p, at].astype(jnp.float32)
        traces = windowed(table_times(ih, il, images.reshape(groups * rows, width)), onsets_ref, v)
        spectra = table_times(fh, fl, traces).astype(jnp.bfloat16).reshape(groups, rows, width)
        for p in range(panels):
            out_ref[:, p, at] = spectra
        for ref in traces_ref:
            ref[:, v] = traces.astype(jnp.bfloat16).reshape(groups, -1, width)


def upgoing_blocks(parts, onsets, tables, rows, with_traces):
    groups, panels, height, width = parts.shape
    out_shape = [jax.ShapeDtypeStruct(parts.shape, jnp.bfloat16)]
    if with_traces:
        out_shape.append(jax.ShapeDtypeStruct((groups, height // rows, NT // groups, width), jnp.bfloat16))
    return call(
        lambda *refs: upgoing_kernel(rows, *refs), "upgoing_blocks", out_shape, (*tables, onsets, parts)
    )


def focus_kernel(rows, ih, il, fh, fl, onsets_ref, first_ref, returns_ref, out_ref):
    groups, height, width = returns_ref.shape
    for v in range(height // rows):
        at = slice(v * rows, (v + 1) * rows)
        returns = returns_ref[:, at].reshape(groups * rows, width)
        traces = windowed(table_times(ih, il, returns), onsets_ref, v)
        spectra = first_ref[v] + table_times(fh, fl, traces)
        out_ref[:, at] = spectra.astype(jnp.bfloat16).reshape(groups, rows, width)


def focus_blocks(returns, first, onsets, tables, rows):
    return call(
        lambda *refs: focus_kernel(rows, *refs),
        "focus_blocks",
        jax.ShapeDtypeStruct(returns.shape, jnp.bfloat16),
        (*tables, onsets, first, returns),
    )


def trace_kernel(rows, ih, il, onsets_ref, returns_ref, out_ref):
    groups, count, _, width = out_ref.shape
    for v in range(count):
        returns = returns_ref[:, v * rows : (v + 1) * rows].reshape(groups * rows, width)
        traces = windowed(table_times(ih, il, returns), onsets_ref, v)
        out_ref[:, v] = traces.astype(jnp.bfloat16).reshape(groups, -1, width)


def trace_blocks(returns, onsets, inverse, rows, count):
    groups, _, width = returns.shape
    return call(
        lambda *refs: trace_kernel(rows, *refs),
        "trace_blocks",
        jax.ShapeDtypeStruct((groups, count, NT // groups, width), jnp.bfloat16),
        (*inverse, onsets, returns),
    )


def exchange(blocks, axis):
    return lax.all_to_all(blocks, axis, split_axis=0, concat_axis=0, tiled=True)


def local(reflection, focus_init, onsets):
    groups = lax.axis_size("freq")
    panels = lax.axis_size("panel")
    freqs = reflection.shape[1]
    share, sources, width = focus_init.shape
    count = sources // groups
    rows = 2 * freqs
    forward, inverse = [[jnp.asarray(t) for t in pair] for pair in band_tables(freqs * groups, NT)]
    tables = inverse + forward

    def to_all(blocks):
        flat = blocks.reshape((groups * panels,) + blocks.shape[2:])
        return exchange(flat, ("freq", "panel")).reshape(blocks.shape)

    def in_time(samples):
        samples = samples.reshape(groups, count, share, width)
        return jnp.transpose(samples, (2, 0, 1, 3)).reshape(share, sources, width).astype(jnp.float32)

    sent = focus_init.astype(jnp.bfloat16).reshape(share, groups, count, width).transpose(1, 2, 0, 3)
    first, blocks = start_bands(exchange(sent, "freq"), forward, rows)
    for iteration in range(ITERS):
        last = iteration == ITERS - 1
        bands = exchange(blocks, "freq")
        images = image_blocks(bands, reflection, panels, iteration == 0)
        if iteration == 0:
            reflection = images[1]
        spectra, *traces = upgoing_blocks(to_all(images[0]), onsets, tables, rows, last)
        returns = exchange(return_blocks(to_all(spectra), reflection, traces), "freq")
        if last:
            upgoing = in_time(returns[:, count * rows :])
            traces = trace_blocks(returns, onsets, inverse, rows, count)
            focusing = focus_init + in_time(exchange(traces, "freq"))
        else:
            blocks = focus_blocks(returns, first, onsets, tables, rows)
    return (focusing, upgoing)


def solution(mesh):
    placed = (P(None, "freq", None, "panel"), P("freq", None, "panel"), P(None, "panel"))
    return jax.shard_map(
        local,
        mesh=mesh,
        in_specs=placed,
        out_specs=(P("freq", None, "panel"), P("freq", None, "panel")),
        check_vma=False,
    )
```

time: 656 us -> 316 us (0.48); the launches traced: 647 us -> 316 us
  waiting for transfers between devices: 327 us -> 10.7 us
  blocking collectives: 177 us -> 264 us
  matrix products: 50.4 us -> 0 us
  Pallas kernels: 0 us -> 29.4 us
  local copies, waits for them, and re-layouts: 31.1 us -> 2.42 us
  other arithmetic: 23.5 us -> 3.95 us
  starting transfers between devices: 23.5 us -> 4.1 us
  between operations: 14.6 us -> 0.78 us
    reduce_scatter x2 -> x0, waiting for transfers between devices: 154 us -> none  [local(): lax.psum_scatter(jnp.stack([image_real_part, image_imag_part], axis=1).as...]
    all_gather x2 -> x0, waiting for transfers between devices: 124 us -> none  [local(): lax.all_gather(upgoing_bands, 'panel', axis=3, tiled=True)]
    all_to_all x12 -> x9, blocking collectives: 177 us -> 264 us  [exchange(): return lax.all_to_all(blocks, axis, split_axis=0, concat_axis=0, tiled=True)]
    dot_general x12 -> x0, matrix products: 50.4 us -> none  [the longest x2 22.6 us: local(): jnp.einsum('cjrs,jdvs->jcdvr', reflection, focus_bands, preferred_element...]
    all_to_all x4 -> x1, waiting for transfers between devices: 49.2 us -> 10.7 us  [exchange(): return lax.all_to_all(blocks, axis, split_axis=0, concat_axis=0, tiled=True)]
    pallas_call x0 -> x9, Pallas kernels: none -> 29.4 us  [call(): pl.pallas_call(kernel, in_specs=specs or [IN_VMEM] * len(args), out_specs...]
    all_to_all x4 -> x1, starting transfers between devices: 23.4 us -> 4.1 us  [exchange(): return lax.all_to_all(blocks, axis, split_axis=0, concat_axis=0, tiled=True)]
    all_to_all x22 -> x0, local copies, waits for them, and re-layouts: 7.4 us -> none  [the longest x4 2.73 us: to_frequency(): lax.all_to_all(traces.astype(jnp.bfloat16), 'freq', split_axis=1, concat_...]
  transfers between devices with their start and end apart: 8 -> 1, of which waited for: 8 -> 1; matrix products, arithmetic and copies ran while one was open for 1% -> 1% of each run, Pallas kernels for 0% -> 0%
where the time goes in v2:
time: 316 us
  blocking collectives  264 us (84%)
  Pallas kernels  29.4 us (9%)
  waiting for transfers between devices  10.7 us (3%)
  starting transfers between devices  4.1 us (1%)
  other arithmetic  3.95 us (1%)
    all_to_all x9, blocking collectives, exchange(): return lax.all_to_all(blocks, axis, split_axis=0, concat_axis=0, tiled=True)  264 us
    pallas_call x9, Pallas kernels, call(): pl.pallas_call(kernel, in_specs=specs or [IN_VMEM] * len(args), out_specs...  29.4 us
    all_to_all x1, waiting for transfers between devices, exchange(): return lax.all_to_all(blocks, axis, split_axis=0, concat_axis=0, tiled=True)  10.7 us
  transfers between devices with their start and end apart: 1, of which 1 were waited for; matrix products, arithmetic and copies ran while one was open for 1% of the time, Pallas kernels for 0%

profile of v2, /device:TPU:1, one launch (start us, length us, event | category | flops | bytes accessed | tf_op | source)
XLA Modules:
  0.0 315.7 jit_solution(17675138195338369394)
XLA Ops:
  0.6 1.5 convert_element_type.24
  2.1 0.0 copy-start.2
  2.1 0.0 copy-start.3
  2.1 0.2 copy.12
  2.4 19.5 %all_to_all.50.traces_ref = bf16[16,3,32,256]{3,2,1,0:T(8,128)(2,1)S(1)} all-to-all(bf16[16,3,32,256]{3,2,1,0:T(8,128)(2,1)S(1)} %bitcast.29), channel_id=1, replica_groups=mesh['freq'=16,'panel'=8] {'freq'}, dimensions={0} | all-to-all | bytes 1572864 | tf_op jit(solution)/shard_map/all_to_all | solution.py:292
  21.9 0.0 copy-done.2
  21.9 0.0 copy-done.3
  21.9 0.6 start_bands.1
  22.5 11.9 %all_to_all.51.refs_0_ = bf16[16,48,256]{2,1,0:T(8,128)(2,1)S(1)} all-to-all(bf16[16,48,256]{2,1,0:T(8,128)(2,1)S(1)} %get-tuple-element.9), channel_id=1, replica_groups=mesh['freq'=16,'panel'=8] {'freq'}, dimensions={0} | all-to-all | bytes 786432 | tf_op jit(solution)/shard_map/all_to_all | solution.py:292
  34.4 8.2 %image_blocks.2 = (bf16[16,8,48,256]{3,2,1,0:T(8,128)(2,1)S(1)}, bf16[2,8,2048,256]{3,2,1,0:T(8,128)(2,1)S(1)}) custom-call(bf16[16,48,256]{2,1,0:T(8,128)(2,1)S(1)} %all_to_all.51.refs_0_, bf16[2,8,2048,256]{3,2,1,0:T(8,128)(2,1)} %refs_1_.5), custom_call_target="tpu_custom_call" | custom-call | flops 1610612736 | bytes 34340864 | tf_op jit(solution)/shard_map/image_blocks/pallas_call | solution.py:113
  42.6 0.0 copy-start
  42.6 0.0 copy-start.1
  42.6 0.0 copy-start.4
  42.6 48.4 %all_to_all.52 = bf16[128,48,256]{2,1,0:T(8,128)(2,1)S(1)} all-to-all(bf16[128,48,256]{2,1,0:T(8,128)(2,1)S(1)} %bitcast.26), channel_id=1, replica_groups=mesh['freq'=16,'panel'=8] {'freq','panel'}, dimensions={0} | all-to-all | bytes 6291456 | tf_op jit(solution)/shard_map/all_to_all | solution.py:292
  91.0 0.0 copy-done
  91.0 0.0 copy-done.1
  91.0 0.0 copy-done.4
  91.0 2.1 upgoing_blocks.2
  93.2 46.1 %all_to_all.53 = bf16[128,48,256]{2,1,0:T(8,128)(2,1)S(1)} all-to-all(bf16[128,48,256]{2,1,0:T(8,128)(2,1)S(1)} %bitcast.21), channel_id=1, replica_groups=mesh['freq'=16,'panel'=8] {'freq','panel'}, dimensions={0} | all-to-all | bytes 6291456 | tf_op jit(solution)/shard_map/all_to_all | solution.py:292
  139.3 3.9 %return_blocks.2 = bf16[16,48,256]{2,1,0:T(8,128)(2,1)S(1)} custom-call(bf16[16,8,48,256]{3,2,1,0:T(8,128)(2,1)S(1)} %bitcast.19, bf16[2,8,2048,256]{3,2,1,0:T(8,128)(2,1)S(1)} %get-tuple-element.11.refl_ref.refs_1_), custom_call_target="tpu_custom_call" | custom-call | flops 1610612736 | bytes 39845888 | tf_op jit(solution)/shard_map/return_blocks/pallas_call | solution.py:113
  143.2 13.3 %all_to_all.54.refs_6_ = bf16[16,48,256]{2,1,0:T(8,128)(2,1)S(1)} all-to-all(bf16[16,48,256]{2,1,0:T(8,128)(2,1)S(1)} %return_blocks.2), channel_id=1, replica_groups=mesh['freq'=16,'panel'=8] {'freq'}, dimensions={0} | all-to-all | bytes 786432 | tf_op jit(solution)/shard_map/all_to_all | solution.py:292
  156.5 1.5 focus_blocks.1
  158.1 12.1 %all_to_all.55.refs_0_ = bf16[16,48,256]{2,1,0:T(8,128)(2,1)S(1)} all-to-all(bf16[16,48,256]{2,1,0:T(8,128)(2,1)S(1)} %focus_blocks.1), channel_id=1, replica_groups=mesh['freq'=16,'panel'=8] {'freq'}, dimensions={0} | all-to-all | bytes 786432 | tf_op jit(solution)/shard_map/all_to_all | solution.py:292
  170.2 5.4 %image_blocks.3 = bf16[16,8,48,256]{3,2,1,0:T(8,128)(2,1)S(1)} custom-call(bf16[16,48,256]{2,1,0:T(8,128)(2,1)S(1)} %all_to_all.55.refs_0_, bf16[2,8,2048,256]{3,2,1,0:T(8,128)(2,1)S(1)} %get-tuple-element.11.refl_ref.refs_1_), custom_call_target="tpu_custom_call" | custom-call | flops 1610612736 | bytes 34340864 | tf_op jit(solution)/shard_map/image_blocks/pallas_call | solution.py:113
  175.6 44.7 %all_to_all.56 = bf16[128,48,256]{2,1,0:T(8,128)(2,1)S(1)} all-to-all(bf16[128,48,256]{2,1,0:T(8,128)(2,1)S(1)} %bitcast.22), channel_id=1, replica_groups=mesh['freq'=16,'panel'=8] {'freq','panel'}, dimensions={0} | all-to-all | bytes 6291456 | tf_op jit(solution)/shard_map/all_to_all | solution.py:292
  220.3 2.1 upgoing_blocks.3
  222.5 46.1 %all_to_all.57 = bf16[128,48,256]{2,1,0:T(8,128)(2,1)S(1)} all-to-all(bf16[128,48,256]{2,1,0:T(8,128)(2,1)S(1)} %bitcast.25), channel_id=1, replica_groups=mesh['freq'=16,'panel'=8] {'freq','panel'}, dimensions={0} | all-to-all | bytes 6291456 | tf_op jit(solution)/shard_map/all_to_all | solution.py:292
  268.6 3.9 %return_blocks.3 = bf16[16,144,256]{2,1,0:T(8,128)(2,1)S(1)} custom-call(bf16[16,8,48,256]{3,2,1,0:T(8,128)(2,1)S(1)} %bitcast.24, bf16[2,8,2048,256]{3,2,1,0:T(8,128)(2,1)S(1)} %get-tuple-element.11.refl_ref.refs_1_, bf16[16,3,32,256]{3,2,1,0:T(8,128)(2,1)S(1)} %get-tuple-element.13.more_0_), custom_call_target="tpu_custom_call" | custom-call | flops 1610612736 | bytes 41418752 | tf_op jit(solution)/shard_map/return_blocks/pallas_call | solution.py:113
  272.5 22.1 %all_to_all.58.refs_3_ = bf16[16,144,256]{2,1,0:T(8,128)(2,1)S(1)} all-to-all(bf16[16,144,256]{2,1,0:T(8,128)(2,1)S(1)} %return_blocks.3), channel_id=1, replica_groups=mesh['freq'=16,'panel'=8] {'freq'}, dimensions={0} | all-to-all | bytes 2359296 | tf_op jit(solution)/shard_map/all_to_all | solution.py:292
  294.6 1.6 trace_blocks.1
  296.3 4.1 %all-to-all-start.9 = ((bf16[16,3,32,256]{3,2,1,0:T(8,128)(2,1)}), bf16[16,3,32,256]{3,2,1,0:T(8,128)(2,1)S(1)}, u32[]{:S(2)}, u32[]{:S(2)}) async-start(bf16[16,3,32,256]{3,2,1,0:T(8,128)(2,1)} %trace_blocks.1), calls=%async_computation.9 | async-start | bytes 1572864 | tf_op jit(solution)/shard_map/all_to_all | solution.py:292
  300.4 0.1 slice.4
  300.4 0.2 convert.5
  300.6 2.1 copy.14
  302.7 0.0 copy-start.5
  302.7 10.7 %all-to-all-done.9 = bf16[16,3,32,256]{3,2,1,0:T(8,128)(2,1)S(1)} async-done(((bf16[16,3,32,256]{3,2,1,0:T(8,128)(2,1)}), bf16[16,3,32,256]{3,2,1,0:T(8,128)(2,1)S(1)}, u32[]{:S(2)}, u32[]{:S(2)}) %all-to-all-start.9) | async-done | bytes 786464 | tf_op jit(solution)/shard_map/all_to_all | solution.py:292
  313.4 0.2 convert_element_type.34
  313.6 0.0 copy-done.5
  313.6 2.1 copy_add_fusion
Async XLA Ops:
  2.1 19.8 %copy-start.2 = (bf16[256,512]{1,0:T(8,128)(2,1)S(1)}, bf16[256,512]{1,0:T(8,128)(2,1)}, u32[]{:S(2)}) copy-start(bf16[256,512]{1,0:T(8,128)(2,1)} %constant.9.clone.low.refs_3_) | copy-start | bytes 786436
  2.1 19.8 %copy-start.3 = (bf16[256,512]{1,0:T(8,128)(2,1)S(1)}, bf16[256,512]{1,0:T(8,128)(2,1)}, u32[]{:S(2)}) copy-start(bf16[256,512]{1,0:T(8,128)(2,1)} %constant.8.clone.high.refs_2_) | copy-start | bytes 786436
  42.6 48.5 %copy-start = (bf16[512,256]{1,0:T(8,128)(2,1)S(1)}, bf16[512,256]{1,0:T(8,128)(2,1)}, u32[]{:S(2)}) copy-start(bf16[512,256]{1,0:T(8,128)(2,1)} %constant.11.clone.refs_1_) | copy-start | bytes 786436
  42.6 48.5 %copy-start.1 = (bf16[512,256]{1,0:T(8,128)(2,1)S(1)}, bf16[512,256]{1,0:T(8,128)(2,1)}, u32[]{:S(2)}) copy-start(bf16[512,256]{1,0:T(8,128)(2,1)} %constant.10.clone.refs_0_) | copy-start | bytes 786436
  42.6 48.5 %copy-start.4 = (s32[48,256]{1,0:T(8,128)S(1)}, s32[48,256]{1,0:T(8,128)}, u32[]{:S(2)}) copy-start(s32[48,256]{1,0:T(8,128)} %refs_2_.4) | copy-start | bytes 147460
  296.3 17.2 %all-to-all-start.9 = ((bf16[16,3,32,256]{3,2,1,0:T(8,128)(2,1)}), bf16[16,3,32,256]{3,2,1,0:T(8,128)(2,1)S(1)}, u32[]{:S(2)}, u32[]{:S(2)}) async-start(bf16[16,3,32,256]{3,2,1,0:T(8,128)(2,1)} %trace_blocks.1), calls=%async_computation.9 | async-start | bytes 1572864 | tf_op jit(solution)/shard_map/all_to_all | solution.py:292
  302.7 10.9 %copy-start.5 = (f32[32,48,256]{2,1,0:T(8,128)S(1)}, f32[32,48,256]{2,1,0:T(8,128)}, u32[]{:S(2)}) copy-start(f32[32,48,256]{2,1,0:T(8,128)} %param.8) | copy-start | bytes 4718596

commit v3 on v2

--- a/solution.py
+++ b/solution.py
@@ -73,36 +73,59 @@
     out_ref[...] = flat.reshape(out_ref.shape)
 
 
-def image_kernel(first, bands_ref, refl_ref, out_ref, *more):
-    held_ref = more[0] if first else refl_ref
-    rows, direct, crossed = more[first : first + 3]
-    _, freqs, height, width = refl_ref.shape
+EARLY = (5, 7, 6)
+LATE = (1, 3, 4, 2, 0)
+
+
+def fetch(order, refl_ref, held_ref, sems):
+    share = held_ref.shape[2] // len(order)
+    copies = []
+    for i, k in enumerate(order):
+        start = pl.multiple_of((lax.axis_index("panel") ^ k) * share, share)
+        copies.append(
+            pltpu.make_async_copy(
+                refl_ref.at[:, :, pl.ds(start, share)], held_ref.at[:, :, pl.ds(i * share, share)], sems.at[i]
+            )
+        )
+        copies[-1].start()
+    return copies
+
+
+def image_kernel(order, spread, first, bands_ref, *refs):
+    if spread:
+        refl_ref, *refs = refs
+    else:
+        crossed, refl_ref, *refs = refs
+        direct = bands_ref
+    out_refs, refs = refs[: len(order)], refs[len(order) :]
+    if spread:
+        direct, crossed, *refs = refs
+    held_ref, copies = refl_ref, []
+    if first:
+        held_ref, *refs = refs
+        copies = fetch(order, refl_ref, held_ref, refs[-1])
+
+    _, freqs, height, _ = held_ref.shape
     step = 2 * freqs
-    count = rows.shape[1] // step
-    groups, panels, block, share = out_ref.shape
-
-    copies = []
-    if first:
-        for p in range(panels):
-            part = (slice(None), slice(None), pl.ds(p * share, share))
-            copies.append(pltpu.make_async_copy(refl_ref.at[part], held_ref.at[part], more[-1].at[p]))
-            copies[-1].start()
-
-    fill(rows, bands_ref[...])
-    for j in range(freqs):
-        real, imag = pick(rows, 2 * j, step, count), pick(rows, 2 * j + 1, step, count)
-        direct[j] = jnp.concatenate([real, imag], axis=0).astype(jnp.bfloat16)
-        crossed[j] = jnp.concatenate([-imag, real], axis=0).astype(jnp.bfloat16)
-
-    for p in range(panels):
+    groups, block, share = out_refs[0].shape
+    count = groups * block // step
+    if spread:
+        rows = refs[0]
+        fill(rows, bands_ref[...])
+        for j in range(freqs):
+            real, imag = pick(rows, 2 * j, step, count), pick(rows, 2 * j + 1, step, count)
+            direct[j] = jnp.concatenate([real, imag], axis=0).astype(jnp.bfloat16)
+            crossed[j] = jnp.concatenate([-imag, real], axis=0).astype(jnp.bfloat16)
+
+    for i, out_ref in enumerate(out_refs):
         if first:
-            copies[p].wait()
-        at = slice(p * share, (p + 1) * share)
+            copies[i].wait()
+        at = slice(i * share, (i + 1) * share)
         images = [
             dot_nt(direct[j], held_ref[0, j, at]) + dot_nt(crossed[j], held_ref[1, j, at]) for j in range(freqs)
         ]
         images = jnp.stack(images).reshape(step, count, share)
-        out_ref[:, p] = jnp.swapaxes(images, 0, 1).astype(jnp.bfloat16).reshape(groups, block, share)
+        out_ref[...] = jnp.swapaxes(images, 0, 1).astype(jnp.bfloat16).reshape(groups, block, share)
 
 
 IN_VMEM = pl.BlockSpec(memory_space=pltpu.VMEM)
@@ -122,48 +145,61 @@
     )(*args)
 
 
-def image_blocks(bands, reflection, panels, first):
-    groups, height, width = bands.shape
-    _, freqs, receivers, _ = reflection.shape
-    count = groups * height // (2 * freqs)
-    out_shape = [jax.ShapeDtypeStruct((groups, panels, height, receivers // panels), jnp.bfloat16)]
-    scratch = [
-        pltpu.VMEM((width // 128, groups * height, 128), jnp.float32),
-        pltpu.VMEM((freqs, 2 * count, width), jnp.bfloat16),
-        pltpu.VMEM((freqs, 2 * count, width), jnp.bfloat16),
-    ]
+def image_blocks(order, sources, reflection, panels, first):
+    spread = len(sources) == 1
+    _, freqs, receivers, width = reflection.shape
+    share = receivers // (panels if first else len(order))
+    if spread:
+        groups, height, _ = sources[0].shape
+        count = groups * height // (2 * freqs)
+        by_freq = jax.ShapeDtypeStruct((freqs, 2 * count, width), jnp.bfloat16)
+    else:
+        count = sources[0].shape[1] // 2
+        height = 2 * freqs * count // lax.axis_size("freq")
+        groups = lax.axis_size("freq")
+    out_shape = [jax.ShapeDtypeStruct((groups, height, share), jnp.bfloat16)] * len(order)
+    scratch = []
+    if spread:
+        out_shape += [by_freq, by_freq]
+        scratch.append(pltpu.VMEM((width // 128, groups * height, 128), jnp.float32))
     specs = None
     if first:
-        out_shape.append(pltpu.VMEM(reflection.shape, reflection.dtype))
-        scratch.append(pltpu.SemaphoreType.DMA((panels,)))
-        specs = [IN_VMEM, pl.BlockSpec(memory_space=pltpu.HBM)]
+        out_shape.append(pltpu.VMEM((2, freqs, share * len(order), width), reflection.dtype))
+        scratch.append(pltpu.SemaphoreType.DMA((len(order),)))
+        specs = [IN_VMEM] * len(sources) + [pl.BlockSpec(memory_space=pltpu.HBM)]
         reflection = pltpu.with_memory_space_constraint(reflection, pltpu.HBM)
-    return call(
-        lambda *refs: image_kernel(int(first), *refs),
+    outs = call(
+        lambda *refs: image_kernel(order, spread, first, *refs),
         "image_blocks",
         out_shape,
-        (bands, reflection),
+        (*sources, reflection),
         scratch,
         specs,
-        flops=4 * reflection.size * count,
-    )
-
-
-def return_kernel(bands_ref, refl_ref, *more):
-    out_ref, rows, results = more[-3:]
-    groups, panels, block, width = bands_ref.shape
+        flops=4 * 2 * freqs * share * len(order) * width * count,
+    )
+    blocks, outs = outs[: len(order)], outs[len(order) :]
+    return blocks, outs[:2] if spread else sources, outs[-1] if first else reflection
+
+
+def return_kernel(panels, final, *refs):
+    blocks, refl_ref, refs = refs[:panels], refs[panels], refs[panels + 1 :]
+    groups, block, width = blocks[0].shape
     freqs = refl_ref.shape[1]
     step = 2 * freqs
     count = groups * block // step
     lanes = width // 128
+    if final:
+        before, *more, out_ref, rows, results = refs
+    else:
+        total_ref, rows = refs
 
     for p in range(panels):
-        flat = bands_ref[:, p].reshape(groups * block, width).astype(jnp.float32)
+        flat = blocks[p][...].reshape(groups * block, width).astype(jnp.float32)
         for h in range(lanes):
             rows[p * lanes + h] = flat[:, h * 128 : (h + 1) * 128]
 
     for j in range(freqs):
-        total = None
+        total = before[j] if final else None
         for p in range(panels):
             of_panel = rows.at[pl.ds(p * lanes, lanes)]
             real = pick(of_panel, 2 * j, step, count)
@@ -173,27 +209,37 @@
             at = slice(p * width, (p + 1) * width)
             part = dot(direct, refl_ref[0, j, at]) + dot(crossed, refl_ref[1, j, at])
             total = part if total is None else total + part
-        place(results, 2 * j, step, total[:count])
-        place(results, 2 * j + 1, step, total[count:])
-    emptied(results, out_ref.at[:, :block])
-    if len(more) > 3:
-        out_ref[:, block:] = more[0][...].reshape(groups, -1, width)
-
-
-def return_blocks(bands, reflection, traces=()):
-    groups, panels, height, width = bands.shape
+        if final:
+            place(results, 2 * j, step, total[:count])
+            place(results, 2 * j + 1, step, total[count:])
+        else:
+            total_ref[j] = total
+    if final:
+        emptied(results, out_ref.at[:, :block])
+        for ref in more:
+            out_ref[:, block:] = ref[...].reshape(groups, -1, width)
+
+
+def return_blocks(blocks, reflection, before=None, traces=()):
+    panels = len(blocks)
+    groups, height, width = blocks[0].shape
     _, freqs, _, sources = reflection.shape
+    count = groups * height // (2 * freqs)
+    final = before is not None
     more = sum(t.size // (groups * width) for t in traces)
-    return call(
-        return_kernel,
+    scratch = [pltpu.VMEM((panels * width // 128, groups * height, 128), jnp.float32)]
+    if final:
+        out_shape = jax.ShapeDtypeStruct((groups, height + more, sources), jnp.bfloat16)
+        scratch.append(pltpu.VMEM((sources // 128, groups * height, 128), jnp.float32))
+    else:
+        out_shape = jax.ShapeDtypeStruct((freqs, 2 * count, sources), jnp.float32)
+    return call(
+        lambda *refs: return_kernel(panels, final, *refs),
         "return_blocks",
-        jax.ShapeDtypeStruct((groups, height + more, sources), jnp.bfloat16),
-        (bands, reflection, *traces),
-        [
-            pltpu.VMEM((panels * width // 128, groups * height, 128), jnp.float32),
-            pltpu.VMEM((sources // 128, groups * height, 128), jnp.float32),
-        ],
-        flops=4 * reflection.size * groups * height // (2 * freqs),
+        out_shape,
+        (*blocks, reflection, *([before] if final else []), *traces),
+        scratch,
+        flops=4 * reflection.size * count,
     )
 
 
@@ -226,28 +272,24 @@
     )
 
 
-def upgoing_kernel(rows, ih, il, fh, fl, onsets_ref, parts_ref, out_ref, *traces_ref):
-    groups, panels, height, width = parts_ref.shape
+def upgoing_kernel(rows, ih, il, fh, fl, onsets_ref, images_ref, out_ref, *traces_ref):
+    groups, height, width = images_ref.shape
     for v in range(height // rows):
         at = slice(v * rows, (v + 1) * rows)
-        images = parts_ref[:, 0, at].astype(jnp.float32)
-        for p in range(1, panels):
-            images = images + parts_ref[:, p, at].astype(jnp.float32)
-        traces = windowed(table_times(ih, il, images.reshape(groups * rows, width)), onsets_ref, v)
-        spectra = table_times(fh, fl, traces).astype(jnp.bfloat16).reshape(groups, rows, width)
-        for p in range(panels):
-            out_ref[:, p, at] = spectra
+        images = images_ref[:, at].reshape(groups * rows, width)
+        traces = windowed(table_times(ih, il, images), onsets_ref, v)
+        out_ref[:, at] = table_times(fh, fl, traces).astype(jnp.bfloat16).reshape(groups, rows, width)
         for ref in traces_ref:
             ref[:, v] = traces.astype(jnp.bfloat16).reshape(groups, -1, width)
 
 
-def upgoing_blocks(parts, onsets, tables, rows, with_traces):
-    groups, panels, height, width = parts.shape
-    out_shape = [jax.ShapeDtypeStruct(parts.shape, jnp.bfloat16)]
+def upgoing_blocks(images, onsets, tables, rows, with_traces):
+    groups, height, width = images.shape
+    out_shape = [jax.ShapeDtypeStruct(images.shape, jnp.bfloat16)]
     if with_traces:
         out_shape.append(jax.ShapeDtypeStruct((groups, height // rows, NT // groups, width), jnp.bfloat16))
     return call(
-        lambda *refs: upgoing_kernel(rows, *refs), "upgoing_blocks", out_shape, (*tables, onsets, parts)
+        lambda *refs: upgoing_kernel(rows, *refs), "upgoing_blocks", out_shape, (*tables, onsets, images)
     )
 
 
@@ -290,6 +332,17 @@
 
 def exchange(blocks, axis):
     return lax.all_to_all(blocks, axis, split_axis=0, concat_axis=0, tiled=True)
+
+
+def send(block, k):
+    return lax.ppermute(block, "panel", [(i, i ^ k) for i in range(lax.axis_size("panel"))])
+
+
+def added(*blocks):
+    total = blocks[0].astype(jnp.float32)
+    for block in blocks[1:]:
+        total = total + block.astype(jnp.float32)
+    return total.astype(jnp.bfloat16)
 
 
 def local(reflection, focus_init, onsets):
@@ -302,24 +355,28 @@
     forward, inverse = [[jnp.asarray(t) for t in pair] for pair in band_tables(freqs * groups, NT)]
     tables = inverse + forward
 
-    def to_all(blocks):
-        flat = blocks.reshape((groups * panels,) + blocks.shape[2:])
-        return exchange(flat, ("freq", "panel")).reshape(blocks.shape)
-
     def in_time(samples):
         samples = samples.reshape(groups, count, share, width)
         return jnp.transpose(samples, (2, 0, 1, 3)).reshape(share, sources, width).astype(jnp.float32)
 
     sent = focus_init.astype(jnp.bfloat16).reshape(share, groups, count, width).transpose(1, 2, 0, 3)
     first, blocks = start_bands(exchange(sent, "freq"), forward, rows)
+    early = late = reflection
     for iteration in range(ITERS):
-        last = iteration == ITERS - 1
+        is_first, last = iteration == 0, iteration == ITERS - 1
         bands = exchange(blocks, "freq")
-        images = image_blocks(bands, reflection, panels, iteration == 0)
-        if iteration == 0:
-            reflection = images[1]
-        spectra, *traces = upgoing_blocks(to_all(images[0]), onsets, tables, rows, last)
-        returns = exchange(return_blocks(to_all(spectra), reflection, traces), "freq")
+        (b5, b7, b6), by_freq, early = image_blocks(EARLY, (bands,), early, panels, is_first)
+        r5, r7, r6 = send(b5, 1), send(b7, 3), send(b6, 4)
+        (b1, b3, b4, b2, b0), _, late = image_blocks(LATE, tuple(by_freq), late, panels, is_first)
+        s1, s3 = send(b1, 1), send(b3, 3)
+        s2, s4 = send(added(b2, r6), 2), send(added(b4, r5, r7), 4)
+        images = exchange(added(b0, s1, s3, s2, s4), "freq")
+        spectra, *traces = upgoing_blocks(images, onsets, tables, rows, last)
+        m0 = exchange(spectra, "freq")
+        m2, m4, m1, m3 = send(m0, 2), send(m0, 4), send(m0, 1), send(m0, 3)
+        m6, m5, m7 = send(m2, 4), send(m4, 1), send(m4, 3)
+        partial = return_blocks((m1, m3, m4, m2, m0), late)
+        returns = exchange(return_blocks((m5, m7, m6), early, partial, traces), "freq")
         if last:
             upgoing = in_time(returns[:, count * rows :])
             traces = trace_blocks(returns, onsets, inverse, rows, count)

time: 316 us -> 286 us (0.905)
  blocking collectives: 264 us -> 128 us
  waiting for transfers between devices: 10.7 us -> 79.1 us
  starting transfers between devices: 4.1 us -> 40.4 us
    all_to_all x9, blocking collectives: 264 us -> 128 us  [exchange(): return lax.all_to_all(blocks, axis, split_axis=0, concat_axis=0, tiled=True)]
    ppermute x0 -> x28, waiting for transfers between devices: none -> 68.3 us  [send(): lax.ppermute(block, 'panel', [(i, i ^ k) for i in range(lax.axis_size('pa...]
    ppermute x0 -> x28, starting transfers between devices: none -> 36.3 us  [send(): lax.ppermute(block, 'panel', [(i, i ^ k) for i in range(lax.axis_size('pa...]
    pallas_call x9 -> x13, Pallas kernels: 29.4 us -> 30.2 us  [call(): pl.pallas_call(kernel, in_specs=specs or [IN_VMEM] * len(args), out_specs...]
  transfers between devices with their start and end apart: 1 -> 29, of which waited for: 1 -> 14; matrix products, arithmetic and copies ran while one was open for 1% -> 1% of each run, Pallas kernels for 0% -> 5%
where the time goes in v3:
time: 286 us
  blocking collectives  128 us (45%)
  waiting for transfers between devices  79.1 us (28%)
  starting transfers between devices  40.4 us (14%)
  Pallas kernels  30.2 us (11%)
  other arithmetic  4.95 us (2%)
    all_to_all x9, blocking collectives, exchange(): return lax.all_to_all(blocks, axis, split_axis=0, concat_axis=0, tiled=True)  128 us
    ppermute x28, waiting for transfers between devices, send(): lax.ppermute(block, 'panel', [(i, i ^ k) for i in range(lax.axis_size('pa...  68.3 us
    ppermute x28, starting transfers between devices, send(): lax.ppermute(block, 'panel', [(i, i ^ k) for i in range(lax.axis_size('pa...  36.3 us
    pallas_call x13, Pallas kernels, call(): pl.pallas_call(kernel, in_specs=specs or [IN_VMEM] * len(args), out_specs...  30.2 us
    all_to_all x1, waiting for transfers between devices, exchange(): return lax.all_to_all(blocks, axis, split_axis=0, concat_axis=0, tiled=True)  10.7 us
  transfers between devices with their start and end apart: 29, of which 14 were waited for; matrix products, arithmetic and copies ran while one was open for 1% of the time, Pallas kernels for 5%

profile of v3, /device:TPU:1, one launch (start us, length us, event | category | flops | bytes accessed | tf_op | source)
XLA Modules:
  0.0 285.9 jit_solution(160390125127001978)
XLA Ops:
  0.6 1.5 convert_element_type.102
  2.4 19.5 %all_to_all.50.traces_ref = bf16[16,3,32,256]{3,2,1,0:T(8,128)(2,1)S(1)} all-to-all(bf16[16,3,32,256]{3,2,1,0:T(8,128)(2,1)S(1)} %bitcast.13), channel_id=1, replica_groups=mesh['freq'=16,'panel'=8] {'freq'}, dimensions={0} | all-to-all | bytes 1572864 | tf_op jit(solution)/shard_map/all_to_all | solution.py:334
  21.9 0.6 start_bands.1
  22.5 11.9 %all_to_all.51.refs_0_ = bf16[16,48,256]{2,1,0:T(8,128)(2,1)S(1)} all-to-all(bf16[16,48,256]{2,1,0:T(8,128)(2,1)S(1)} %get-tuple-element.29), channel_id=1, replica_groups=mesh['freq'=16,'panel'=8] {'freq'}, dimensions={0} | all-to-all | bytes 786432 | tf_op jit(solution)/shard_map/all_to_all | solution.py:334
  34.4 4.1 %image_blocks.4 = (bf16[16,48,256]{2,1,0:T(8,128)(2,1)S(1)}, bf16[16,48,256]{2,1,0:T(8,128)(2,1)S(1)}, bf16[16,48,256]{2,1,0:T(8,128)(2,1)S(1)}, bf16[8,96,256]{...) custom-call(bf16[16,48,256]{2,1,0:T(8,128)(2,1)S(1)} %all_to_all.51.refs_0_, ...), custom_call_target="tpu_custom_call" | custom-call | flops 603979776 | bytes 34340864 | tf_op jit(solution)/shard_map/image_blocks/pallas_call | solution.py:136
  38.4 2.5 collective-permute-start.2
  41.0 1.6 collective-permute-start.4
  42.6 2.2 collective-permute-start.5
  44.8 5.7 %image_blocks.5 = (bf16[16,48,256]{2,1,0:T(8,128)(2,1)S(1)}, bf16[16,48,256]{2,1,0:T(8,128)(2,1)S(1)}, bf16[16,48,256]{2,1,0:T(8,128)(2,1)S(1)}, bf16[16,48,256]...) custom-call(bf16[8,96,256]{2,1,0:T(8,128)(2,1)S(1)} %get-tuple-element.30.refs_0_, ...), custom_call_target="tpu_custom_call" | custom-call | flops 1006632960 | bytes 35127296 | tf_op jit(solution)/shard_map/image_blocks/pallas_call | solution.py:136
  50.5 0.8 collective-permute-start
  51.3 0.6 collective-permute-start.1
  52.1 2.0 collective-permute-start.3
  54.2 1.7 collective-permute-start.6
  55.9 3.3 %collective-permute-done = bf16[16,48,256]{2,1,0:T(8,128)(2,1)S(1)} collective-permute-done((bf16[16,48,256]{2,1,0:T(8,128)(2,1)S(1)}, bf16[16,48,256]{2,1,0:T(8,128)(2,1)S(1)}, u32[]{:S(2)}, u32[]{:S(2)}) %collective-permute-start) | collective-permute-done | bytes 393248 | tf_op jit(solution)/shard_map/ppermute | solution.py:338
  59.2 4.0 %collective-permute-done.1 = bf16[16,48,256]{2,1,0:T(8,128)(2,1)S(1)} collective-permute-done((bf16[16,48,256]{2,1,0:T(8,128)(2,1)S(1)}, bf16[16,48,256]{2,1,0:T(8,128)(2,1)S(1)}, u32[]{:S(2)}, u32[]{:S(2)}) %collective-permute-start.1) | collective-permute-done | bytes 393248 | tf_op jit(solution)/shard_map/ppermute | solution.py:338
  63.2 7.2 %collective-permute-done.3 = bf16[16,48,256]{2,1,0:T(8,128)(2,1)S(1)} collective-permute-done((bf16[16,48,256]{2,1,0:T(8,128)(2,1)S(1)}, bf16[16,48,256]{2,1,0:T(8,128)(2,1)S(1)}, u32[]{:S(2)}, u32[]{:S(2)}) %collective-permute-start.3) | collective-permute-done | bytes 393248 | tf_op jit(solution)/shard_map/ppermute | solution.py:338
  70.7 13.4 %all_to_all.52.refs_5_ = bf16[16,48,256]{2,1,0:T(8,128)(2,1)S(1)} all-to-all(bf16[16,48,256]{2,1,0:T(8,128)(2,1)S(1)} %add_convert_fusion.3), channel_id=1, replica_groups=mesh['freq'=16,'panel'=8] {'freq'}, dimensions={0} | all-to-all | bytes 786432 | tf_op jit(solution)/shard_map/all_to_all | solution.py:334
  84.1 1.5 upgoing_blocks.2
  85.7 12.1 %all_to_all.53.refs_4_ = bf16[16,48,256]{2,1,0:T(8,128)(2,1)S(1)} all-to-all(bf16[16,48,256]{2,1,0:T(8,128)(2,1)S(1)} %upgoing_blocks.2), channel_id=1, replica_groups=mesh['freq'=16,'panel'=8] {'freq'}, dimensions={0} | all-to-all | bytes 786432 | tf_op jit(solution)/shard_map/all_to_all | solution.py:334
  97.8 1.5 collective-permute-start.10
  99.2 1.5 collective-permute-start.7
  100.7 0.6 collective-permute-start.13
  101.3 0.6 collective-permute-start.12
  101.9 6.8 %collective-permute-done.10.refs_3_ = bf16[16,48,256]{2,1,0:T(8,128)(2,1)S(1)} collective-permute-done((bf16[16,48,256]{2,1,0:T(8,128)(2,1)S(1)}, bf16[16,48,256]{2,1,0:T(8,128)(2,1)S(1)}, u32[]{:S(2)}, u32[]{:S(2)}) %collective-permute-start.10) | collective-permute-done | bytes 393248 | tf_op jit(solution)/shard_map/ppermute | solution.py:338
  108.7 1.5 collective-permute-start.11
  110.2 1.6 collective-permute-start.9
  111.9 6.8 %collective-permute-done.13.refs_1_ = bf16[16,48,256]{2,1,0:T(8,128)(2,1)S(1)} collective-permute-done((bf16[16,48,256]{2,1,0:T(8,128)(2,1)S(1)}, bf16[16,48,256]{2,1,0:T(8,128)(2,1)S(1)}, u32[]{:S(2)}, u32[]{:S(2)}) %collective-permute-start.13) | collective-permute-done | bytes 393248 | tf_op jit(solution)/shard_map/ppermute | solution.py:338
  118.7 2.3 return_blocks.4.refs_4_
  121.1 6.1 %collective-permute-done.9.refs_1_ = bf16[16,48,256]{2,1,0:T(8,128)(2,1)S(1)} collective-permute-done((bf16[16,48,256]{2,1,0:T(8,128)(2,1)S(1)}, bf16[16,48,256]{2,1,0:T(8,128)(2,1)S(1)}, u32[]{:S(2)}, u32[]{:S(2)}) %collective-permute-start.9) | collective-permute-done | bytes 393248 | tf_op jit(solution)/shard_map/ppermute | solution.py:338
  127.2 1.7 return_blocks.5
  128.9 11.9 %all_to_all.54.refs_6_ = bf16[16,48,256]{2,1,0:T(8,128)(2,1)S(1)} all-to-all(bf16[16,48,256]{2,1,0:T(8,128)(2,1)S(1)} %return_blocks.5), channel_id=1, replica_groups=mesh['freq'=16,'panel'=8] {'freq'}, dimensions={0} | all-to-all | bytes 786432 | tf_op jit(solution)/shard_map/all_to_all | solution.py:334
  140.8 1.5 focus_blocks.1
  142.3 12.1 %all_to_all.55.refs_0_ = bf16[16,48,256]{2,1,0:T(8,128)(2,1)S(1)} all-to-all(bf16[16,48,256]{2,1,0:T(8,128)(2,1)S(1)} %focus_blocks.1), channel_id=1, replica_groups=mesh['freq'=16,'panel'=8] {'freq'}, dimensions={0} | all-to-all | bytes 786432 | tf_op jit(solution)/shard_map/all_to_all | solution.py:334
  154.4 2.2 image_blocks.6
  156.6 1.6 collective-permute-start.16
  158.2 1.8 collective-permute-start.19
  160.0 3.4 %image_blocks.7 = (bf16[16,48,256]{2,1,0:T(8,128)(2,1)S(1)}, bf16[16,48,256]{2,1,0:T(8,128)(2,1)S(1)}, bf16[16,48,256]{2,1,0:T(8,128)(2,1)S(1)}, bf16[16,48,256]...) custom-call(bf16[8,96,256]{2,1,0:T(8,128)(2,1)S(1)} %get-tuple-element.42.refs_0_, ...), custom_call_target="tpu_custom_call" | custom-call | flops 1006632960 | bytes 22544384 | tf_op jit(solution)/shard_map/image_blocks/pallas_call | solution.py:136
  163.4 0.8 collective-permute-start.14
  164.2 1.0 collective-permute-start.15
  165.2 2.4 collective-permute-done.16
  167.7 1.6 collective-permute-start.17
  169.5 1.6 collective-permute-start.20
  171.0 4.7 %collective-permute-done.14 = bf16[16,48,256]{2,1,0:T(8,128)(2,1)S(1)} collective-permute-done((bf16[16,48,256]{2,1,0:T(8,128)(2,1)S(1)}, bf16[16,48,256]{2,1,0:T(8,128)(2,1)S(1)}, u32[]{:S(2)}, u32[]{:S(2)}) %collective-permute-start.14) | collective-permute-done | bytes 393248 | tf_op jit(solution)/shard_map/ppermute | solution.py:338
  175.8 1.0 collective-permute-done.15
  176.7 8.8 %collective-permute-done.17 = bf16[16,48,256]{2,1,0:T(8,128)(2,1)S(1)} collective-permute-done((bf16[16,48,256]{2,1,0:T(8,128)(2,1)S(1)}, bf16[16,48,256]{2,1,0:T(8,128)(2,1)S(1)}, u32[]{:S(2)}, u32[]{:S(2)}) %collective-permute-start.17) | collective-permute-done | bytes 393248 | tf_op jit(solution)/shard_map/ppermute | solution.py:338
  185.8 13.4 %all_to_all.56.refs_5_ = bf16[16,48,256]{2,1,0:T(8,128)(2,1)S(1)} all-to-all(bf16[16,48,256]{2,1,0:T(8,128)(2,1)S(1)} %add_convert_fusion), channel_id=1, replica_groups=mesh['freq'=16,'panel'=8] {'freq'}, dimensions={0} | all-to-all | bytes 786432 | tf_op jit(solution)/shard_map/all_to_all | solution.py:334
  199.2 1.5 upgoing_blocks.3
  200.8 12.1 %all_to_all.57.refs_4_ = bf16[16,48,256]{2,1,0:T(8,128)(2,1)S(1)} all-to-all(bf16[16,48,256]{2,1,0:T(8,128)(2,1)S(1)} %get-tuple-element.52), channel_id=1, replica_groups=mesh['freq'=16,'panel'=8] {'freq'}, dimensions={0} | all-to-all | bytes 786432 | tf_op jit(solution)/shard_map/all_to_all | solution.py:334
  212.8 1.5 collective-permute-start.24
  214.3 2.5 collective-permute-start.21
  216.8 1.0 collective-permute-start.27
  217.9 5.9 %collective-permute-done.24.refs_3_ = bf16[16,48,256]{2,1,0:T(8,128)(2,1)S(1)} collective-permute-done((bf16[16,48,256]{2,1,0:T(8,128)(2,1)S(1)}, bf16[16,48,256]{2,1,0:T(8,128)(2,1)S(1)}, u32[]{:S(2)}, u32[]{:S(2)}) %collective-permute-start.24) | collective-permute-done | bytes 393248 | tf_op jit(solution)/shard_map/ppermute | solution.py:338
  223.8 2.5 collective-permute-start.25
  226.3 1.6 collective-permute-start.23
  227.9 5.9 %collective-permute-done.27.refs_1_ = bf16[16,48,256]{2,1,0:T(8,128)(2,1)S(1)} collective-permute-done((bf16[16,48,256]{2,1,0:T(8,128)(2,1)S(1)}, bf16[16,48,256]{2,1,0:T(8,128)(2,1)S(1)}, u32[]{:S(2)}, u32[]{:S(2)}) %collective-permute-start.27) | collective-permute-done | bytes 393248 | tf_op jit(solution)/shard_map/ppermute | solution.py:338
  233.8 2.3 return_blocks.6.refs_4_
  236.1 5.3 %collective-permute-done.23.refs_1_ = bf16[16,48,256]{2,1,0:T(8,128)(2,1)S(1)} collective-permute-done((bf16[16,48,256]{2,1,0:T(8,128)(2,1)S(1)}, bf16[16,48,256]{2,1,0:T(8,128)(2,1)S(1)}, u32[]{:S(2)}, u32[]{:S(2)}) %collective-permute-start.23) | collective-permute-done | bytes 393248 | tf_op jit(solution)/shard_map/ppermute | solution.py:338
  241.4 1.7 return_blocks.7
  243.2 21.7 %all_to_all.58.refs_3_ = bf16[16,144,256]{2,1,0:T(8,128)(2,1)S(1)} all-to-all(bf16[16,144,256]{2,1,0:T(8,128)(2,1)S(1)} %return_blocks.7), channel_id=1, replica_groups=mesh['freq'=16,'panel'=8] {'freq'}, dimensions={0} | all-to-all | bytes 2359296 | tf_op jit(solution)/shard_map/all_to_all | solution.py:334
  264.9 1.6 trace_blocks.1
  266.5 4.1 %all-to-all-start.9 = ((bf16[16,3,32,256]{3,2,1,0:T(8,128)(2,1)}), bf16[16,3,32,256]{3,2,1,0:T(8,128)(2,1)S(1)}, u32[]{:S(2)}, u32[]{:S(2)}) async-start(bf16[16,3,32,256]{3,2,1,0:T(8,128)(2,1)} %trace_blocks.1), calls=%async_computation.9 | async-start | bytes 1572864 | tf_op jit(solution)/shard_map/all_to_all | solution.py:334
  270.8 2.1 copy.14
  272.9 10.7 %all-to-all-done.9 = bf16[16,3,32,256]{3,2,1,0:T(8,128)(2,1)S(1)} async-done(((bf16[16,3,32,256]{3,2,1,0:T(8,128)(2,1)}), bf16[16,3,32,256]{3,2,1,0:T(8,128)(2,1)S(1)}, u32[]{:S(2)}, u32[]{:S(2)}) %all-to-all-start.9) | async-done | bytes 786464 | tf_op jit(solution)/shard_map/all_to_all | solution.py:334
  283.8 2.1 copy_add_fusion
  (41 shorter events, 1.9 us)
Async XLA Ops:
  2.1 19.8 %copy-start.2 = (bf16[256,512]{1,0:T(8,128)(2,1)S(1)}, bf16[256,512]{1,0:T(8,128)(2,1)}, u32[]{:S(2)}) copy-start(bf16[256,512]{1,0:T(8,128)(2,1)} %constant.9.clone.low.refs_3_) | copy-start | bytes 786436
  2.1 19.8 %copy-start.3 = (bf16[256,512]{1,0:T(8,128)(2,1)S(1)}, bf16[256,512]{1,0:T(8,128)(2,1)}, u32[]{:S(2)}) copy-start(bf16[256,512]{1,0:T(8,128)(2,1)} %constant.8.clone.high.refs_2_) | copy-start | bytes 786436
  38.4 13.5 %collective-permute-start.2 = (bf16[16,48,256]{2,1,0:T(8,128)(2,1)S(1)}, bf16[16,48,256]{2,1,0:T(8,128)(2,1)S(1)}, u32[]{:S(2)}, u32[]{:S(2)}) collective-permute-start(bf16[16,48,256]{2,1,0:T(8,128)(2,1)S(1)} %get-tuple-element.36), channel_id=1, source_target_pairs={{0,4},{1,5},{2,6},{3,7},{4,0},{5,1},{6,2},{7,3},{8,12},{9,13},{10,... | collective-permute-start | bytes 1179656 | tf_op jit(solution)/shard_map/ppermute | solution.py:338
  41.0 13.1 %collective-permute-start.4 = (bf16[16,48,256]{2,1,0:T(8,128)(2,1)S(1)}, bf16[16,48,256]{2,1,0:T(8,128)(2,1)S(1)}, u32[]{:S(2)}, u32[]{:S(2)}) collective-permute-start(bf16[16,48,256]{2,1,0:T(8,128)(2,1)S(1)} %get-tuple-element.38), channel_id=1, source_target_pairs={{0,1},{1,0},{2,3},{3,2},{4,5},{5,4},{6,7},{7,6},{8,9},{9,8},{10,11... | collective-permute-start | bytes 1179656 | tf_op jit(solution)/shard_map/ppermute | solution.py:338
  42.6 11.4 %collective-permute-start.5 = (bf16[16,48,256]{2,1,0:T(8,128)(2,1)S(1)}, bf16[16,48,256]{2,1,0:T(8,128)(2,1)S(1)}, u32[]{:S(2)}, u32[]{:S(2)}) collective-permute-start(bf16[16,48,256]{2,1,0:T(8,128)(2,1)S(1)} %get-tuple-element.39), channel_id=1, source_target_pairs={{0,3},{1,2},{2,1},{3,0},{4,7},{5,6},{6,5},{7,4},{8,11},{9,10},{10,... | collective-permute-start | bytes 1179656 | tf_op jit(solution)/shard_map/ppermute | solution.py:338
  50.5 8.7 %collective-permute-start = (bf16[16,48,256]{2,1,0:T(8,128)(2,1)S(1)}, bf16[16,48,256]{2,1,0:T(8,128)(2,1)S(1)}, u32[]{:S(2)}, u32[]{:S(2)}) collective-permute-start(bf16[16,48,256]{2,1,0:T(8,128)(2,1)S(1)} %get-tuple-element.33), channel_id=1, source_target_pairs={{0,1},{1,0},{2,3},{3,2},{4,5},{5,4},{6,7},{7,6},{8,9},{9,8},{10,11... | collective-permute-start | bytes 1179656 | tf_op jit(solution)/shard_map/ppermute | solution.py:338
  51.3 11.9 %collective-permute-start.1 = (bf16[16,48,256]{2,1,0:T(8,128)(2,1)S(1)}, bf16[16,48,256]{2,1,0:T(8,128)(2,1)S(1)}, u32[]{:S(2)}, u32[]{:S(2)}) collective-permute-start(bf16[16,48,256]{2,1,0:T(8,128)(2,1)S(1)} %get-tuple-element.34), channel_id=1, source_target_pairs={{0,3},{1,2},{2,1},{3,0},{4,7},{5,6},{6,5},{7,4},{8,11},{9,10},{10,... | collective-permute-start | bytes 1179656 | tf_op jit(solution)/shard_map/ppermute | solution.py:338
  52.1 18.4 %collective-permute-start.3 = (bf16[16,48,256]{2,1,0:T(8,128)(2,1)S(1)}, bf16[16,48,256]{2,1,0:T(8,128)(2,1)S(1)}, u32[]{:S(2)}, u32[]{:S(2)}) collective-permute-start(bf16[16,48,256]{2,1,0:T(8,128)(2,1)S(1)} %add_convert_fusion.5), channel_id=1, source_target_pairs={{0,2},{1,3},{2,0},{3,1},{4,6},{5,7},{6,4},{7,5},{8,10},{9,11},{10,... | collective-permute-start | bytes 1179656 | tf_op jit(solution)/shard_map/ppermute | solution.py:338
  54.2 16.2 %collective-permute-start.6 = (bf16[16,48,256]{2,1,0:T(8,128)(2,1)S(1)}, bf16[16,48,256]{2,1,0:T(8,128)(2,1)S(1)}, u32[]{:S(2)}, u32[]{:S(2)}) collective-permute-start(bf16[16,48,256]{2,1,0:T(8,128)(2,1)S(1)} %add_convert_fusion.4), channel_id=1, source_target_pairs={{0,4},{1,5},{2,6},{3,7},{4,0},{5,1},{6,2},{7,3},{8,12},{9,13},{10,... | collective-permute-start | bytes 1179656 | tf_op jit(solution)/shard_map/ppermute | solution.py:338
  70.4 13.7 %copy-start = (bf16[512,256]{1,0:T(8,128)(2,1)S(1)}, bf16[512,256]{1,0:T(8,128)(2,1)}, u32[]{:S(2)}) copy-start(bf16[512,256]{1,0:T(8,128)(2,1)} %constant.11.clone.refs_1_) | copy-start | bytes 786436
  70.4 13.7 %copy-start.1 = (bf16[512,256]{1,0:T(8,128)(2,1)S(1)}, bf16[512,256]{1,0:T(8,128)(2,1)}, u32[]{:S(2)}) copy-start(bf16[512,256]{1,0:T(8,128)(2,1)} %constant.10.clone.refs_0_) | copy-start | bytes 786436
  70.4 13.7 %copy-start.4 = (s32[48,256]{1,0:T(8,128)S(1)}, s32[48,256]{1,0:T(8,128)}, u32[]{:S(2)}) copy-start(s32[48,256]{1,0:T(8,128)} %refs_2_.6) | copy-start | bytes 147460
  97.8 11.0 %collective-permute-start.10 = (bf16[16,48,256]{2,1,0:T(8,128)(2,1)S(1)}, bf16[16,48,256]{2,1,0:T(8,128)(2,1)S(1)}, u32[]{:S(2)}, u32[]{:S(2)}) collective-permute-start(bf16[16,48,256]{2,1,0:T(8,128)(2,1)S(1)} %all_to_all.53.refs_4_), channel_id=1, source_target_pairs={{0,2},{1,3},{2,0},{3,1},{4,6},{5,7},{6,4},{7,5},{8,10},{9,11},{10,... | collective-permute-start | bytes 1179656 | tf_op jit(solution)/shard_map/ppermute | solution.py:338
  99.2 11.0 %collective-permute-start.7 = (bf16[16,48,256]{2,1,0:T(8,128)(2,1)S(1)}, bf16[16,48,256]{2,1,0:T(8,128)(2,1)S(1)}, u32[]{:S(2)}, u32[]{:S(2)}) collective-permute-start(bf16[16,48,256]{2,1,0:T(8,128)(2,1)S(1)} %all_to_all.53.refs_4_), channel_id=1, source_target_pairs={{0,4},{1,5},{2,6},{3,7},{4,0},{5,1},{6,2},{7,3},{8,12},{9,13},{10,... | collective-permute-start | bytes 1179656 | tf_op jit(solution)/shard_map/ppermute | solution.py:338
  100.7 18.0 %collective-permute-start.13 = (bf16[16,48,256]{2,1,0:T(8,128)(2,1)S(1)}, bf16[16,48,256]{2,1,0:T(8,128)(2,1)S(1)}, u32[]{:S(2)}, u32[]{:S(2)}) collective-permute-start(bf16[16,48,256]{2,1,0:T(8,128)(2,1)S(1)} %all_to_all.53.refs_4_), channel_id=1, source_target_pairs={{0,3},{1,2},{2,1},{3,0},{4,7},{5,6},{6,5},{7,4},{8,11},{9,10},{10,... | collective-permute-start | bytes 1179656 | tf_op jit(solution)/shard_map/ppermute | solution.py:338
  101.3 17.4 %collective-permute-start.12 = (bf16[16,48,256]{2,1,0:T(8,128)(2,1)S(1)}, bf16[16,48,256]{2,1,0:T(8,128)(2,1)S(1)}, u32[]{:S(2)}, u32[]{:S(2)}) collective-permute-start(bf16[16,48,256]{2,1,0:T(8,128)(2,1)S(1)} %all_to_all.53.refs_4_), channel_id=1, source_target_pairs={{0,1},{1,0},{2,3},{3,2},{4,5},{5,4},{6,7},{7,6},{8,9},{9,8},{10,11... | collective-permute-start | bytes 1179656 | tf_op jit(solution)/shard_map/ppermute | solution.py:338
  108.7 12.3 %collective-permute-start.11 = (bf16[16,48,256]{2,1,0:T(8,128)(2,1)S(1)}, bf16[16,48,256]{2,1,0:T(8,128)(2,1)S(1)}, u32[]{:S(2)}, u32[]{:S(2)}) collective-permute-start(bf16[16,48,256]{2,1,0:T(8,128)(2,1)S(1)} %collective-permute-done.10.refs_3_), channel_id=1, source_target_pairs={{0,4},{1,5},{2,6},{3,7},{4,0},{5,1},{6,2},{7,3},{8,12},{9,13},{10,... | collective-permute-start | bytes 1179656 | tf_op jit(solution)/shard_map/ppermute | solution.py:338
  110.2 16.9 %collective-permute-start.9 = (bf16[16,48,256]{2,1,0:T(8,128)(2,1)S(1)}, bf16[16,48,256]{2,1,0:T(8,128)(2,1)S(1)}, u32[]{:S(2)}, u32[]{:S(2)}) collective-permute-start(bf16[16,48,256]{2,1,0:T(8,128)(2,1)S(1)} %collective-permute-done.7.refs_2_), channel_id=1, source_target_pairs={{0,3},{1,2},{2,1},{3,0},{4,7},{5,6},{6,5},{7,4},{8,11},{9,10},{10,... | collective-permute-start | bytes 1179656 | tf_op jit(solution)/shard_map/ppermute | solution.py:338
  111.9 15.3 %collective-permute-start.8 = (bf16[16,48,256]{2,1,0:T(8,128)(2,1)S(1)}, bf16[16,48,256]{2,1,0:T(8,128)(2,1)S(1)}, u32[]{:S(2)}, u32[]{:S(2)}) collective-permute-start(bf16[16,48,256]{2,1,0:T(8,128)(2,1)S(1)} %collective-permute-done.7.refs_2_), channel_id=1, source_target_pairs={{0,1},{1,0},{2,3},{3,2},{4,5},{5,4},{6,7},{7,6},{8,9},{9,8},{10,11... | collective-permute-start | bytes 1179656 | tf_op jit(solution)/shard_map/ppermute | solution.py:338
  156.6 11.0 %collective-permute-start.16 = (bf16[16,48,256]{2,1,0:T(8,128)(2,1)S(1)}, bf16[16,48,256]{2,1,0:T(8,128)(2,1)S(1)}, u32[]{:S(2)}, u32[]{:S(2)}) collective-permute-start(bf16[16,48,256]{2,1,0:T(8,128)(2,1)S(1)} %get-tuple-element.48), channel_id=1, source_target_pairs={{0,4},{1,5},{2,6},{3,7},{4,0},{5,1},{6,2},{7,3},{8,12},{9,13},{10,... | collective-permute-start | bytes 1179656 | tf_op jit(solution)/shard_map/ppermute | solution.py:338
  158.2 11.1 %collective-permute-start.18 = (bf16[16,48,256]{2,1,0:T(8,128)(2,1)S(1)}, bf16[16,48,256]{2,1,0:T(8,128)(2,1)S(1)}, u32[]{:S(2)}, u32[]{:S(2)}) collective-permute-start(bf16[16,48,256]{2,1,0:T(8,128)(2,1)S(1)} %get-tuple-element.50), channel_id=1, source_target_pairs={{0,1},{1,0},{2,3},{3,2},{4,5},{5,4},{6,7},{7,6},{8,9},{9,8},{10,11... | collective-permute-start | bytes 1179656 | tf_op jit(solution)/shard_map/ppermute | solution.py:338
  158.2 11.1 %collective-permute-start.19 = (bf16[16,48,256]{2,1,0:T(8,128)(2,1)S(1)}, bf16[16,48,256]{2,1,0:T(8,128)(2,1)S(1)}, u32[]{:S(2)}, u32[]{:S(2)}) collective-permute-start(bf16[16,48,256]{2,1,0:T(8,128)(2,1)S(1)} %get-tuple-element.51), channel_id=1, source_target_pairs={{0,3},{1,2},{2,1},{3,0},{4,7},{5,6},{6,5},{7,4},{8,11},{9,10},{10,... | collective-permute-start | bytes 1179656 | tf_op jit(solution)/shard_map/ppermute | solution.py:338
  163.4 12.4 %collective-permute-start.14 = (bf16[16,48,256]{2,1,0:T(8,128)(2,1)S(1)}, bf16[16,48,256]{2,1,0:T(8,128)(2,1)S(1)}, u32[]{:S(2)}, u32[]{:S(2)}) collective-permute-start(bf16[16,48,256]{2,1,0:T(8,128)(2,1)S(1)} %get-tuple-element.45), channel_id=1, source_target_pairs={{0,1},{1,0},{2,3},{3,2},{4,5},{5,4},{6,7},{7,6},{8,9},{9,8},{10,11... | collective-permute-start | bytes 1179656 | tf_op jit(solution)/shard_map/ppermute | solution.py:338
  164.2 12.5 %collective-permute-start.15 = (bf16[16,48,256]{2,1,0:T(8,128)(2,1)S(1)}, bf16[16,48,256]{2,1,0:T(8,128)(2,1)S(1)}, u32[]{:S(2)}, u32[]{:S(2)}) collective-permute-start(bf16[16,48,256]{2,1,0:T(8,128)(2,1)S(1)} %get-tuple-element.46), channel_id=1, source_target_pairs={{0,3},{1,2},{2,1},{3,0},{4,7},{5,6},{6,5},{7,4},{8,11},{9,10},{10,... | collective-permute-start | bytes 1179656 | tf_op jit(solution)/shard_map/ppermute | solution.py:338
  167.7 17.8 %collective-permute-start.17 = (bf16[16,48,256]{2,1,0:T(8,128)(2,1)S(1)}, bf16[16,48,256]{2,1,0:T(8,128)(2,1)S(1)}, u32[]{:S(2)}, u32[]{:S(2)}) collective-permute-start(bf16[16,48,256]{2,1,0:T(8,128)(2,1)S(1)} %add_convert_fusion.2), channel_id=1, source_target_pairs={{0,2},{1,3},{2,0},{3,1},{4,6},{5,7},{6,4},{7,5},{8,10},{9,11},{10,... | collective-permute-start | bytes 1179656 | tf_op jit(solution)/shard_map/ppermute | solution.py:338
  169.5 16.1 %collective-permute-start.20 = (bf16[16,48,256]{2,1,0:T(8,128)(2,1)S(1)}, bf16[16,48,256]{2,1,0:T(8,128)(2,1)S(1)}, u32[]{:S(2)}, u32[]{:S(2)}) collective-permute-start(bf16[16,48,256]{2,1,0:T(8,128)(2,1)S(1)} %add_convert_fusion.1), channel_id=1, source_target_pairs={{0,4},{1,5},{2,6},{3,7},{4,0},{5,1},{6,2},{7,3},{8,12},{9,13},{10,... | collective-permute-start | bytes 1179656 | tf_op jit(solution)/shard_map/ppermute | solution.py:338
  212.8 11.0 %collective-permute-start.24 = (bf16[16,48,256]{2,1,0:T(8,128)(2,1)S(1)}, bf16[16,48,256]{2,1,0:T(8,128)(2,1)S(1)}, u32[]{:S(2)}, u32[]{:S(2)}) collective-permute-start(bf16[16,48,256]{2,1,0:T(8,128)(2,1)S(1)} %all_to_all.57.refs_4_), channel_id=1, source_target_pairs={{0,2},{1,3},{2,0},{3,1},{4,6},{5,7},{6,4},{7,5},{8,10},{9,11},{10,... | collective-permute-start | bytes 1179656 | tf_op jit(solution)/shard_map/ppermute | solution.py:338
  214.3 12.0 %collective-permute-start.21 = (bf16[16,48,256]{2,1,0:T(8,128)(2,1)S(1)}, bf16[16,48,256]{2,1,0:T(8,128)(2,1)S(1)}, u32[]{:S(2)}, u32[]{:S(2)}) collective-permute-start(bf16[16,48,256]{2,1,0:T(8,128)(2,1)S(1)} %all_to_all.57.refs_4_), channel_id=1, source_target_pairs={{0,4},{1,5},{2,6},{3,7},{4,0},{5,1},{6,2},{7,3},{8,12},{9,13},{10,... | collective-permute-start | bytes 1179656 | tf_op jit(solution)/shard_map/ppermute | solution.py:338
  216.8 17.0 %collective-permute-start.27 = (bf16[16,48,256]{2,1,0:T(8,128)(2,1)S(1)}, bf16[16,48,256]{2,1,0:T(8,128)(2,1)S(1)}, u32[]{:S(2)}, u32[]{:S(2)}) collective-permute-start(bf16[16,48,256]{2,1,0:T(8,128)(2,1)S(1)} %all_to_all.57.refs_4_), channel_id=1, source_target_pairs={{0,3},{1,2},{2,1},{3,0},{4,7},{5,6},{6,5},{7,4},{8,11},{9,10},{10,... | collective-permute-start | bytes 1179656 | tf_op jit(solution)/shard_map/ppermute | solution.py:338
  217.8 16.0 %collective-permute-start.26 = (bf16[16,48,256]{2,1,0:T(8,128)(2,1)S(1)}, bf16[16,48,256]{2,1,0:T(8,128)(2,1)S(1)}, u32[]{:S(2)}, u32[]{:S(2)}) collective-permute-start(bf16[16,48,256]{2,1,0:T(8,128)(2,1)S(1)} %all_to_all.57.refs_4_), channel_id=1, source_target_pairs={{0,1},{1,0},{2,3},{3,2},{4,5},{5,4},{6,7},{7,6},{8,9},{9,8},{10,11... | collective-permute-start | bytes 1179656 | tf_op jit(solution)/shard_map/ppermute | solution.py:338
  223.8 12.3 %collective-permute-start.25 = (bf16[16,48,256]{2,1,0:T(8,128)(2,1)S(1)}, bf16[16,48,256]{2,1,0:T(8,128)(2,1)S(1)}, u32[]{:S(2)}, u32[]{:S(2)}) collective-permute-start(bf16[16,48,256]{2,1,0:T(8,128)(2,1)S(1)} %collective-permute-done.24.refs_3_), channel_id=1, source_target_pairs={{0,4},{1,5},{2,6},{3,7},{4,0},{5,1},{6,2},{7,3},{8,12},{9,13},{10,... | collective-permute-start | bytes 1179656 | tf_op jit(solution)/shard_map/ppermute | solution.py:338
  226.3 15.2 %collective-permute-start.23 = (bf16[16,48,256]{2,1,0:T(8,128)(2,1)S(1)}, bf16[16,48,256]{2,1,0:T(8,128)(2,1)S(1)}, u32[]{:S(2)}, u32[]{:S(2)}) collective-permute-start(bf16[16,48,256]{2,1,0:T(8,128)(2,1)S(1)} %collective-permute-done.21.refs_2_), channel_id=1, source_target_pairs={{0,3},{1,2},{2,1},{3,0},{4,7},{5,6},{6,5},{7,4},{8,11},{9,10},{10,... | collective-permute-start | bytes 1179656 | tf_op jit(solution)/shard_map/ppermute | solution.py:338
  227.9 13.5 %collective-permute-start.22 = (bf16[16,48,256]{2,1,0:T(8,128)(2,1)S(1)}, bf16[16,48,256]{2,1,0:T(8,128)(2,1)S(1)}, u32[]{:S(2)}, u32[]{:S(2)}) collective-permute-start(bf16[16,48,256]{2,1,0:T(8,128)(2,1)S(1)} %collective-permute-done.21.refs_2_), channel_id=1, source_target_pairs={{0,1},{1,0},{2,3},{3,2},{4,5},{5,4},{6,7},{7,6},{8,9},{9,8},{10,11... | collective-permute-start | bytes 1179656 | tf_op jit(solution)/shard_map/ppermute | solution.py:338
  266.5 17.1 %all-to-all-start.9 = ((bf16[16,3,32,256]{3,2,1,0:T(8,128)(2,1)}), bf16[16,3,32,256]{3,2,1,0:T(8,128)(2,1)S(1)}, u32[]{:S(2)}, u32[]{:S(2)}) async-start(bf16[16,3,32,256]{3,2,1,0:T(8,128)(2,1)} %trace_blocks.1), calls=%async_computation.9 | async-start | bytes 1572864 | tf_op jit(solution)/shard_map/all_to_all | solution.py:334
  272.9 10.9 %copy-start.5 = (f32[32,48,256]{2,1,0:T(8,128)S(1)}, f32[32,48,256]{2,1,0:T(8,128)}, u32[]{:S(2)}) copy-start(f32[32,48,256]{2,1,0:T(8,128)} %param.8) | copy-start | bytes 4718596

commit v4 on v3

--- a/solution.py
+++ b/solution.py
@@ -73,25 +73,25 @@
     out_ref[...] = flat.reshape(out_ref.shape)
 
 
-EARLY = (5, 7, 6)
-LATE = (1, 3, 4, 2, 0)
-
-
-def fetch(order, refl_ref, held_ref, sems):
-    share = held_ref.shape[2] // len(order)
-    copies = []
-    for i, k in enumerate(order):
+EARLY = (6, 5, 7)
+LATE = (2, 3, 1, 4, 0)
+NEIGHBOURS, REST = (3, 1), (2, 4, 0)
+
+
+def fetch(held, order, refl_ref, held_ref, sems):
+    share = held_ref.shape[2] // len(held)
+    copies = {}
+    for k in order + tuple(k for k in held if k not in order):
+        i = held.index(k)
         start = pl.multiple_of((lax.axis_index("panel") ^ k) * share, share)
-        copies.append(
-            pltpu.make_async_copy(
-                refl_ref.at[:, :, pl.ds(start, share)], held_ref.at[:, :, pl.ds(i * share, share)], sems.at[i]
-            )
+        copies[k] = pltpu.make_async_copy(
+            refl_ref.at[:, :, pl.ds(start, share)], held_ref.at[:, :, pl.ds(i * share, share)], sems.at[i]
         )
-        copies[-1].start()
+        copies[k].start()
     return copies
 
 
-def image_kernel(order, spread, first, bands_ref, *refs):
+def image_kernel(order, held, spread, first, keep, bands_ref, *refs):
     if spread:
         refl_ref, *refs = refs
     else:
@@ -100,10 +100,10 @@
     out_refs, refs = refs[: len(order)], refs[len(order) :]
     if spread:
         direct, crossed, *refs = refs
-    held_ref, copies = refl_ref, []
+    held_ref, copies = refl_ref, {}
     if first:
-        held_ref, *refs = refs
-        copies = fetch(order, refl_ref, held_ref, refs[-1])
+        *refs, held_ref, sems = refs if keep is False else (*refs[1:-1], refs[0], refs[-1])
+        copies = fetch(held, order, refl_ref, held_ref, sems)
 
     _, freqs, height, _ = held_ref.shape
     step = 2 * freqs
@@ -117,15 +117,18 @@
             direct[j] = jnp.concatenate([real, imag], axis=0).astype(jnp.bfloat16)
             crossed[j] = jnp.concatenate([-imag, real], axis=0).astype(jnp.bfloat16)
 
-    for i, out_ref in enumerate(out_refs):
+    for k, out_ref in zip(order, out_refs, strict=True):
         if first:
-            copies[i].wait()
+            copies.pop(k).wait()
+        i = held.index(k)
         at = slice(i * share, (i + 1) * share)
         images = [
             dot_nt(direct[j], held_ref[0, j, at]) + dot_nt(crossed[j], held_ref[1, j, at]) for j in range(freqs)
         ]
         images = jnp.stack(images).reshape(step, count, share)
         out_ref[...] = jnp.swapaxes(images, 0, 1).astype(jnp.bfloat16).reshape(groups, block, share)
+    for copy in copies.values():
+        copy.wait()
 
 
 IN_VMEM = pl.BlockSpec(memory_space=pltpu.VMEM)
@@ -145,10 +148,10 @@
     )(*args)
 
 
-def image_blocks(order, sources, reflection, panels, first):
+def image_blocks(order, held, sources, reflection, panels, first, keep=True):
     spread = len(sources) == 1
     _, freqs, receivers, width = reflection.shape
-    share = receivers // (panels if first else len(order))
+    share = receivers // (panels if first else len(held))
     if spread:
         groups, height, _ = sources[0].shape
         count = groups * height // (2 * freqs)
@@ -164,12 +167,12 @@
         scratch.append(pltpu.VMEM((width // 128, groups * height, 128), jnp.float32))
     specs = None
     if first:
-        out_shape.append(pltpu.VMEM((2, freqs, share * len(order), width), reflection.dtype))
-        scratch.append(pltpu.SemaphoreType.DMA((len(order),)))
+        (out_shape if keep else scratch).append(pltpu.VMEM((2, freqs, share * len(held), width), reflection.dtype))
+        scratch.append(pltpu.SemaphoreType.DMA((len(held),)))
         specs = [IN_VMEM] * len(sources) + [pl.BlockSpec(memory_space=pltpu.HBM)]
         reflection = pltpu.with_memory_space_constraint(reflection, pltpu.HBM)
     outs = call(
-        lambda *refs: image_kernel(order, spread, first, *refs),
+        lambda *refs: image_kernel(order, held, spread, first, keep, *refs),
         "image_blocks",
         out_shape,
         (*sources, reflection),
@@ -178,7 +181,24 @@
         flops=4 * 2 * freqs * share * len(order) * width * count,
     )
     blocks, outs = outs[: len(order)], outs[len(order) :]
-    return blocks, outs[:2] if spread else sources, outs[-1] if first else reflection
+    return blocks, outs[:2] if spread else sources, outs[-1] if first and keep else reflection
+
+
+def fetch_kernel(refl_ref, _, held_ref, sems):
+    for copy in fetch(EARLY, EARLY, refl_ref, held_ref, sems).values():
+        copy.wait()
+
+
+def fetch_early(reflection, panels, after):
+    parts, freqs, receivers, width = reflection.shape
+    return call(
+        fetch_kernel,
+        "fetch_early",
+        pltpu.VMEM((parts, freqs, receivers // panels * len(EARLY), width), reflection.dtype),
+        (pltpu.with_memory_space_constraint(reflection, pltpu.HBM), after),
+        [pltpu.SemaphoreType.DMA((len(EARLY),))],
+        [pl.BlockSpec(memory_space=pltpu.HBM), pl.BlockSpec(memory_space=pl.ANY)],
+    )
 
 
 def return_kernel(panels, final, *refs):
@@ -365,20 +385,25 @@
     for iteration in range(ITERS):
         is_first, last = iteration == 0, iteration == ITERS - 1
         bands = exchange(blocks, "freq")
-        (b5, b7, b6), by_freq, early = image_blocks(EARLY, (bands,), early, panels, is_first)
+        (b6, b5, b7), by_freq, early = image_blocks(EARLY, EARLY, (bands,), early, panels, is_first)
         r5, r7, r6 = send(b5, 1), send(b7, 3), send(b6, 4)
-        (b1, b3, b4, b2, b0), _, late = image_blocks(LATE, tuple(by_freq), late, panels, is_first)
+        near = NEIGHBOURS if is_first else LATE
+        (b3, b1), _, _ = image_blocks(NEIGHBOURS, near, tuple(by_freq), late, panels, is_first, keep=False)
         s1, s3 = send(b1, 1), send(b3, 3)
+        (b2, b4, b0), _, late = image_blocks(REST, LATE, tuple(by_freq), late, panels, is_first)
         s2, s4 = send(added(b2, r6), 2), send(added(b4, r5, r7), 4)
         images = exchange(added(b0, s1, s3, s2, s4), "freq")
         spectra, *traces = upgoing_blocks(images, onsets, tables, rows, last)
         m0 = exchange(spectra, "freq")
         m2, m4, m1, m3 = send(m0, 2), send(m0, 4), send(m0, 1), send(m0, 3)
         m6, m5, m7 = send(m2, 4), send(m4, 1), send(m4, 3)
-        partial = return_blocks((m1, m3, m4, m2, m0), late)
-        returns = exchange(return_blocks((m5, m7, m6), early, partial, traces), "freq")
+        partial = return_blocks((m2, m3, m1, m4, m0), late)
         if last:
-            upgoing = in_time(returns[:, count * rows :])
+            partial, upgoing = lax.optimization_barrier((partial, exchange(traces[0], "freq")))
+            early = fetch_early(reflection, panels, upgoing)
+        returns = exchange(return_blocks((m6, m5, m7), early, partial), "freq")
+        if last:
+            upgoing = in_time(upgoing)
             traces = trace_blocks(returns, onsets, inverse, rows, count)
             focusing = focus_init + in_time(exchange(traces, "freq"))
         else:

time: 286 us -> 284 us (level)
  waiting for transfers between devices: 79.1 us -> 66.3 us
  Pallas kernels: 30.2 us -> 36.8 us
  starting transfers between devices: 40.4 us -> 46.6 us
  blocking collectives: 128 us -> 122 us
  local copies, waits for them, and re-layouts: 2.41 us -> 6.32 us
    ppermute x28, waiting for transfers between devices: 68.3 us -> 55.5 us  [send(): lax.ppermute(block, 'panel', [(i, i ^ k) for i in range(lax.axis_size('pa...]
    pallas_call x13 -> x16, Pallas kernels: 30.2 us -> 36.8 us  [call(): pl.pallas_call(kernel, in_specs=specs or [IN_VMEM] * len(args), out_specs...]
    all_to_all x9, blocking collectives: 128 us -> 122 us  [exchange(): return lax.all_to_all(blocks, axis, split_axis=0, concat_axis=0, tiled=True)]
    all_to_all x1 -> x2, starting transfers between devices: 4.06 us -> 9.7 us  [exchange(): return lax.all_to_all(blocks, axis, split_axis=0, concat_axis=0, tiled=True)]
    unnamed x13 -> x17, local copies, waits for them, and re-layouts: 2.09 us -> 6.07 us
    all_to_all x1 -> x2, waiting for transfers between devices: 10.7 us -> 10.8 us  [exchange(): return lax.all_to_all(blocks, axis, split_axis=0, concat_axis=0, tiled=True)]
  transfers between devices with their start and end apart: 29 -> 30, of which waited for: 14 -> 16; matrix products, arithmetic and copies ran while one was open for 1% -> 1% of each run, Pallas kernels for 5% -> 6%
where the time goes in v4:
time: 284 us
  blocking collectives  122 us (43%)
  waiting for transfers between devices  66.3 us (23%)
  starting transfers between devices  46.6 us (16%)
  Pallas kernels  36.8 us (13%)
  local copies, waits for them, and re-layouts  6.32 us (2%)
  other arithmetic  4.94 us (2%)
    all_to_all x9, blocking collectives, exchange(): return lax.all_to_all(blocks, axis, split_axis=0, concat_axis=0, tiled=True)  122 us
    ppermute x28, waiting for transfers between devices, send(): lax.ppermute(block, 'panel', [(i, i ^ k) for i in range(lax.axis_size('pa...  55.5 us
    ppermute x28, starting transfers between devices, send(): lax.ppermute(block, 'panel', [(i, i ^ k) for i in range(lax.axis_size('pa...  36.9 us
    pallas_call x16, Pallas kernels, call(): pl.pallas_call(kernel, in_specs=specs or [IN_VMEM] * len(args), out_specs...  36.8 us
    all_to_all x2, waiting for transfers between devices, exchange(): return lax.all_to_all(blocks, axis, split_axis=0, concat_axis=0, tiled=True)  10.8 us
    all_to_all x2, starting transfers between devices, exchange(): return lax.all_to_all(blocks, axis, split_axis=0, concat_axis=0, tiled=True)  9.7 us
    unnamed x17, local copies, waits for them, and re-layouts  6.07 us
  transfers between devices with their start and end apart: 30, of which 16 were waited for; matrix products, arithmetic and copies ran while one was open for 1% of the time, Pallas kernels for 6%

profile of v4, /device:TPU:1, one launch (start us, length us, event | category | flops | bytes accessed | tf_op | source)
XLA Modules:
  0.0 283.5 jit_solution(8853752174808075881)
XLA Ops:
  0.6 1.5 convert_element_type.99
  2.4 19.5 %all_to_all.55.traces_ref = bf16[16,3,32,256]{3,2,1,0:T(8,128)(2,1)S(1)} all-to-all(bf16[16,3,32,256]{3,2,1,0:T(8,128)(2,1)S(1)} %bitcast.11), channel_id=1, replica_groups=mesh['freq'=16,'panel'=8] {'freq'}, dimensions={0} | all-to-all | bytes 1572864 | tf_op jit(solution)/shard_map/all_to_all | solution.py:354
  22.5 11.9 %all_to_all.56.refs_0_ = bf16[16,48,256]{2,1,0:T(8,128)(2,1)S(1)} all-to-all(bf16[16,48,256]{2,1,0:T(8,128)(2,1)S(1)} %get-tuple-element.31), channel_id=1, replica_groups=mesh['freq'=16,'panel'=8] {'freq'}, dimensions={0} | all-to-all | bytes 786432 | tf_op jit(solution)/shard_map/all_to_all | solution.py:354
  34.4 4.1 %image_blocks.6 = (bf16[16,48,256]{2,1,0:T(8,128)(2,1)S(1)}, bf16[16,48,256]{2,1,0:T(8,128)(2,1)S(1)}, bf16[16,48,256]{2,1,0:T(8,128)(2,1)S(1)}, bf16[8,96,256]{...) custom-call(bf16[16,48,256]{2,1,0:T(8,128)(2,1)S(1)} %all_to_all.56.refs_0_, ...), custom_call_target="tpu_custom_call" | custom-call | flops 603979776 | bytes 34340864 | tf_op jit(solution)/shard_map/image_blocks/pallas_call | solution.py:139
  38.4 1.7 collective-permute-start.4
  40.1 2.2 collective-permute-start.5
  42.4 2.4 collective-permute-start.2
  44.8 3.2 %image_blocks.8 = (bf16[16,48,256]{2,1,0:T(8,128)(2,1)S(1)}, bf16[16,48,256]{2,1,0:T(8,128)(2,1)S(1)}) custom-call(bf16[8,96,256]{2,1,0:T(8,128)(2,1)S(1)} %get-tuple-element.32.refs_0_, bf16[8,96,256]{2,1,0:T(8,128)(2,1)S(1)} %get-tuple-element.33.refs_1_, bf16[2,8,2048,256]{3,2,1,0:T(8,128)(2,1)} %refl_ref.1), custom_call_target="tpu_custom_call" | custom-call | flops 402653184 | bytes 35127296 | tf_op jit(solution)/shard_map/image_blocks/pallas_call | solution.py:139
  48.1 0.8 collective-permute-start
  49.5 4.1 %image_blocks.7 = (bf16[16,48,256]{2,1,0:T(8,128)(2,1)S(1)}, bf16[16,48,256]{2,1,0:T(8,128)(2,1)S(1)}, bf16[16,48,256]{2,1,0:T(8,128)(2,1)S(1)}, bf16[2,8,1280,256]{3,2,1,0:T(8,128)(2,1)S(1)}) custom-call(bf16[8,96,256]{2,1,0:T(8,128)(2,1)S(1)} %get-tuple-element.32.refs_0_, bf16[8,96,256]{2,1,0:T(8,128)(2,1)S(1)} %get-tuple-element.33.refs_1_, ...), custom_call_target="tpu_custom_call" | custom-call | flops 603979776 | bytes 35127296 | tf_op jit(solution)/shard_map/image_blocks/pallas_call | solution.py:139
  54.5 2.0 collective-permute-start.3
  56.7 2.2 collective-permute-done.1
  59.0 4.7 %collective-permute-done.6 = bf16[16,48,256]{2,1,0:T(8,128)(2,1)S(1)} collective-permute-done((bf16[16,48,256]{2,1,0:T(8,128)(2,1)S(1)}, bf16[16,48,256]{2,1,0:T(8,128)(2,1)S(1)}, u32[]{:S(2)}, u32[]{:S(2)}) %collective-permute-start.6) | collective-permute-done | bytes 393248 | tf_op jit(solution)/shard_map/ppermute | solution.py:358
  63.7 4.6 %collective-permute-done.3 = bf16[16,48,256]{2,1,0:T(8,128)(2,1)S(1)} collective-permute-done((bf16[16,48,256]{2,1,0:T(8,128)(2,1)S(1)}, bf16[16,48,256]{2,1,0:T(8,128)(2,1)S(1)}, u32[]{:S(2)}, u32[]{:S(2)}) %collective-permute-start.3) | collective-permute-done | bytes 393248 | tf_op jit(solution)/shard_map/ppermute | solution.py:358
  68.5 13.5 %all_to_all.57.refs_5_ = bf16[16,48,256]{2,1,0:T(8,128)(2,1)S(1)} all-to-all(bf16[16,48,256]{2,1,0:T(8,128)(2,1)S(1)} %add_convert_fusion.3), channel_id=1, replica_groups=mesh['freq'=16,'panel'=8] {'freq'}, dimensions={0} | all-to-all | bytes 786432 | tf_op jit(solution)/shard_map/all_to_all | solution.py:354
  82.0 1.5 upgoing_blocks.2
  83.6 12.1 %all_to_all.58.refs_4_ = bf16[16,48,256]{2,1,0:T(8,128)(2,1)S(1)} all-to-all(bf16[16,48,256]{2,1,0:T(8,128)(2,1)S(1)} %upgoing_blocks.2), channel_id=1, replica_groups=mesh['freq'=16,'panel'=8] {'freq'}, dimensions={0} | all-to-all | bytes 786432 | tf_op jit(solution)/shard_map/all_to_all | solution.py:354
  95.7 2.5 collective-permute-start.9
  98.1 1.5 collective-permute-start.7
  100.8 5.8 %collective-permute-done.9.refs_3_ = bf16[16,48,256]{2,1,0:T(8,128)(2,1)S(1)} collective-permute-done((bf16[16,48,256]{2,1,0:T(8,128)(2,1)S(1)}, bf16[16,48,256]{2,1,0:T(8,128)(2,1)S(1)}, u32[]{:S(2)}, u32[]{:S(2)}) %collective-permute-start.9) | collective-permute-done | bytes 393248 | tf_op jit(solution)/shard_map/ppermute | solution.py:358
  106.6 1.8 collective-permute-start.11
  108.8 2.0 collective-permute-start.8
  110.8 8.2 %collective-permute-done.12.refs_1_ = bf16[16,48,256]{2,1,0:T(8,128)(2,1)S(1)} collective-permute-done((bf16[16,48,256]{2,1,0:T(8,128)(2,1)S(1)}, bf16[16,48,256]{2,1,0:T(8,128)(2,1)S(1)}, u32[]{:S(2)}, u32[]{:S(2)}) %collective-permute-start.12) | collective-permute-done | bytes 393248 | tf_op jit(solution)/shard_map/ppermute | solution.py:358
  119.1 2.3 return_blocks.4.refs_4_
  121.4 3.6 %collective-permute-done.10.refs_1_ = bf16[16,48,256]{2,1,0:T(8,128)(2,1)S(1)} collective-permute-done((bf16[16,48,256]{2,1,0:T(8,128)(2,1)S(1)}, bf16[16,48,256]{2,1,0:T(8,128)(2,1)S(1)}, u32[]{:S(2)}, u32[]{:S(2)}) %collective-permute-start.10) | collective-permute-done | bytes 393248 | tf_op jit(solution)/shard_map/ppermute | solution.py:358
  125.0 2.5 collective-permute-done.11.refs_2_
  127.5 1.7 return_blocks.5
  129.3 11.5 %all_to_all.59.refs_6_ = bf16[16,48,256]{2,1,0:T(8,128)(2,1)S(1)} all-to-all(bf16[16,48,256]{2,1,0:T(8,128)(2,1)S(1)} %return_blocks.5), channel_id=1, replica_groups=mesh['freq'=16,'panel'=8] {'freq'}, dimensions={0} | all-to-all | bytes 786432 | tf_op jit(solution)/shard_map/all_to_all | solution.py:354
  140.8 1.5 focus_blocks.1
  142.3 12.1 %all_to_all.60.refs_0_ = bf16[16,48,256]{2,1,0:T(8,128)(2,1)S(1)} all-to-all(bf16[16,48,256]{2,1,0:T(8,128)(2,1)S(1)} %focus_blocks.1), channel_id=1, replica_groups=mesh['freq'=16,'panel'=8] {'freq'}, dimensions={0} | all-to-all | bytes 786432 | tf_op jit(solution)/shard_map/all_to_all | solution.py:354
  154.4 2.2 image_blocks.9
  156.6 1.6 collective-permute-start.16
  158.2 1.7 collective-permute-start.19
  159.9 1.5 image_blocks.11
  161.4 0.8 collective-permute-start.14
  162.2 1.0 collective-permute-start.15
  163.3 2.1 image_blocks.10
  165.4 2.2 collective-permute-done.16
  167.7 1.5 collective-permute-start.17
  169.4 1.6 collective-permute-start.20
  171.0 4.8 %collective-permute-done.14 = bf16[16,48,256]{2,1,0:T(8,128)(2,1)S(1)} collective-permute-done((bf16[16,48,256]{2,1,0:T(8,128)(2,1)S(1)}, bf16[16,48,256]{2,1,0:T(8,128)(2,1)S(1)}, u32[]{:S(2)}, u32[]{:S(2)}) %collective-permute-start.14) | collective-permute-done | bytes 393248 | tf_op jit(solution)/shard_map/ppermute | solution.py:358
  175.8 1.0 collective-permute-done.15
  176.7 8.8 %collective-permute-done.17 = bf16[16,48,256]{2,1,0:T(8,128)(2,1)S(1)} collective-permute-done((bf16[16,48,256]{2,1,0:T(8,128)(2,1)S(1)}, bf16[16,48,256]{2,1,0:T(8,128)(2,1)S(1)}, u32[]{:S(2)}, u32[]{:S(2)}) %collective-permute-start.17) | collective-permute-done | bytes 393248 | tf_op jit(solution)/shard_map/ppermute | solution.py:358
  185.8 13.4 %all_to_all.61.refs_5_ = bf16[16,48,256]{2,1,0:T(8,128)(2,1)S(1)} all-to-all(bf16[16,48,256]{2,1,0:T(8,128)(2,1)S(1)} %add_convert_fusion), channel_id=1, replica_groups=mesh['freq'=16,'panel'=8] {'freq'}, dimensions={0} | all-to-all | bytes 786432 | tf_op jit(solution)/shard_map/all_to_all | solution.py:354
  199.2 2.2 upgoing_blocks.3
  201.4 12.1 %all_to_all.62.refs_4_ = bf16[16,48,256]{2,1,0:T(8,128)(2,1)S(1)} all-to-all(bf16[16,48,256]{2,1,0:T(8,128)(2,1)S(1)} %get-tuple-element.54), channel_id=1, replica_groups=mesh['freq'=16,'panel'=8] {'freq'}, dimensions={0} | all-to-all | bytes 786432 | tf_op jit(solution)/shard_map/all_to_all | solution.py:354
  213.4 1.5 collective-permute-start.21
  214.9 2.4 collective-permute-start.23
  217.4 5.1 %all-to-all-start.8 = ((bf16[16,3,32,256]{3,2,1,0:T(8,128)(2,1)}), bf16[16,3,32,256]{3,2,1,0:T(8,128)(2,1)S(1)}, u32[]{:S(2)}, u32[]{:S(2)}) async-start(bf16[16,3,32,256]{3,2,1,0:T(8,128)(2,1)} %get-tuple-element.55), calls=%async_computation.8 | async-start | bytes 1572864 | tf_op jit(solution)/shard_map/all_to_all | solution.py:354
  222.5 1.0 collective-permute-start.26
  223.7 0.7 collective-permute-done.21.refs_0_
  224.4 2.4 collective-permute-start.22
  226.9 1.6 collective-permute-start.25
  228.6 5.5 %collective-permute-done.26.refs_1_ = bf16[16,48,256]{2,1,0:T(8,128)(2,1)S(1)} collective-permute-done((bf16[16,48,256]{2,1,0:T(8,128)(2,1)S(1)}, bf16[16,48,256]{2,1,0:T(8,128)(2,1)S(1)}, u32[]{:S(2)}, u32[]{:S(2)}) %collective-permute-start.26) | collective-permute-done | bytes 393248 | tf_op jit(solution)/shard_map/ppermute | solution.py:358
  234.1 4.0 %copy-done.1 = bf16[2,8,1280,256]{3,2,1,0:T(8,128)(2,1)S(1)} copy-done((bf16[2,8,1280,256]{3,2,1,0:T(8,128)(2,1)S(1)}, bf16[2,8,1280,256]{3,2,1,0:T(8,128)(2,1)}, u32[]{:S(2)}) %copy-start.1) | copy-done | bytes 10485784
  238.1 2.3 return_blocks.6.refs_4_
  240.4 2.9 %fetch_early.1.refs_3_ = bf16[2,8,768,256]{3,2,1,0:T(8,128)(2,1)S(1)} custom-call(bf16[2,8,2048,256]{3,2,1,0:T(8,128)(2,1)} %refl_ref.1, bf16[16,3,32,256]{3,2,1,0:T(8,128)(2,1)S(1)} %all-to-all-done.8._), custom_call_target="tpu_custom_call" | custom-call | bytes 35127296 | tf_op jit(solution)/shard_map/fetch_early/pallas_call | solution.py:139
  243.3 3.0 %return_blocks.7 = bf16[16,48,256]{2,1,0:T(8,128)(2,1)S(1)} custom-call(bf16[16,48,256]{2,1,0:T(8,128)(2,1)} %collective-permute-done.22.refs_0_, bf16[16,48,256]{2,1,0:T(8,128)(2,1)} %collective-permute-done.24.refs_1_, bf16[16,48,256]{2,1,0:T(8,128)(2,1)} %collective-permute-done.25.refs_2_, bf16[2,8,768,256]{3,2,1,0:T(8,128)(2,1)S(1)} %fetch_early.1.refs_3_, ...), custom_call_target="tpu_custom_call" | custom-call | flops 603979776 | bytes 16515072 | tf_op jit(solution)/shard_map/return_blocks/pallas_call | solution.py:139
  246.3 15.6 %all_to_all.63.refs_3_ = bf16[16,48,256]{2,1,0:T(8,128)(2,1)S(1)} all-to-all(bf16[16,48,256]{2,1,0:T(8,128)(2,1)S(1)} %return_blocks.7), channel_id=1, replica_groups=mesh['freq'=16,'panel'=8] {'freq'}, dimensions={0} | all-to-all | bytes 786432 | tf_op jit(solution)/shard_map/all_to_all | solution.py:354
  262.0 1.6 trace_blocks.1
  263.6 4.6 %all-to-all-start.10 = ((bf16[16,3,32,256]{3,2,1,0:T(8,128)(2,1)}), bf16[16,3,32,256]{3,2,1,0:T(8,128)(2,1)S(1)}, u32[]{:S(2)}, u32[]{:S(2)}) async-start(bf16[16,3,32,256]{3,2,1,0:T(8,128)(2,1)} %trace_blocks.1), calls=%async_computation.10 | async-start | bytes 1572864 | tf_op jit(solution)/shard_map/all_to_all | solution.py:354
  268.3 2.1 copy.11
  270.4 10.8 %all-to-all-done.10 = bf16[16,3,32,256]{3,2,1,0:T(8,128)(2,1)S(1)} async-done(((bf16[16,3,32,256]{3,2,1,0:T(8,128)(2,1)}), bf16[16,3,32,256]{3,2,1,0:T(8,128)(2,1)S(1)}, u32[]{:S(2)}, u32[]{:S(2)}) %all-to-all-start.10) | async-done | bytes 786464 | tf_op jit(solution)/shard_map/all_to_all | solution.py:354
  281.4 2.1 copy_add_fusion
  (49 shorter events, 5.6 us)
Async XLA Ops:
  2.1 19.8 %copy-start.2 = (bf16[256,512]{1,0:T(8,128)(2,1)S(1)}, bf16[256,512]{1,0:T(8,128)(2,1)}, u32[]{:S(2)}) copy-start(bf16[256,512]{1,0:T(8,128)(2,1)} %constant.8.clone.high.refs_2_) | copy-start | bytes 786436
  2.1 19.8 %copy-start.3 = (bf16[256,512]{1,0:T(8,128)(2,1)S(1)}, bf16[256,512]{1,0:T(8,128)(2,1)}, u32[]{:S(2)}) copy-start(bf16[256,512]{1,0:T(8,128)(2,1)} %constant.9.clone.low.refs_3_) | copy-start | bytes 786436
  38.4 15.2 %collective-permute-start.4 = (bf16[16,48,256]{2,1,0:T(8,128)(2,1)S(1)}, bf16[16,48,256]{2,1,0:T(8,128)(2,1)S(1)}, u32[]{:S(2)}, u32[]{:S(2)}) collective-permute-start(bf16[16,48,256]{2,1,0:T(8,128)(2,1)S(1)} %get-tuple-element.40), channel_id=1, source_target_pairs={{0,1},{1,0},{2,3},{3,2},{4,5},{5,4},{6,7},{7,6},{8,9},{9,8},{10,11... | collective-permute-start | bytes 1179656 | tf_op jit(solution)/shard_map/ppermute | solution.py:358
  40.1 13.5 %collective-permute-start.5 = (bf16[16,48,256]{2,1,0:T(8,128)(2,1)S(1)}, bf16[16,48,256]{2,1,0:T(8,128)(2,1)S(1)}, u32[]{:S(2)}, u32[]{:S(2)}) collective-permute-start(bf16[16,48,256]{2,1,0:T(8,128)(2,1)S(1)} %get-tuple-element.41), channel_id=1, source_target_pairs={{0,3},{1,2},{2,1},{3,0},{4,7},{5,6},{6,5},{7,4},{8,11},{9,10},{10,... | collective-permute-start | bytes 1179656 | tf_op jit(solution)/shard_map/ppermute | solution.py:358
  42.4 12.0 %collective-permute-start.2 = (bf16[16,48,256]{2,1,0:T(8,128)(2,1)S(1)}, bf16[16,48,256]{2,1,0:T(8,128)(2,1)S(1)}, u32[]{:S(2)}, u32[]{:S(2)}) collective-permute-start(bf16[16,48,256]{2,1,0:T(8,128)(2,1)S(1)} %get-tuple-element.38), channel_id=1, source_target_pairs={{0,4},{1,5},{2,6},{3,7},{4,0},{5,1},{6,2},{7,3},{8,12},{9,13},{10,... | collective-permute-start | bytes 1179656 | tf_op jit(solution)/shard_map/ppermute | solution.py:358
  48.1 8.7 %collective-permute-start = (bf16[16,48,256]{2,1,0:T(8,128)(2,1)S(1)}, bf16[16,48,256]{2,1,0:T(8,128)(2,1)S(1)}, u32[]{:S(2)}, u32[]{:S(2)}) collective-permute-start(bf16[16,48,256]{2,1,0:T(8,128)(2,1)S(1)} %get-tuple-element.35), channel_id=1, source_target_pairs={{0,1},{1,0},{2,3},{3,2},{4,5},{5,4},{6,7},{7,6},{8,9},{9,8},{10,11... | collective-permute-start | bytes 1179656 | tf_op jit(solution)/shard_map/ppermute | solution.py:358
  48.9 10.1 %collective-permute-start.1 = (bf16[16,48,256]{2,1,0:T(8,128)(2,1)S(1)}, bf16[16,48,256]{2,1,0:T(8,128)(2,1)S(1)}, u32[]{:S(2)}, u32[]{:S(2)}) collective-permute-start(bf16[16,48,256]{2,1,0:T(8,128)(2,1)S(1)} %get-tuple-element.36), channel_id=1, source_target_pairs={{0,3},{1,2},{2,1},{3,0},{4,7},{5,6},{6,5},{7,4},{8,11},{9,10},{10,... | collective-permute-start | bytes 1179656 | tf_op jit(solution)/shard_map/ppermute | solution.py:358
  53.6 109.6 %copy-start = (bf16[2,8,1280,256]{3,2,1,0:T(8,128)(2,1)}, bf16[2,8,1280,256]{3,2,1,0:T(8,128)(2,1)S(1)}, u32[]{:S(2)}) copy-start(bf16[2,8,1280,256]{3,2,1,0:T(8,128)(2,1)S(1)} %get-tuple-element.43.refs_5_.refs_2_) | copy-start | bytes 31457284
  53.8 9.9 %collective-permute-start.6 = (bf16[16,48,256]{2,1,0:T(8,128)(2,1)S(1)}, bf16[16,48,256]{2,1,0:T(8,128)(2,1)S(1)}, u32[]{:S(2)}, u32[]{:S(2)}) collective-permute-start(bf16[16,48,256]{2,1,0:T(8,128)(2,1)S(1)} %add_convert_fusion.4), channel_id=1, source_target_pairs={{0,4},{1,5},{2,6},{3,7},{4,0},{5,1},{6,2},{7,3},{8,12},{9,13},{10,... | collective-permute-start | bytes 1179656 | tf_op jit(solution)/shard_map/ppermute | solution.py:358
  54.5 13.8 %collective-permute-start.3 = (bf16[16,48,256]{2,1,0:T(8,128)(2,1)S(1)}, bf16[16,48,256]{2,1,0:T(8,128)(2,1)S(1)}, u32[]{:S(2)}, u32[]{:S(2)}) collective-permute-start(bf16[16,48,256]{2,1,0:T(8,128)(2,1)S(1)} %add_convert_fusion.5), channel_id=1, source_target_pairs={{0,2},{1,3},{2,0},{3,1},{4,6},{5,7},{6,4},{7,5},{8,10},{9,11},{10,... | collective-permute-start | bytes 1179656 | tf_op jit(solution)/shard_map/ppermute | solution.py:358
  68.3 13.8 %copy-start.4 = (bf16[512,256]{1,0:T(8,128)(2,1)S(1)}, bf16[512,256]{1,0:T(8,128)(2,1)}, u32[]{:S(2)}) copy-start(bf16[512,256]{1,0:T(8,128)(2,1)} %constant.10.clone.refs_0_) | copy-start | bytes 786436
  68.3 13.8 %copy-start.5 = (bf16[512,256]{1,0:T(8,128)(2,1)S(1)}, bf16[512,256]{1,0:T(8,128)(2,1)}, u32[]{:S(2)}) copy-start(bf16[512,256]{1,0:T(8,128)(2,1)} %constant.11.clone.refs_1_) | copy-start | bytes 786436
  68.3 13.8 %copy-start.6 = (s32[48,256]{1,0:T(8,128)S(1)}, s32[48,256]{1,0:T(8,128)}, u32[]{:S(2)}) copy-start(s32[48,256]{1,0:T(8,128)} %refs_2_.8) | copy-start | bytes 147460
  95.7 10.9 %collective-permute-start.9 = (bf16[16,48,256]{2,1,0:T(8,128)(2,1)S(1)}, bf16[16,48,256]{2,1,0:T(8,128)(2,1)S(1)}, u32[]{:S(2)}, u32[]{:S(2)}) collective-permute-start(bf16[16,48,256]{2,1,0:T(8,128)(2,1)S(1)} %all_to_all.58.refs_4_), channel_id=1, source_target_pairs={{0,4},{1,5},{2,6},{3,7},{4,0},{5,1},{6,2},{7,3},{8,12},{9,13},{10,... | collective-permute-start | bytes 1179656 | tf_op jit(solution)/shard_map/ppermute | solution.py:358
  98.1 10.7 %collective-permute-start.7 = (bf16[16,48,256]{2,1,0:T(8,128)(2,1)S(1)}, bf16[16,48,256]{2,1,0:T(8,128)(2,1)S(1)}, u32[]{:S(2)}, u32[]{:S(2)}) collective-permute-start(bf16[16,48,256]{2,1,0:T(8,128)(2,1)S(1)} %all_to_all.58.refs_4_), channel_id=1, source_target_pairs={{0,2},{1,3},{2,0},{3,1},{4,6},{5,7},{6,4},{7,5},{8,10},{9,11},{10,... | collective-permute-start | bytes 1179656 | tf_op jit(solution)/shard_map/ppermute | solution.py:358
  99.6 19.5 %collective-permute-start.12 = (bf16[16,48,256]{2,1,0:T(8,128)(2,1)S(1)}, bf16[16,48,256]{2,1,0:T(8,128)(2,1)S(1)}, u32[]{:S(2)}, u32[]{:S(2)}) collective-permute-start(bf16[16,48,256]{2,1,0:T(8,128)(2,1)S(1)} %all_to_all.58.refs_4_), channel_id=1, source_target_pairs={{0,3},{1,2},{2,1},{3,0},{4,7},{5,6},{6,5},{7,4},{8,11},{9,10},{10,... | collective-permute-start | bytes 1179656 | tf_op jit(solution)/shard_map/ppermute | solution.py:358
  100.2 18.9 %collective-permute-start.13 = (bf16[16,48,256]{2,1,0:T(8,128)(2,1)S(1)}, bf16[16,48,256]{2,1,0:T(8,128)(2,1)S(1)}, u32[]{:S(2)}, u32[]{:S(2)}) collective-permute-start(bf16[16,48,256]{2,1,0:T(8,128)(2,1)S(1)} %all_to_all.58.refs_4_), channel_id=1, source_target_pairs={{0,1},{1,0},{2,3},{3,2},{4,5},{5,4},{6,7},{7,6},{8,9},{9,8},{10,11... | collective-permute-start | bytes 1179656 | tf_op jit(solution)/shard_map/ppermute | solution.py:358
  106.6 18.4 %collective-permute-start.10 = (bf16[16,48,256]{2,1,0:T(8,128)(2,1)S(1)}, bf16[16,48,256]{2,1,0:T(8,128)(2,1)S(1)}, u32[]{:S(2)}, u32[]{:S(2)}) collective-permute-start(bf16[16,48,256]{2,1,0:T(8,128)(2,1)S(1)} %collective-permute-done.9.refs_3_), channel_id=1, source_target_pairs={{0,1},{1,0},{2,3},{3,2},{4,5},{5,4},{6,7},{7,6},{8,9},{9,8},{10,11... | collective-permute-start | bytes 1179656 | tf_op jit(solution)/shard_map/ppermute | solution.py:358
  106.6 20.9 %collective-permute-start.11 = (bf16[16,48,256]{2,1,0:T(8,128)(2,1)S(1)}, bf16[16,48,256]{2,1,0:T(8,128)(2,1)S(1)}, u32[]{:S(2)}, u32[]{:S(2)}) collective-permute-start(bf16[16,48,256]{2,1,0:T(8,128)(2,1)S(1)} %collective-permute-done.9.refs_3_), channel_id=1, source_target_pairs={{0,3},{1,2},{2,1},{3,0},{4,7},{5,6},{6,5},{7,4},{8,11},{9,10},{10,... | collective-permute-start | bytes 1179656 | tf_op jit(solution)/shard_map/ppermute | solution.py:358
  108.8 18.7 %collective-permute-start.8 = (bf16[16,48,256]{2,1,0:T(8,128)(2,1)S(1)}, bf16[16,48,256]{2,1,0:T(8,128)(2,1)S(1)}, u32[]{:S(2)}, u32[]{:S(2)}) collective-permute-start(bf16[16,48,256]{2,1,0:T(8,128)(2,1)S(1)} %collective-permute-done.7.refs_0_), channel_id=1, source_target_pairs={{0,4},{1,5},{2,6},{3,7},{4,0},{5,1},{6,2},{7,3},{8,12},{9,13},{10,... | collective-permute-start | bytes 1179656 | tf_op jit(solution)/shard_map/ppermute | solution.py:358
  156.6 11.0 %collective-permute-start.16 = (bf16[16,48,256]{2,1,0:T(8,128)(2,1)S(1)}, bf16[16,48,256]{2,1,0:T(8,128)(2,1)S(1)}, u32[]{:S(2)}, u32[]{:S(2)}) collective-permute-start(bf16[16,48,256]{2,1,0:T(8,128)(2,1)S(1)} %get-tuple-element.50), channel_id=1, source_target_pairs={{0,4},{1,5},{2,6},{3,7},{4,0},{5,1},{6,2},{7,3},{8,12},{9,13},{10,... | collective-permute-start | bytes 1179656 | tf_op jit(solution)/shard_map/ppermute | solution.py:358
  158.2 11.1 %collective-permute-start.18 = (bf16[16,48,256]{2,1,0:T(8,128)(2,1)S(1)}, bf16[16,48,256]{2,1,0:T(8,128)(2,1)S(1)}, u32[]{:S(2)}, u32[]{:S(2)}) collective-permute-start(bf16[16,48,256]{2,1,0:T(8,128)(2,1)S(1)} %get-tuple-element.52), channel_id=1, source_target_pairs={{0,1},{1,0},{2,3},{3,2},{4,5},{5,4},{6,7},{7,6},{8,9},{9,8},{10,11... | collective-permute-start | bytes 1179656 | tf_op jit(solution)/shard_map/ppermute | solution.py:358
  158.2 11.1 %collective-permute-start.19 = (bf16[16,48,256]{2,1,0:T(8,128)(2,1)S(1)}, bf16[16,48,256]{2,1,0:T(8,128)(2,1)S(1)}, u32[]{:S(2)}, u32[]{:S(2)}) collective-permute-start(bf16[16,48,256]{2,1,0:T(8,128)(2,1)S(1)} %get-tuple-element.53), channel_id=1, source_target_pairs={{0,3},{1,2},{2,1},{3,0},{4,7},{5,6},{6,5},{7,4},{8,11},{9,10},{10,... | collective-permute-start | bytes 1179656 | tf_op jit(solution)/shard_map/ppermute | solution.py:358
  161.4 14.4 %collective-permute-start.14 = (bf16[16,48,256]{2,1,0:T(8,128)(2,1)S(1)}, bf16[16,48,256]{2,1,0:T(8,128)(2,1)S(1)}, u32[]{:S(2)}, u32[]{:S(2)}) collective-permute-start(bf16[16,48,256]{2,1,0:T(8,128)(2,1)S(1)} %get-tuple-element.47), channel_id=1, source_target_pairs={{0,1},{1,0},{2,3},{3,2},{4,5},{5,4},{6,7},{7,6},{8,9},{9,8},{10,11... | collective-permute-start | bytes 1179656 | tf_op jit(solution)/shard_map/ppermute | solution.py:358
  162.2 14.5 %collective-permute-start.15 = (bf16[16,48,256]{2,1,0:T(8,128)(2,1)S(1)}, bf16[16,48,256]{2,1,0:T(8,128)(2,1)S(1)}, u32[]{:S(2)}, u32[]{:S(2)}) collective-permute-start(bf16[16,48,256]{2,1,0:T(8,128)(2,1)S(1)} %get-tuple-element.48), channel_id=1, source_target_pairs={{0,3},{1,2},{2,1},{3,0},{4,7},{5,6},{6,5},{7,4},{8,11},{9,10},{10,... | collective-permute-start | bytes 1179656 | tf_op jit(solution)/shard_map/ppermute | solution.py:358
  167.7 17.8 %collective-permute-start.17 = (bf16[16,48,256]{2,1,0:T(8,128)(2,1)S(1)}, bf16[16,48,256]{2,1,0:T(8,128)(2,1)S(1)}, u32[]{:S(2)}, u32[]{:S(2)}) collective-permute-start(bf16[16,48,256]{2,1,0:T(8,128)(2,1)S(1)} %add_convert_fusion.2), channel_id=1, source_target_pairs={{0,2},{1,3},{2,0},{3,1},{4,6},{5,7},{6,4},{7,5},{8,10},{9,11},{10,... | collective-permute-start | bytes 1179656 | tf_op jit(solution)/shard_map/ppermute | solution.py:358
  169.4 16.1 %collective-permute-start.20 = (bf16[16,48,256]{2,1,0:T(8,128)(2,1)S(1)}, bf16[16,48,256]{2,1,0:T(8,128)(2,1)S(1)}, u32[]{:S(2)}, u32[]{:S(2)}) collective-permute-start(bf16[16,48,256]{2,1,0:T(8,128)(2,1)S(1)} %add_convert_fusion.1), channel_id=1, source_target_pairs={{0,4},{1,5},{2,6},{3,7},{4,0},{5,1},{6,2},{7,3},{8,12},{9,13},{10,... | collective-permute-start | bytes 1179656 | tf_op jit(solution)/shard_map/ppermute | solution.py:358
  213.4 10.9 %collective-permute-start.21 = (bf16[16,48,256]{2,1,0:T(8,128)(2,1)S(1)}, bf16[16,48,256]{2,1,0:T(8,128)(2,1)S(1)}, u32[]{:S(2)}, u32[]{:S(2)}) collective-permute-start(bf16[16,48,256]{2,1,0:T(8,128)(2,1)S(1)} %all_to_all.62.refs_4_), channel_id=1, source_target_pairs={{0,2},{1,3},{2,0},{3,1},{4,6},{5,7},{6,4},{7,5},{8,10},{9,11},{10,... | collective-permute-start | bytes 1179656 | tf_op jit(solution)/shard_map/ppermute | solution.py:358
  214.9 11.9 %collective-permute-start.23 = (bf16[16,48,256]{2,1,0:T(8,128)(2,1)S(1)}, bf16[16,48,256]{2,1,0:T(8,128)(2,1)S(1)}, u32[]{:S(2)}, u32[]{:S(2)}) collective-permute-start(bf16[16,48,256]{2,1,0:T(8,128)(2,1)S(1)} %all_to_all.62.refs_4_), channel_id=1, source_target_pairs={{0,4},{1,5},{2,6},{3,7},{4,0},{5,1},{6,2},{7,3},{8,12},{9,13},{10,... | collective-permute-start | bytes 1179656 | tf_op jit(solution)/shard_map/ppermute | solution.py:358
  217.4 23.0 %all-to-all-start.8 = ((bf16[16,3,32,256]{3,2,1,0:T(8,128)(2,1)}), bf16[16,3,32,256]{3,2,1,0:T(8,128)(2,1)S(1)}, u32[]{:S(2)}, u32[]{:S(2)}) async-start(bf16[16,3,32,256]{3,2,1,0:T(8,128)(2,1)} %get-tuple-element.55), calls=%async_computation.8 | async-start | bytes 1572864 | tf_op jit(solution)/shard_map/all_to_all | solution.py:354
  222.5 11.6 %collective-permute-start.26 = (bf16[16,48,256]{2,1,0:T(8,128)(2,1)S(1)}, bf16[16,48,256]{2,1,0:T(8,128)(2,1)S(1)}, u32[]{:S(2)}, u32[]{:S(2)}) collective-permute-start(bf16[16,48,256]{2,1,0:T(8,128)(2,1)S(1)} %all_to_all.62.refs_4_), channel_id=1, source_target_pairs={{0,3},{1,2},{2,1},{3,0},{4,7},{5,6},{6,5},{7,4},{8,11},{9,10},{10,... | collective-permute-start | bytes 1179656 | tf_op jit(solution)/shard_map/ppermute | solution.py:358
  223.5 10.6 %collective-permute-start.27 = (bf16[16,48,256]{2,1,0:T(8,128)(2,1)S(1)}, bf16[16,48,256]{2,1,0:T(8,128)(2,1)S(1)}, u32[]{:S(2)}, u32[]{:S(2)}) collective-permute-start(bf16[16,48,256]{2,1,0:T(8,128)(2,1)S(1)} %all_to_all.62.refs_4_), channel_id=1, source_target_pairs={{0,1},{1,0},{2,3},{3,2},{4,5},{5,4},{6,7},{7,6},{8,9},{9,8},{10,11... | collective-permute-start | bytes 1179656 | tf_op jit(solution)/shard_map/ppermute | solution.py:358
  224.4 18.9 %collective-permute-start.22 = (bf16[16,48,256]{2,1,0:T(8,128)(2,1)S(1)}, bf16[16,48,256]{2,1,0:T(8,128)(2,1)}, u32[]{:S(2)}, u32[]{:S(2)}) collective-permute-start(bf16[16,48,256]{2,1,0:T(8,128)(2,1)S(1)} %collective-permute-done.21.refs_0_), channel_id=1, source_target_pairs={{0,4},{1,5},{2,6},{3,7},{4,0},{5,1},{6,2},{7,3},{8,12},{9,13},{10,... | collective-permute-start | bytes 1179656 | tf_op jit(solution)/shard_map/ppermute | solution.py:358
  226.8 16.5 %collective-permute-start.24 = (bf16[16,48,256]{2,1,0:T(8,128)(2,1)S(1)}, bf16[16,48,256]{2,1,0:T(8,128)(2,1)}, u32[]{:S(2)}, u32[]{:S(2)}) collective-permute-start(bf16[16,48,256]{2,1,0:T(8,128)(2,1)S(1)} %collective-permute-done.23.refs_3_), channel_id=1, source_target_pairs={{0,1},{1,0},{2,3},{3,2},{4,5},{5,4},{6,7},{7,6},{8,9},{9,8},{10,11... | collective-permute-start | bytes 1179656 | tf_op jit(solution)/shard_map/ppermute | solution.py:358
  226.9 16.4 %collective-permute-start.25 = (bf16[16,48,256]{2,1,0:T(8,128)(2,1)S(1)}, bf16[16,48,256]{2,1,0:T(8,128)(2,1)}, u32[]{:S(2)}, u32[]{:S(2)}) collective-permute-start(bf16[16,48,256]{2,1,0:T(8,128)(2,1)S(1)} %collective-permute-done.23.refs_3_), channel_id=1, source_target_pairs={{0,3},{1,2},{2,1},{3,0},{4,7},{5,6},{6,5},{7,4},{8,11},{9,10},{10,... | collective-permute-start | bytes 1179656 | tf_op jit(solution)/shard_map/ppermute | solution.py:358
  234.1 4.0 %copy-start.1 = (bf16[2,8,1280,256]{3,2,1,0:T(8,128)(2,1)S(1)}, bf16[2,8,1280,256]{3,2,1,0:T(8,128)(2,1)}, u32[]{:S(2)}) copy-start(bf16[2,8,1280,256]{3,2,1,0:T(8,128)(2,1)} %copy-done) | copy-start | bytes 31457284
  263.6 17.6 %all-to-all-start.10 = ((bf16[16,3,32,256]{3,2,1,0:T(8,128)(2,1)}), bf16[16,3,32,256]{3,2,1,0:T(8,128)(2,1)S(1)}, u32[]{:S(2)}, u32[]{:S(2)}) async-start(bf16[16,3,32,256]{3,2,1,0:T(8,128)(2,1)} %trace_blocks.1), calls=%async_computation.10 | async-start | bytes 1572864 | tf_op jit(solution)/shard_map/all_to_all | solution.py:354
  270.4 11.0 %copy-start.7 = (f32[32,48,256]{2,1,0:T(8,128)S(1)}, f32[32,48,256]{2,1,0:T(8,128)}, u32[]{:S(2)}) copy-start(f32[32,48,256]{2,1,0:T(8,128)} %param.8) | copy-start | bytes 4718596

commit v5 on v4

--- a/solution.py
+++ b/solution.py
@@ -73,9 +73,9 @@
     out_ref[...] = flat.reshape(out_ref.shape)
 
 
-EARLY = (6, 5, 7)
-LATE = (2, 3, 1, 4, 0)
-NEIGHBOURS, REST = (3, 1), (2, 4, 0)
+EARLY = (5, 7)
+LATE = (2, 3, 1, 4, 0, 6)
+NEIGHBOURS, REST, LAST = (6, 3, 1), (2, 4, 0), (6, 5, 7)
 
 
 def fetch(held, order, refl_ref, held_ref, sems):
@@ -185,23 +185,23 @@
 
 
 def fetch_kernel(refl_ref, _, held_ref, sems):
-    for copy in fetch(EARLY, EARLY, refl_ref, held_ref, sems).values():
+    for copy in fetch(LAST, LAST, refl_ref, held_ref, sems).values():
         copy.wait()
 
 
-def fetch_early(reflection, panels, after):
+def fetch_last(reflection, panels, after):
     parts, freqs, receivers, width = reflection.shape
     return call(
         fetch_kernel,
-        "fetch_early",
-        pltpu.VMEM((parts, freqs, receivers // panels * len(EARLY), width), reflection.dtype),
+        "fetch_last",
+        pltpu.VMEM((parts, freqs, receivers // panels * len(LAST), width), reflection.dtype),
         (pltpu.with_memory_space_constraint(reflection, pltpu.HBM), after),
-        [pltpu.SemaphoreType.DMA((len(EARLY),))],
+        [pltpu.SemaphoreType.DMA((len(LAST),))],
         [pl.BlockSpec(memory_space=pltpu.HBM), pl.BlockSpec(memory_space=pl.ANY)],
     )
 
 
-def return_kernel(panels, final, *refs):
+def return_kernel(panels, final, order, *refs):
     blocks, refl_ref, refs = refs[:panels], refs[panels], refs[panels + 1 :]
     groups, block, width = blocks[0].shape
     freqs = refl_ref.shape[1]
@@ -209,25 +209,39 @@
     count = groups * block // step
     lanes = width // 128
     if final:
-        before, *more, out_ref, rows, results = refs
+        before, out_ref, rows, results = refs
     else:
-        total_ref, rows = refs
+        total_ref, rows, *refs = refs
+    if order:
+        held_ref, sems = refs
+        copies = fetch(order, order, refl_ref, held_ref, sems)
+        refl_ref = held_ref
 
     for p in range(panels):
         flat = blocks[p][...].reshape(groups * block, width).astype(jnp.float32)
         for h in range(lanes):
             rows[p * lanes + h] = flat[:, h * 128 : (h + 1) * 128]
 
+    def product(j, p):
+        of_panel = rows.at[pl.ds(p * lanes, lanes)]
+        real = pick(of_panel, 2 * j, step, count)
+        imag = pick(of_panel, 2 * j + 1, step, count)
+        direct = jnp.concatenate([real, imag], axis=0).astype(jnp.bfloat16)
+        crossed = jnp.concatenate([imag, -real], axis=0).astype(jnp.bfloat16)
+        at = slice(p * width, (p + 1) * width)
+        return dot(direct, refl_ref[0, j, at]) + dot(crossed, refl_ref[1, j, at])
+
+    for p, k in enumerate(order):
+        copies[k].wait()
+        for j in range(freqs):
+            total_ref[j] = product(j, p) if p == 0 else total_ref[j] + product(j, p)
+    if order:
+        return
+
     for j in range(freqs):
         total = before[j] if final else None
         for p in range(panels):
-            of_panel = rows.at[pl.ds(p * lanes, lanes)]
-            real = pick(of_panel, 2 * j, step, count)
-            imag = pick(of_panel, 2 * j + 1, step, count)
-            direct = jnp.concatenate([real, imag], axis=0).astype(jnp.bfloat16)
-            crossed = jnp.concatenate([imag, -real], axis=0).astype(jnp.bfloat16)
-            at = slice(p * width, (p + 1) * width)
-            part = dot(direct, refl_ref[0, j, at]) + dot(crossed, refl_ref[1, j, at])
+            part = product(j, p)
             total = part if total is None else total + part
         if final:
             place(results, 2 * j, step, total[:count])
@@ -235,31 +249,35 @@
         else:
             total_ref[j] = total
     if final:
-        emptied(results, out_ref.at[:, :block])
-        for ref in more:
-            out_ref[:, block:] = ref[...].reshape(groups, -1, width)
-
-
-def return_blocks(blocks, reflection, before=None, traces=()):
+        emptied(results, out_ref)
+
+
+def return_blocks(blocks, reflection, before=None, order=()):
     panels = len(blocks)
     groups, height, width = blocks[0].shape
     _, freqs, _, sources = reflection.shape
     count = groups * height // (2 * freqs)
     final = before is not None
-    more = sum(t.size // (groups * width) for t in traces)
     scratch = [pltpu.VMEM((panels * width // 128, groups * height, 128), jnp.float32)]
+    specs = None
     if final:
-        out_shape = jax.ShapeDtypeStruct((groups, height + more, sources), jnp.bfloat16)
+        out_shape = jax.ShapeDtypeStruct((groups, height, sources), jnp.bfloat16)
         scratch.append(pltpu.VMEM((sources // 128, groups * height, 128), jnp.float32))
     else:
         out_shape = jax.ShapeDtypeStruct((freqs, 2 * count, sources), jnp.float32)
-    return call(
-        lambda *refs: return_kernel(panels, final, *refs),
+    if order:
+        scratch.append(pltpu.VMEM((2, freqs, width * panels, sources), reflection.dtype))
+        scratch.append(pltpu.SemaphoreType.DMA((panels,)))
+        specs = [IN_VMEM] * panels + [pl.BlockSpec(memory_space=pltpu.HBM)]
+        reflection = pltpu.with_memory_space_constraint(reflection, pltpu.HBM)
+    return call(
+        lambda *refs: return_kernel(panels, final, order, *refs),
         "return_blocks",
         out_shape,
-        (*blocks, reflection, *([before] if final else []), *traces),
+        (*blocks, reflection, *([before] if final else [])),
         scratch,
-        flops=4 * reflection.size * count,
+        specs,
+        flops=4 * 2 * freqs * width * panels * sources * count,
     )
 
 
@@ -385,11 +403,11 @@
     for iteration in range(ITERS):
         is_first, last = iteration == 0, iteration == ITERS - 1
         bands = exchange(blocks, "freq")
-        (b6, b5, b7), by_freq, early = image_blocks(EARLY, EARLY, (bands,), early, panels, is_first)
-        r5, r7, r6 = send(b5, 1), send(b7, 3), send(b6, 4)
+        (b5, b7), by_freq, early = image_blocks(EARLY, EARLY, (bands,), early, panels, is_first)
+        r5, r7 = send(b5, 1), send(b7, 3)
         near = NEIGHBOURS if is_first else LATE
-        (b3, b1), _, _ = image_blocks(NEIGHBOURS, near, tuple(by_freq), late, panels, is_first, keep=False)
-        s1, s3 = send(b1, 1), send(b3, 3)
+        (b6, b3, b1), _, _ = image_blocks(NEIGHBOURS, near, tuple(by_freq), late, panels, is_first, keep=False)
+        r6, s1, s3 = send(b6, 4), send(b1, 1), send(b3, 3)
         (b2, b4, b0), _, late = image_blocks(REST, LATE, tuple(by_freq), late, panels, is_first)
         s2, s4 = send(added(b2, r6), 2), send(added(b4, r5, r7), 4)
         images = exchange(added(b0, s1, s3, s2, s4), "freq")
@@ -397,11 +415,14 @@
         m0 = exchange(spectra, "freq")
         m2, m4, m1, m3 = send(m0, 2), send(m0, 4), send(m0, 1), send(m0, 3)
         m6, m5, m7 = send(m2, 4), send(m4, 1), send(m4, 3)
-        partial = return_blocks((m2, m3, m1, m4, m0), late)
         if last:
+            partial = return_blocks((m2, m3, m1, m4, m0), reflection, order=LATE[:5])
             partial, upgoing = lax.optimization_barrier((partial, exchange(traces[0], "freq")))
-            early = fetch_early(reflection, panels, upgoing)
-        returns = exchange(return_blocks((m6, m5, m7), early, partial), "freq")
+            returns = return_blocks((m6, m5, m7), fetch_last(reflection, panels, upgoing), partial)
+        else:
+            partial = return_blocks((m2, m3, m1, m4, m0, m6), late)
+            returns = return_blocks((m5, m7), early, partial)
+        returns = exchange(returns, "freq")
         if last:
             upgoing = in_time(upgoing)
             traces = trace_blocks(returns, onsets, inverse, rows, count)

time: 284 us -> 280 us (0.986)
  waiting for transfers between devices: 66.3 us -> 56 us
  local copies, waits for them, and re-layouts: 6.32 us -> 2.34 us
  Pallas kernels: 36.8 us -> 40.6 us
  starting transfers between devices: 46.6 us -> 49.7 us
  blocking collectives: 122 us -> 125 us
    ppermute x28, waiting for transfers between devices: 55.5 us -> 45.2 us  [send(): lax.ppermute(block, 'panel', [(i, i ^ k) for i in range(lax.axis_size('pa...]
    unnamed x17 -> x13, local copies, waits for them, and re-layouts: 6.07 us -> 2.09 us
    pallas_call x16, Pallas kernels: 36.8 us -> 40.6 us  [call(): pl.pallas_call(kernel, in_specs=specs or [IN_VMEM] * len(args), out_specs...]
    all_to_all x9, blocking collectives: 122 us -> 125 us  [exchange(): return lax.all_to_all(blocks, axis, split_axis=0, concat_axis=0, tiled=True)]
    ppermute x28, starting transfers between devices: 36.9 us -> 40 us  [send(): lax.ppermute(block, 'panel', [(i, i ^ k) for i in range(lax.axis_size('pa...]
  transfers between devices with their start and end apart: 30 -> 30, of which waited for: 16 -> 18; matrix products, arithmetic and copies ran while one was open for 1% -> 1% of each run, Pallas kernels for 6% -> 9%
where the time goes in v5:
time: 280 us; the launch traced here: 279 us
  blocking collectives  125 us (45%)
  waiting for transfers between devices  56 us (20%)
  starting transfers between devices  49.7 us (18%)
  Pallas kernels  40.6 us (14%)
  other arithmetic  4.94 us (2%)
    all_to_all x9, blocking collectives, exchange(): return lax.all_to_all(blocks, axis, split_axis=0, concat_axis=0, tiled=True)  125 us
    ppermute x28, waiting for transfers between devices, send(): lax.ppermute(block, 'panel', [(i, i ^ k) for i in range(lax.axis_size('pa...  45.2 us
    pallas_call x16, Pallas kernels, call(): pl.pallas_call(kernel, in_specs=specs or [IN_VMEM] * len(args), out_specs...  40.6 us
    ppermute x28, starting transfers between devices, send(): lax.ppermute(block, 'panel', [(i, i ^ k) for i in range(lax.axis_size('pa...  40 us
    all_to_all x2, waiting for transfers between devices, exchange(): return lax.all_to_all(blocks, axis, split_axis=0, concat_axis=0, tiled=True)  10.8 us
    all_to_all x2, starting transfers between devices, exchange(): return lax.all_to_all(blocks, axis, split_axis=0, concat_axis=0, tiled=True)  9.7 us
  transfers between devices with their start and end apart: 30, of which 18 were waited for; matrix products, arithmetic and copies ran while one was open for 1% of the time, Pallas kernels for 9%

profile of v5, /device:TPU:1, one launch (start us, length us, event | category | flops | bytes accessed | tf_op | source)
XLA Modules:
  0.0 279.5 jit_solution(8365462540061152766)
XLA Ops:
  0.6 1.5 convert_element_type.99
  2.4 19.5 %all_to_all.55.traces_ref = bf16[16,3,32,256]{3,2,1,0:T(8,128)(2,1)S(1)} all-to-all(bf16[16,3,32,256]{3,2,1,0:T(8,128)(2,1)S(1)} %bitcast.11), channel_id=1, replica_groups=mesh['freq'=16,'panel'=8] {'freq'}, dimensions={0} | all-to-all | bytes 1572864 | tf_op jit(solution)/shard_map/all_to_all | solution.py:372
  21.9 0.6 start_bands.1
  22.5 11.9 %all_to_all.56.refs_0_ = bf16[16,48,256]{2,1,0:T(8,128)(2,1)S(1)} all-to-all(bf16[16,48,256]{2,1,0:T(8,128)(2,1)S(1)} %get-tuple-element.31), channel_id=1, replica_groups=mesh['freq'=16,'panel'=8] {'freq'}, dimensions={0} | all-to-all | bytes 786432 | tf_op jit(solution)/shard_map/all_to_all | solution.py:372
  34.4 3.2 %image_blocks.6 = (bf16[16,48,256]{2,1,0:T(8,128)(2,1)S(1)}, bf16[16,48,256]{2,1,0:T(8,128)(2,1)S(1)}, bf16[8,96,256]{2,1,0:T(8,128)(2,1)S(1)}, bf16[8,96,256]{2...) custom-call(bf16[16,48,256]{2,1,0:T(8,128)(2,1)S(1)} %all_to_all.56.refs_0_, bf16[2,8,2048,256]{3,2,1,0:T(8,128)(2,1)} %refl_ref.1), custom_call_target="tpu_custom_call" | custom-call | flops 402653184 | bytes 34340864 | tf_op jit(solution)/shard_map/image_blocks/pallas_call | solution.py:139
  37.6 3.8 %collective-permute-start.5 = (bf16[16,48,256]{2,1,0:T(8,128)(2,1)S(1)}, bf16[16,48,256]{2,1,0:T(8,128)(2,1)S(1)}, u32[]{:S(2)}, u32[]{:S(2)}) collective-permute-start(bf16[16,48,256]{2,1,0:T(8,128)(2,1)S(1)} %get-tuple-element.41), channel_id=1, source_target_pairs={{0,3},{1,2},{2,1},{3,0},{4,7},{5,6},{6,5},{7,4},{8,11},{9,10},{10,... | collective-permute-start | bytes 1179656 | tf_op jit(solution)/shard_map/ppermute | solution.py:376
  41.4 4.0 %image_blocks.8 = (bf16[16,48,256]{2,1,0:T(8,128)(2,1)S(1)}, bf16[16,48,256]{2,1,0:T(8,128)(2,1)S(1)}, bf16[16,48,256]{2,1,0:T(8,128)(2,1)S(1)}) custom-call(bf16[8,96,256]{2,1,0:T(8,128)(2,1)S(1)} %get-tuple-element.32.refs_0_, bf16[8,96,256]{2,1,0:T(8,128)(2,1)S(1)} %get-tuple-element.33.refs_1_, bf16[2,8,2048,256]{3,2,1,0:T(8,128)(2,1)} %refl_ref.1), custom_call_target="tpu_custom_call" | custom-call | flops 603979776 | bytes 35127296 | tf_op jit(solution)/shard_map/image_blocks/pallas_call | solution.py:139
  45.5 2.5 collective-permute-start.2
  48.2 1.3 collective-permute-start
  49.5 4.7 %image_blocks.7 = (bf16[16,48,256]{2,1,0:T(8,128)(2,1)S(1)}, bf16[16,48,256]{2,1,0:T(8,128)(2,1)S(1)}, bf16[16,48,256]{2,1,0:T(8,128)(2,1)S(1)}, bf16[2,8,1536,256]{3,2,1,0:T(8,128)(2,1)S(1)}) custom-call(bf16[8,96,256]{2,1,0:T(8,128)(2,1)S(1)} %get-tuple-element.32.refs_0_, bf16[8,96,256]{2,1,0:T(8,128)(2,1)S(1)} %get-tuple-element.33.refs_1_, ...), custom_call_target="tpu_custom_call" | custom-call | flops 603979776 | bytes 35127296 | tf_op jit(solution)/shard_map/image_blocks/pallas_call | solution.py:139
  54.4 0.6 collective-permute-start.6
  55.0 1.2 collective-permute-done.2
  56.3 1.4 collective-permute-start.3
  58.1 1.3 collective-permute-done
  59.4 4.9 %collective-permute-done.6 = bf16[16,48,256]{2,1,0:T(8,128)(2,1)S(1)} collective-permute-done((bf16[16,48,256]{2,1,0:T(8,128)(2,1)S(1)}, bf16[16,48,256]{2,1,0:T(8,128)(2,1)S(1)}, u32[]{:S(2)}, u32[]{:S(2)}) %collective-permute-start.6) | collective-permute-done | bytes 393248 | tf_op jit(solution)/shard_map/ppermute | solution.py:376
  64.3 3.6 %collective-permute-done.3 = bf16[16,48,256]{2,1,0:T(8,128)(2,1)S(1)} collective-permute-done((bf16[16,48,256]{2,1,0:T(8,128)(2,1)S(1)}, bf16[16,48,256]{2,1,0:T(8,128)(2,1)S(1)}, u32[]{:S(2)}, u32[]{:S(2)}) %collective-permute-start.3) | collective-permute-done | bytes 393248 | tf_op jit(solution)/shard_map/ppermute | solution.py:376
  68.1 14.1 %all_to_all.57.refs_5_ = bf16[16,48,256]{2,1,0:T(8,128)(2,1)S(1)} all-to-all(bf16[16,48,256]{2,1,0:T(8,128)(2,1)S(1)} %add_convert_fusion.3), channel_id=1, replica_groups=mesh['freq'=16,'panel'=8] {'freq'}, dimensions={0} | all-to-all | bytes 786432 | tf_op jit(solution)/shard_map/all_to_all | solution.py:372
  82.2 1.5 upgoing_blocks.2
  83.8 12.1 %all_to_all.58.refs_4_ = bf16[16,48,256]{2,1,0:T(8,128)(2,1)S(1)} all-to-all(bf16[16,48,256]{2,1,0:T(8,128)(2,1)S(1)} %upgoing_blocks.2), channel_id=1, replica_groups=mesh['freq'=16,'panel'=8] {'freq'}, dimensions={0} | all-to-all | bytes 786432 | tf_op jit(solution)/shard_map/all_to_all | solution.py:372
  95.8 1.3 collective-permute-start.10
  97.1 2.5 collective-permute-start.7
  99.6 2.3 collective-permute-start.11
  101.8 5.0 %collective-permute-done.10.refs_0_ = bf16[16,48,256]{2,1,0:T(8,128)(2,1)S(1)} collective-permute-done((bf16[16,48,256]{2,1,0:T(8,128)(2,1)S(1)}, bf16[16,48,256]{2,1,0:T(8,128)(2,1)S(1)}, u32[]{:S(2)}, u32[]{:S(2)}) %collective-permute-start.10) | collective-permute-done | bytes 393248 | tf_op jit(solution)/shard_map/ppermute | solution.py:376
  106.8 2.5 collective-permute-start.13
  109.3 1.1 collective-permute-start.8
  111.0 5.8 %collective-permute-done.11.refs_1_ = bf16[16,48,256]{2,1,0:T(8,128)(2,1)S(1)} collective-permute-done((bf16[16,48,256]{2,1,0:T(8,128)(2,1)S(1)}, bf16[16,48,256]{2,1,0:T(8,128)(2,1)S(1)}, u32[]{:S(2)}, u32[]{:S(2)}) %collective-permute-start.11) | collective-permute-done | bytes 393248 | tf_op jit(solution)/shard_map/ppermute | solution.py:376
  116.8 2.7 return_blocks.4.refs_3_
  119.5 3.4 %collective-permute-done.8.refs_0_ = bf16[16,48,256]{2,1,0:T(8,128)(2,1)S(1)} collective-permute-done((bf16[16,48,256]{2,1,0:T(8,128)(2,1)S(1)}, bf16[16,48,256]{2,1,0:T(8,128)(2,1)S(1)}, u32[]{:S(2)}, u32[]{:S(2)}) %collective-permute-start.8) | collective-permute-done | bytes 393248 | tf_op jit(solution)/shard_map/ppermute | solution.py:376
  123.0 1.3 return_blocks.5
  124.3 14.1 %all_to_all.59.refs_6_ = bf16[16,48,256]{2,1,0:T(8,128)(2,1)S(1)} all-to-all(bf16[16,48,256]{2,1,0:T(8,128)(2,1)S(1)} %return_blocks.5), channel_id=1, replica_groups=mesh['freq'=16,'panel'=8] {'freq'}, dimensions={0} | all-to-all | bytes 786432 | tf_op jit(solution)/shard_map/all_to_all | solution.py:372
  138.4 1.5 focus_blocks.1
  140.0 12.1 %all_to_all.60.refs_0_ = bf16[16,48,256]{2,1,0:T(8,128)(2,1)S(1)} all-to-all(bf16[16,48,256]{2,1,0:T(8,128)(2,1)S(1)} %focus_blocks.1), channel_id=1, replica_groups=mesh['freq'=16,'panel'=8] {'freq'}, dimensions={0} | all-to-all | bytes 786432 | tf_op jit(solution)/shard_map/all_to_all | solution.py:372
  152.0 1.5 image_blocks.9
  153.6 1.8 collective-permute-start.19
  155.4 2.1 image_blocks.11
  157.5 2.5 collective-permute-start.16
  160.0 1.5 collective-permute-start.15
  161.9 2.1 image_blocks.10
  164.7 2.5 collective-permute-start.20
  167.2 1.0 collective-permute-done.16
  168.3 2.0 collective-permute-start.17
  170.3 2.4 collective-permute-done.15
  172.9 2.1 collective-permute-done.20
  175.0 7.1 %collective-permute-done.17 = bf16[16,48,256]{2,1,0:T(8,128)(2,1)S(1)} collective-permute-done((bf16[16,48,256]{2,1,0:T(8,128)(2,1)S(1)}, bf16[16,48,256]{2,1,0:T(8,128)(2,1)S(1)}, u32[]{:S(2)}, u32[]{:S(2)}) %collective-permute-start.17) | collective-permute-done | bytes 393248 | tf_op jit(solution)/shard_map/ppermute | solution.py:376
  182.3 13.8 %all_to_all.61.refs_5_ = bf16[16,48,256]{2,1,0:T(8,128)(2,1)S(1)} all-to-all(bf16[16,48,256]{2,1,0:T(8,128)(2,1)S(1)} %add_convert_fusion), channel_id=1, replica_groups=mesh['freq'=16,'panel'=8] {'freq'}, dimensions={0} | all-to-all | bytes 786432 | tf_op jit(solution)/shard_map/all_to_all | solution.py:372
  196.1 2.2 upgoing_blocks.3
  198.3 12.1 %all_to_all.62.refs_4_ = bf16[16,48,256]{2,1,0:T(8,128)(2,1)S(1)} all-to-all(bf16[16,48,256]{2,1,0:T(8,128)(2,1)S(1)} %get-tuple-element.54), channel_id=1, replica_groups=mesh['freq'=16,'panel'=8] {'freq'}, dimensions={0} | all-to-all | bytes 786432 | tf_op jit(solution)/shard_map/all_to_all | solution.py:372
  210.3 0.8 collective-permute-start.21
  211.1 2.5 collective-permute-start.23
  213.6 5.1 %all-to-all-start.8 = ((bf16[16,3,32,256]{3,2,1,0:T(8,128)(2,1)}), bf16[16,3,32,256]{3,2,1,0:T(8,128)(2,1)S(1)}, u32[]{:S(2)}, u32[]{:S(2)}) async-start(bf16[16,3,32,256]{3,2,1,0:T(8,128)(2,1)} %get-tuple-element.55), calls=%async_computation.8 | async-start | bytes 1572864 | tf_op jit(solution)/shard_map/all_to_all | solution.py:372
  218.7 1.5 collective-permute-start.26
  220.6 0.8 collective-permute-done.21.refs_0_
  221.4 2.5 collective-permute-start.22
  223.8 1.7 collective-permute-start.25
  225.5 5.5 %collective-permute-done.26.refs_1_ = bf16[16,48,256]{2,1,0:T(8,128)(2,1)S(1)} collective-permute-done((bf16[16,48,256]{2,1,0:T(8,128)(2,1)S(1)}, bf16[16,48,256]{2,1,0:T(8,128)(2,1)S(1)}, u32[]{:S(2)}, u32[]{:S(2)}) %collective-permute-start.26) | collective-permute-done | bytes 393248 | tf_op jit(solution)/shard_map/ppermute | solution.py:376
  231.0 5.8 %return_blocks.6.refs_4_ = f32[8,96,256]{2,1,0:T(8,128)S(1)} custom-call(bf16[16,48,256]{2,1,0:T(8,128)(2,1)} %collective-permute-done.21.refs_0_, bf16[16,48,256]{2,1,0:T(8,128)(2,1)S(1)} %collective-permute-done.26.refs_1_, bf16[16,48,256]{2,1,0:T(8,128)(2,1)S(1)} %collective-permute-done.27.refs_2_, bf16[16,48,256]{2,1,0:T(8,128)(2,1)} %collective-permute-done.23.refs_3_, ...), custom_call_target="tpu_custom_call" | custom-call | flops 1006632960 | bytes 37486592 | tf_op jit(solution)/shard_map/return_blocks/pallas_call | solution.py:139
  236.8 2.9 %fetch_last.1.refs_3_ = bf16[2,8,768,256]{3,2,1,0:T(8,128)(2,1)S(1)} custom-call(bf16[2,8,2048,256]{3,2,1,0:T(8,128)(2,1)} %refl_ref.1, bf16[16,3,32,256]{3,2,1,0:T(8,128)(2,1)S(1)} %all-to-all-done.8._), custom_call_target="tpu_custom_call" | custom-call | bytes 35127296 | tf_op jit(solution)/shard_map/fetch_last/pallas_call | solution.py:139
  239.7 2.7 return_blocks.7
  242.4 15.5 %all_to_all.63.refs_3_ = bf16[16,48,256]{2,1,0:T(8,128)(2,1)S(1)} all-to-all(bf16[16,48,256]{2,1,0:T(8,128)(2,1)S(1)} %return_blocks.7), channel_id=1, replica_groups=mesh['freq'=16,'panel'=8] {'freq'}, dimensions={0} | all-to-all | bytes 786432 | tf_op jit(solution)/shard_map/all_to_all | solution.py:372
  257.9 1.6 trace_blocks.1
  259.5 4.6 %all-to-all-start.10 = ((bf16[16,3,32,256]{3,2,1,0:T(8,128)(2,1)}), bf16[16,3,32,256]{3,2,1,0:T(8,128)(2,1)S(1)}, u32[]{:S(2)}, u32[]{:S(2)}) async-start(bf16[16,3,32,256]{3,2,1,0:T(8,128)(2,1)} %trace_blocks.1), calls=%async_computation.10 | async-start | bytes 1572864 | tf_op jit(solution)/shard_map/all_to_all | solution.py:372
  264.3 2.1 copy.11
  266.4 10.8 %all-to-all-done.10 = bf16[16,3,32,256]{3,2,1,0:T(8,128)(2,1)S(1)} async-done(((bf16[16,3,32,256]{3,2,1,0:T(8,128)(2,1)}), bf16[16,3,32,256]{3,2,1,0:T(8,128)(2,1)S(1)}, u32[]{:S(2)}, u32[]{:S(2)}) %all-to-all-start.10) | async-done | bytes 786464 | tf_op jit(solution)/shard_map/all_to_all | solution.py:372
  277.4 2.1 copy_add_fusion
  (45 shorter events, 4.2 us)
Async XLA Ops:
  2.1 19.8 %copy-start = (bf16[256,512]{1,0:T(8,128)(2,1)S(1)}, bf16[256,512]{1,0:T(8,128)(2,1)}, u32[]{:S(2)}) copy-start(bf16[256,512]{1,0:T(8,128)(2,1)} %constant.8.clone.high.refs_2_) | copy-start | bytes 786436
  2.1 19.8 %copy-start.1 = (bf16[256,512]{1,0:T(8,128)(2,1)S(1)}, bf16[256,512]{1,0:T(8,128)(2,1)}, u32[]{:S(2)}) copy-start(bf16[256,512]{1,0:T(8,128)(2,1)} %constant.9.clone.low.refs_3_) | copy-start | bytes 786436
  37.6 16.6 %collective-permute-start.5 = (bf16[16,48,256]{2,1,0:T(8,128)(2,1)S(1)}, bf16[16,48,256]{2,1,0:T(8,128)(2,1)S(1)}, u32[]{:S(2)}, u32[]{:S(2)}) collective-permute-start(bf16[16,48,256]{2,1,0:T(8,128)(2,1)S(1)} %get-tuple-element.41), channel_id=1, source_target_pairs={{0,3},{1,2},{2,1},{3,0},{4,7},{5,6},{6,5},{7,4},{8,11},{9,10},{10,... | collective-permute-start | bytes 1179656 | tf_op jit(solution)/shard_map/ppermute | solution.py:376
  41.4 12.8 %collective-permute-start.4 = (bf16[16,48,256]{2,1,0:T(8,128)(2,1)S(1)}, bf16[16,48,256]{2,1,0:T(8,128)(2,1)S(1)}, u32[]{:S(2)}, u32[]{:S(2)}) collective-permute-start(bf16[16,48,256]{2,1,0:T(8,128)(2,1)S(1)} %get-tuple-element.40), channel_id=1, source_target_pairs={{0,1},{1,0},{2,3},{3,2},{4,5},{5,4},{6,7},{7,6},{8,9},{9,8},{10,11... | collective-permute-start | bytes 1179656 | tf_op jit(solution)/shard_map/ppermute | solution.py:376
  45.5 10.7 %collective-permute-start.2 = (bf16[16,48,256]{2,1,0:T(8,128)(2,1)S(1)}, bf16[16,48,256]{2,1,0:T(8,128)(2,1)S(1)}, u32[]{:S(2)}, u32[]{:S(2)}) collective-permute-start(bf16[16,48,256]{2,1,0:T(8,128)(2,1)S(1)} %get-tuple-element.38), channel_id=1, source_target_pairs={{0,4},{1,5},{2,6},{3,7},{4,0},{5,1},{6,2},{7,3},{8,12},{9,13},{10,... | collective-permute-start | bytes 1179656 | tf_op jit(solution)/shard_map/ppermute | solution.py:376
  48.0 10.1 %collective-permute-start.1 = (bf16[16,48,256]{2,1,0:T(8,128)(2,1)S(1)}, bf16[16,48,256]{2,1,0:T(8,128)(2,1)S(1)}, u32[]{:S(2)}, u32[]{:S(2)}) collective-permute-start(bf16[16,48,256]{2,1,0:T(8,128)(2,1)S(1)} %get-tuple-element.36), channel_id=1, source_target_pairs={{0,3},{1,2},{2,1},{3,0},{4,7},{5,6},{6,5},{7,4},{8,11},{9,10},{10,... | collective-permute-start | bytes 1179656 | tf_op jit(solution)/shard_map/ppermute | solution.py:376
  48.2 11.2 %collective-permute-start = (bf16[16,48,256]{2,1,0:T(8,128)(2,1)S(1)}, bf16[16,48,256]{2,1,0:T(8,128)(2,1)S(1)}, u32[]{:S(2)}, u32[]{:S(2)}) collective-permute-start(bf16[16,48,256]{2,1,0:T(8,128)(2,1)S(1)} %get-tuple-element.35), channel_id=1, source_target_pairs={{0,1},{1,0},{2,3},{3,2},{4,5},{5,4},{6,7},{7,6},{8,9},{9,8},{10,11... | collective-permute-start | bytes 1179656 | tf_op jit(solution)/shard_map/ppermute | solution.py:376
  54.4 9.9 %collective-permute-start.6 = (bf16[16,48,256]{2,1,0:T(8,128)(2,1)S(1)}, bf16[16,48,256]{2,1,0:T(8,128)(2,1)S(1)}, u32[]{:S(2)}, u32[]{:S(2)}) collective-permute-start(bf16[16,48,256]{2,1,0:T(8,128)(2,1)S(1)} %add_convert_fusion.4), channel_id=1, source_target_pairs={{0,4},{1,5},{2,6},{3,7},{4,0},{5,1},{6,2},{7,3},{8,12},{9,13},{10,... | collective-permute-start | bytes 1179656 | tf_op jit(solution)/shard_map/ppermute | solution.py:376
  56.3 11.5 %collective-permute-start.3 = (bf16[16,48,256]{2,1,0:T(8,128)(2,1)S(1)}, bf16[16,48,256]{2,1,0:T(8,128)(2,1)S(1)}, u32[]{:S(2)}, u32[]{:S(2)}) collective-permute-start(bf16[16,48,256]{2,1,0:T(8,128)(2,1)S(1)} %add_convert_fusion.5), channel_id=1, source_target_pairs={{0,2},{1,3},{2,0},{3,1},{4,6},{5,7},{6,4},{7,5},{8,10},{9,11},{10,... | collective-permute-start | bytes 1179656 | tf_op jit(solution)/shard_map/ppermute | solution.py:376
  67.9 14.3 %copy-start.2 = (bf16[512,256]{1,0:T(8,128)(2,1)S(1)}, bf16[512,256]{1,0:T(8,128)(2,1)}, u32[]{:S(2)}) copy-start(bf16[512,256]{1,0:T(8,128)(2,1)} %constant.10.clone.refs_0_) | copy-start | bytes 786436
  67.9 14.3 %copy-start.3 = (bf16[512,256]{1,0:T(8,128)(2,1)S(1)}, bf16[512,256]{1,0:T(8,128)(2,1)}, u32[]{:S(2)}) copy-start(bf16[512,256]{1,0:T(8,128)(2,1)} %constant.11.clone.refs_1_) | copy-start | bytes 786436
  67.9 14.3 %copy-start.4 = (s32[48,256]{1,0:T(8,128)S(1)}, s32[48,256]{1,0:T(8,128)}, u32[]{:S(2)}) copy-start(s32[48,256]{1,0:T(8,128)} %refs_2_.8) | copy-start | bytes 147460
  95.8 11.0 %collective-permute-start.10 = (bf16[16,48,256]{2,1,0:T(8,128)(2,1)S(1)}, bf16[16,48,256]{2,1,0:T(8,128)(2,1)S(1)}, u32[]{:S(2)}, u32[]{:S(2)}) collective-permute-start(bf16[16,48,256]{2,1,0:T(8,128)(2,1)S(1)} %all_to_all.58.refs_4_), channel_id=1, source_target_pairs={{0,2},{1,3},{2,0},{3,1},{4,6},{5,7},{6,4},{7,5},{8,10},{9,11},{10,... | collective-permute-start | bytes 1179656 | tf_op jit(solution)/shard_map/ppermute | solution.py:376
  97.1 12.2 %collective-permute-start.7 = (bf16[16,48,256]{2,1,0:T(8,128)(2,1)S(1)}, bf16[16,48,256]{2,1,0:T(8,128)(2,1)S(1)}, u32[]{:S(2)}, u32[]{:S(2)}) collective-permute-start(bf16[16,48,256]{2,1,0:T(8,128)(2,1)S(1)} %all_to_all.58.refs_4_), channel_id=1, source_target_pairs={{0,4},{1,5},{2,6},{3,7},{4,0},{5,1},{6,2},{7,3},{8,12},{9,13},{10,... | collective-permute-start | bytes 1179656 | tf_op jit(solution)/shard_map/ppermute | solution.py:376
  99.6 17.2 %collective-permute-start.11 = (bf16[16,48,256]{2,1,0:T(8,128)(2,1)S(1)}, bf16[16,48,256]{2,1,0:T(8,128)(2,1)S(1)}, u32[]{:S(2)}, u32[]{:S(2)}) collective-permute-start(bf16[16,48,256]{2,1,0:T(8,128)(2,1)S(1)} %all_to_all.58.refs_4_), channel_id=1, source_target_pairs={{0,3},{1,2},{2,1},{3,0},{4,7},{5,6},{6,5},{7,4},{8,11},{9,10},{10,... | collective-permute-start | bytes 1179656 | tf_op jit(solution)/shard_map/ppermute | solution.py:376
  101.8 15.0 %collective-permute-start.12 = (bf16[16,48,256]{2,1,0:T(8,128)(2,1)S(1)}, bf16[16,48,256]{2,1,0:T(8,128)(2,1)S(1)}, u32[]{:S(2)}, u32[]{:S(2)}) collective-permute-start(bf16[16,48,256]{2,1,0:T(8,128)(2,1)S(1)} %all_to_all.58.refs_4_), channel_id=1, source_target_pairs={{0,1},{1,0},{2,3},{3,2},{4,5},{5,4},{6,7},{7,6},{8,9},{9,8},{10,11... | collective-permute-start | bytes 1179656 | tf_op jit(solution)/shard_map/ppermute | solution.py:376
  106.8 10.0 %collective-permute-start.13 = (bf16[16,48,256]{2,1,0:T(8,128)(2,1)S(1)}, bf16[16,48,256]{2,1,0:T(8,128)(2,1)S(1)}, u32[]{:S(2)}, u32[]{:S(2)}) collective-permute-start(bf16[16,48,256]{2,1,0:T(8,128)(2,1)S(1)} %collective-permute-done.10.refs_0_), channel_id=1, source_target_pairs={{0,4},{1,5},{2,6},{3,7},{4,0},{5,1},{6,2},{7,3},{8,12},{9,13},{10,... | collective-permute-start | bytes 1179656 | tf_op jit(solution)/shard_map/ppermute | solution.py:376
  109.3 13.7 %collective-permute-start.8 = (bf16[16,48,256]{2,1,0:T(8,128)(2,1)S(1)}, bf16[16,48,256]{2,1,0:T(8,128)(2,1)S(1)}, u32[]{:S(2)}, u32[]{:S(2)}) collective-permute-start(bf16[16,48,256]{2,1,0:T(8,128)(2,1)S(1)} %collective-permute-done.7.refs_3_), channel_id=1, source_target_pairs={{0,1},{1,0},{2,3},{3,2},{4,5},{5,4},{6,7},{7,6},{8,9},{9,8},{10,11... | collective-permute-start | bytes 1179656 | tf_op jit(solution)/shard_map/ppermute | solution.py:376
  110.4 12.6 %collective-permute-start.9 = (bf16[16,48,256]{2,1,0:T(8,128)(2,1)S(1)}, bf16[16,48,256]{2,1,0:T(8,128)(2,1)S(1)}, u32[]{:S(2)}, u32[]{:S(2)}) collective-permute-start(bf16[16,48,256]{2,1,0:T(8,128)(2,1)S(1)} %collective-permute-done.7.refs_3_), channel_id=1, source_target_pairs={{0,3},{1,2},{2,1},{3,0},{4,7},{5,6},{6,5},{7,4},{8,11},{9,10},{10,... | collective-permute-start | bytes 1179656 | tf_op jit(solution)/shard_map/ppermute | solution.py:376
  153.6 10.7 %collective-permute-start.19 = (bf16[16,48,256]{2,1,0:T(8,128)(2,1)S(1)}, bf16[16,48,256]{2,1,0:T(8,128)(2,1)S(1)}, u32[]{:S(2)}, u32[]{:S(2)}) collective-permute-start(bf16[16,48,256]{2,1,0:T(8,128)(2,1)S(1)} %get-tuple-element.53), channel_id=1, source_target_pairs={{0,3},{1,2},{2,1},{3,0},{4,7},{5,6},{6,5},{7,4},{8,11},{9,10},{10,... | collective-permute-start | bytes 1179656 | tf_op jit(solution)/shard_map/ppermute | solution.py:376
  155.3 9.2 %collective-permute-start.18 = (bf16[16,48,256]{2,1,0:T(8,128)(2,1)S(1)}, bf16[16,48,256]{2,1,0:T(8,128)(2,1)S(1)}, u32[]{:S(2)}, u32[]{:S(2)}) collective-permute-start(bf16[16,48,256]{2,1,0:T(8,128)(2,1)S(1)} %get-tuple-element.52), channel_id=1, source_target_pairs={{0,1},{1,0},{2,3},{3,2},{4,5},{5,4},{6,7},{7,6},{8,9},{9,8},{10,11... | collective-permute-start | bytes 1179656 | tf_op jit(solution)/shard_map/ppermute | solution.py:376
  157.5 10.7 %collective-permute-start.16 = (bf16[16,48,256]{2,1,0:T(8,128)(2,1)S(1)}, bf16[16,48,256]{2,1,0:T(8,128)(2,1)S(1)}, u32[]{:S(2)}, u32[]{:S(2)}) collective-permute-start(bf16[16,48,256]{2,1,0:T(8,128)(2,1)S(1)} %get-tuple-element.50), channel_id=1, source_target_pairs={{0,4},{1,5},{2,6},{3,7},{4,0},{5,1},{6,2},{7,3},{8,12},{9,13},{10,... | collective-permute-start | bytes 1179656 | tf_op jit(solution)/shard_map/ppermute | solution.py:376
  160.0 12.7 %collective-permute-start.15 = (bf16[16,48,256]{2,1,0:T(8,128)(2,1)S(1)}, bf16[16,48,256]{2,1,0:T(8,128)(2,1)S(1)}, u32[]{:S(2)}, u32[]{:S(2)}) collective-permute-start(bf16[16,48,256]{2,1,0:T(8,128)(2,1)S(1)} %get-tuple-element.48), channel_id=1, source_target_pairs={{0,3},{1,2},{2,1},{3,0},{4,7},{5,6},{6,5},{7,4},{8,11},{9,10},{10,... | collective-permute-start | bytes 1179656 | tf_op jit(solution)/shard_map/ppermute | solution.py:376
  161.5 11.4 %collective-permute-start.14 = (bf16[16,48,256]{2,1,0:T(8,128)(2,1)S(1)}, bf16[16,48,256]{2,1,0:T(8,128)(2,1)S(1)}, u32[]{:S(2)}, u32[]{:S(2)}) collective-permute-start(bf16[16,48,256]{2,1,0:T(8,128)(2,1)S(1)} %get-tuple-element.47), channel_id=1, source_target_pairs={{0,1},{1,0},{2,3},{3,2},{4,5},{5,4},{6,7},{7,6},{8,9},{9,8},{10,11... | collective-permute-start | bytes 1179656 | tf_op jit(solution)/shard_map/ppermute | solution.py:376
  164.7 10.3 %collective-permute-start.20 = (bf16[16,48,256]{2,1,0:T(8,128)(2,1)S(1)}, bf16[16,48,256]{2,1,0:T(8,128)(2,1)S(1)}, u32[]{:S(2)}, u32[]{:S(2)}) collective-permute-start(bf16[16,48,256]{2,1,0:T(8,128)(2,1)S(1)} %add_convert_fusion.1), channel_id=1, source_target_pairs={{0,4},{1,5},{2,6},{3,7},{4,0},{5,1},{6,2},{7,3},{8,12},{9,13},{10,... | collective-permute-start | bytes 1179656 | tf_op jit(solution)/shard_map/ppermute | solution.py:376
  168.3 13.8 %collective-permute-start.17 = (bf16[16,48,256]{2,1,0:T(8,128)(2,1)S(1)}, bf16[16,48,256]{2,1,0:T(8,128)(2,1)S(1)}, u32[]{:S(2)}, u32[]{:S(2)}) collective-permute-start(bf16[16,48,256]{2,1,0:T(8,128)(2,1)S(1)} %add_convert_fusion.2), channel_id=1, source_target_pairs={{0,2},{1,3},{2,0},{3,1},{4,6},{5,7},{6,4},{7,5},{8,10},{9,11},{10,... | collective-permute-start | bytes 1179656 | tf_op jit(solution)/shard_map/ppermute | solution.py:376
  210.3 11.0 %collective-permute-start.21 = (bf16[16,48,256]{2,1,0:T(8,128)(2,1)S(1)}, bf16[16,48,256]{2,1,0:T(8,128)(2,1)}, u32[]{:S(2)}, u32[]{:S(2)}) collective-permute-start(bf16[16,48,256]{2,1,0:T(8,128)(2,1)S(1)} %all_to_all.62.refs_4_), channel_id=1, source_target_pairs={{0,2},{1,3},{2,0},{3,1},{4,6},{5,7},{6,4},{7,5},{8,10},{9,11},{10,... | collective-permute-start | bytes 1179656 | tf_op jit(solution)/shard_map/ppermute | solution.py:376
  211.1 12.7 %collective-permute-start.23 = (bf16[16,48,256]{2,1,0:T(8,128)(2,1)S(1)}, bf16[16,48,256]{2,1,0:T(8,128)(2,1)}, u32[]{:S(2)}, u32[]{:S(2)}) collective-permute-start(bf16[16,48,256]{2,1,0:T(8,128)(2,1)S(1)} %all_to_all.62.refs_4_), channel_id=1, source_target_pairs={{0,4},{1,5},{2,6},{3,7},{4,0},{5,1},{6,2},{7,3},{8,12},{9,13},{10,... | collective-permute-start | bytes 1179656 | tf_op jit(solution)/shard_map/ppermute | solution.py:376
  213.6 23.2 %all-to-all-start.8 = ((bf16[16,3,32,256]{3,2,1,0:T(8,128)(2,1)}), bf16[16,3,32,256]{3,2,1,0:T(8,128)(2,1)S(1)}, u32[]{:S(2)}, u32[]{:S(2)}) async-start(bf16[16,3,32,256]{3,2,1,0:T(8,128)(2,1)} %get-tuple-element.55), calls=%async_computation.8 | async-start | bytes 1572864 | tf_op jit(solution)/shard_map/all_to_all | solution.py:372
  218.7 12.3 %collective-permute-start.26 = (bf16[16,48,256]{2,1,0:T(8,128)(2,1)S(1)}, bf16[16,48,256]{2,1,0:T(8,128)(2,1)S(1)}, u32[]{:S(2)}, u32[]{:S(2)}) collective-permute-start(bf16[16,48,256]{2,1,0:T(8,128)(2,1)S(1)} %all_to_all.62.refs_4_), channel_id=1, source_target_pairs={{0,3},{1,2},{2,1},{3,0},{4,7},{5,6},{6,5},{7,4},{8,11},{9,10},{10,... | collective-permute-start | bytes 1179656 | tf_op jit(solution)/shard_map/ppermute | solution.py:376
  220.2 10.7 %collective-permute-start.27 = (bf16[16,48,256]{2,1,0:T(8,128)(2,1)S(1)}, bf16[16,48,256]{2,1,0:T(8,128)(2,1)S(1)}, u32[]{:S(2)}, u32[]{:S(2)}) collective-permute-start(bf16[16,48,256]{2,1,0:T(8,128)(2,1)S(1)} %all_to_all.62.refs_4_), channel_id=1, source_target_pairs={{0,1},{1,0},{2,3},{3,2},{4,5},{5,4},{6,7},{7,6},{8,9},{9,8},{10,11... | collective-permute-start | bytes 1179656 | tf_op jit(solution)/shard_map/ppermute | solution.py:376
  221.4 18.3 %collective-permute-start.22 = (bf16[16,48,256]{2,1,0:T(8,128)(2,1)}, bf16[16,48,256]{2,1,0:T(8,128)(2,1)S(1)}, u32[]{:S(2)}, u32[]{:S(2)}) collective-permute-start(bf16[16,48,256]{2,1,0:T(8,128)(2,1)} %collective-permute-done.21.refs_0_), channel_id=1, source_target_pairs={{0,4},{1,5},{2,6},{3,7},{4,0},{5,1},{6,2},{7,3},{8,12},{9,13},{10,... | collective-permute-start | bytes 1179656 | tf_op jit(solution)/shard_map/ppermute | solution.py:376
  223.8 15.8 %collective-permute-start.24 = (bf16[16,48,256]{2,1,0:T(8,128)(2,1)}, bf16[16,48,256]{2,1,0:T(8,128)(2,1)S(1)}, u32[]{:S(2)}, u32[]{:S(2)}) collective-permute-start(bf16[16,48,256]{2,1,0:T(8,128)(2,1)} %collective-permute-done.23.refs_3_), channel_id=1, source_target_pairs={{0,1},{1,0},{2,3},{3,2},{4,5},{5,4},{6,7},{7,6},{8,9},{9,8},{10,11... | collective-permute-start | bytes 1179656 | tf_op jit(solution)/shard_map/ppermute | solution.py:376
  223.8 15.9 %collective-permute-start.25 = (bf16[16,48,256]{2,1,0:T(8,128)(2,1)}, bf16[16,48,256]{2,1,0:T(8,128)(2,1)}, u32[]{:S(2)}, u32[]{:S(2)}) collective-permute-start(bf16[16,48,256]{2,1,0:T(8,128)(2,1)} %collective-permute-done.23.refs_3_), channel_id=1, source_target_pairs={{0,3},{1,2},{2,1},{3,0},{4,7},{5,6},{6,5},{7,4},{8,11},{9,10},{10,... | collective-permute-start | bytes 1179656 | tf_op jit(solution)/shard_map/ppermute | solution.py:376
  259.5 17.6 %all-to-all-start.10 = ((bf16[16,3,32,256]{3,2,1,0:T(8,128)(2,1)}), bf16[16,3,32,256]{3,2,1,0:T(8,128)(2,1)S(1)}, u32[]{:S(2)}, u32[]{:S(2)}) async-start(bf16[16,3,32,256]{3,2,1,0:T(8,128)(2,1)} %trace_blocks.1), calls=%async_computation.10 | async-start | bytes 1572864 | tf_op jit(solution)/shard_map/all_to_all | solution.py:372
  266.4 11.0 %copy-start.5 = (f32[32,48,256]{2,1,0:T(8,128)S(1)}, f32[32,48,256]{2,1,0:T(8,128)}, u32[]{:S(2)}) copy-start(f32[32,48,256]{2,1,0:T(8,128)} %param.8) | copy-start | bytes 4718596

commit v6 on v5

--- a/solution.py
+++ b/solution.py
@@ -368,6 +368,34 @@
     )
 
 
+def sum_kernel(samples_ref, focus_ref, out_ref, sums, sems):
+    groups, count, share, width = samples_ref.shape
+    half = share // 2
+    copies = []
+    for i in range(2):
+        at = slice(i * half, (i + 1) * half)
+        samples = samples_ref[:, :, at].reshape(groups * count, half, width).astype(jnp.float32)
+        sums[at] = focus_ref[at] + jnp.swapaxes(samples, 0, 1)
+        copies.append(pltpu.make_async_copy(sums.at[at], out_ref.at[at], sems.at[i]))
+        copies[-1].start()
+    for copy in copies:
+        copy.wait()
+
+
+def focus_sum(samples, focus_init):
+    size = 2 * focus_init.size * focus_init.dtype.itemsize
+    return pl.pallas_call(
+        sum_kernel,
+        in_specs=[IN_VMEM, IN_VMEM],
+        out_specs=pl.BlockSpec(memory_space=pltpu.HBM),
+        out_shape=jax.ShapeDtypeStruct(focus_init.shape, focus_init.dtype),
+        scratch_shapes=[pltpu.VMEM(focus_init.shape, focus_init.dtype), pltpu.SemaphoreType.DMA((2,))],
+        compiler_params=pltpu.CompilerParams(vmem_limit_bytes=16 * MIB),
+        cost_estimate=pl.CostEstimate(flops=focus_init.size, bytes_accessed=size, transcendentals=0),
+        name="focus_sum",
+    )(samples, focus_init)
+
+
 def exchange(blocks, axis):
     return lax.all_to_all(blocks, axis, split_axis=0, concat_axis=0, tiled=True)
 
@@ -426,7 +454,7 @@
         if last:
             upgoing = in_time(upgoing)
             traces = trace_blocks(returns, onsets, inverse, rows, count)
-            focusing = focus_init + in_time(exchange(traces, "freq"))
+            focusing = focus_sum(exchange(traces, "freq"), focus_init)
         else:
             blocks = focus_blocks(returns, first, onsets, tables, rows)
     return (focusing, upgoing)

time: 280 us -> 279 us (level)
  transfers between devices with their start and end apart: 30 -> 30, of which waited for: 18 -> 19; matrix products, arithmetic and copies ran while one was open for 1% -> 1% of each run, Pallas kernels for 9% -> 9%
where the time goes in v6:
time: 279 us
  blocking collectives  125 us (45%)
  waiting for transfers between devices  56.3 us (20%)
  starting transfers between devices  49.4 us (18%)
  Pallas kernels  41.1 us (15%)
  local copies, waits for them, and re-layouts  3.22 us (1%)
    all_to_all x9, blocking collectives, exchange(): return lax.all_to_all(blocks, axis, split_axis=0, concat_axis=0, tiled=True)  125 us
    ppermute x28, waiting for transfers between devices, send(): lax.ppermute(block, 'panel', [(i, i ^ k) for i in range(lax.axis_size('pa...  45.5 us
    pallas_call x16, Pallas kernels, call(): pl.pallas_call(kernel, in_specs=specs or [IN_VMEM] * len(args), out_specs...  39.7 us
    ppermute x28, starting transfers between devices, send(): lax.ppermute(block, 'panel', [(i, i ^ k) for i in range(lax.axis_size('pa...  39.7 us
    all_to_all x2, waiting for transfers between devices, exchange(): return lax.all_to_all(blocks, axis, split_axis=0, concat_axis=0, tiled=True)  10.8 us
    all_to_all x2, starting transfers between devices, exchange(): return lax.all_to_all(blocks, axis, split_axis=0, concat_axis=0, tiled=True)  9.7 us
  transfers between devices with their start and end apart: 30, of which 19 were waited for; matrix products, arithmetic and copies ran while one was open for 1% of the time, Pallas kernels for 9%

profile of v6, /device:TPU:1, one launch (start us, length us, event | category | flops | bytes accessed | tf_op | source)
XLA Modules:
  0.0 278.8 jit_solution(8011602527618887470)
XLA Ops:
  0.7 1.5 convert_element_type.90
  2.5 19.5 %all_to_all.55.traces_ref = bf16[16,3,32,256]{3,2,1,0:T(8,128)(2,1)S(1)} all-to-all(bf16[16,3,32,256]{3,2,1,0:T(8,128)(2,1)S(1)} %bitcast.7), channel_id=1, replica_groups=mesh['freq'=16,'panel'=8] {'freq'}, dimensions={0} | all-to-all | bytes 1572864 | tf_op jit(solution)/shard_map/all_to_all | solution.py:400
  22.5 11.9 %all_to_all.56.refs_0_ = bf16[16,48,256]{2,1,0:T(8,128)(2,1)S(1)} all-to-all(bf16[16,48,256]{2,1,0:T(8,128)(2,1)S(1)} %get-tuple-element.31), channel_id=1, replica_groups=mesh['freq'=16,'panel'=8] {'freq'}, dimensions={0} | all-to-all | bytes 786432 | tf_op jit(solution)/shard_map/all_to_all | solution.py:400
  34.4 3.2 %image_blocks.6 = (bf16[16,48,256]{2,1,0:T(8,128)(2,1)S(1)}, bf16[16,48,256]{2,1,0:T(8,128)(2,1)S(1)}, bf16[8,96,256]{2,1,0:T(8,128)(2,1)S(1)}, bf16[8,96,256]{2...) custom-call(bf16[16,48,256]{2,1,0:T(8,128)(2,1)S(1)} %all_to_all.56.refs_0_, bf16[2,8,2048,256]{3,2,1,0:T(8,128)(2,1)} %refl_ref.1), custom_call_target="tpu_custom_call" | custom-call | flops 402653184 | bytes 34340864 | tf_op jit(solution)/shard_map/image_blocks/pallas_call | solution.py:139
  37.7 3.8 %collective-permute-start.5 = (bf16[16,48,256]{2,1,0:T(8,128)(2,1)S(1)}, bf16[16,48,256]{2,1,0:T(8,128)(2,1)S(1)}, u32[]{:S(2)}, u32[]{:S(2)}) collective-permute-start(bf16[16,48,256]{2,1,0:T(8,128)(2,1)S(1)} %get-tuple-element.41), channel_id=1, source_target_pairs={{0,3},{1,2},{2,1},{3,0},{4,7},{5,6},{6,5},{7,4},{8,11},{9,10},{10,... | collective-permute-start | bytes 1179656 | tf_op jit(solution)/shard_map/ppermute | solution.py:404
  41.5 4.0 %image_blocks.8 = (bf16[16,48,256]{2,1,0:T(8,128)(2,1)S(1)}, bf16[16,48,256]{2,1,0:T(8,128)(2,1)S(1)}, bf16[16,48,256]{2,1,0:T(8,128)(2,1)S(1)}) custom-call(bf16[8,96,256]{2,1,0:T(8,128)(2,1)S(1)} %get-tuple-element.32.refs_0_, bf16[8,96,256]{2,1,0:T(8,128)(2,1)S(1)} %get-tuple-element.33.refs_1_, bf16[2,8,2048,256]{3,2,1,0:T(8,128)(2,1)} %refl_ref.1), custom_call_target="tpu_custom_call" | custom-call | flops 603979776 | bytes 35127296 | tf_op jit(solution)/shard_map/image_blocks/pallas_call | solution.py:139
  45.6 2.5 collective-permute-start.2
  48.3 1.2 collective-permute-start
  49.6 4.7 %image_blocks.7 = (bf16[16,48,256]{2,1,0:T(8,128)(2,1)S(1)}, bf16[16,48,256]{2,1,0:T(8,128)(2,1)S(1)}, bf16[16,48,256]{2,1,0:T(8,128)(2,1)S(1)}, bf16[2,8,1536,256]{3,2,1,0:T(8,128)(2,1)S(1)}) custom-call(bf16[8,96,256]{2,1,0:T(8,128)(2,1)S(1)} %get-tuple-element.32.refs_0_, bf16[8,96,256]{2,1,0:T(8,128)(2,1)S(1)} %get-tuple-element.33.refs_1_, ...), custom_call_target="tpu_custom_call" | custom-call | flops 603979776 | bytes 35127296 | tf_op jit(solution)/shard_map/image_blocks/pallas_call | solution.py:139
  54.5 0.6 collective-permute-start.6
  55.1 1.2 collective-permute-done.2
  56.4 1.4 collective-permute-start.3
  58.2 1.3 collective-permute-done
  59.5 4.9 %collective-permute-done.6 = bf16[16,48,256]{2,1,0:T(8,128)(2,1)S(1)} collective-permute-done((bf16[16,48,256]{2,1,0:T(8,128)(2,1)S(1)}, bf16[16,48,256]{2,1,0:T(8,128)(2,1)S(1)}, u32[]{:S(2)}, u32[]{:S(2)}) %collective-permute-start.6) | collective-permute-done | bytes 393248 | tf_op jit(solution)/shard_map/ppermute | solution.py:404
  64.4 3.6 %collective-permute-done.3 = bf16[16,48,256]{2,1,0:T(8,128)(2,1)S(1)} collective-permute-done((bf16[16,48,256]{2,1,0:T(8,128)(2,1)S(1)}, bf16[16,48,256]{2,1,0:T(8,128)(2,1)S(1)}, u32[]{:S(2)}, u32[]{:S(2)}) %collective-permute-start.3) | collective-permute-done | bytes 393248 | tf_op jit(solution)/shard_map/ppermute | solution.py:404
  68.2 14.0 %all_to_all.57.refs_5_ = bf16[16,48,256]{2,1,0:T(8,128)(2,1)S(1)} all-to-all(bf16[16,48,256]{2,1,0:T(8,128)(2,1)S(1)} %add_convert_fusion.3), channel_id=1, replica_groups=mesh['freq'=16,'panel'=8] {'freq'}, dimensions={0} | all-to-all | bytes 786432 | tf_op jit(solution)/shard_map/all_to_all | solution.py:400
  82.3 1.5 upgoing_blocks.2
  83.8 12.1 %all_to_all.58.refs_4_ = bf16[16,48,256]{2,1,0:T(8,128)(2,1)S(1)} all-to-all(bf16[16,48,256]{2,1,0:T(8,128)(2,1)S(1)} %upgoing_blocks.2), channel_id=1, replica_groups=mesh['freq'=16,'panel'=8] {'freq'}, dimensions={0} | all-to-all | bytes 786432 | tf_op jit(solution)/shard_map/all_to_all | solution.py:400
  95.9 1.3 collective-permute-start.10
  97.2 2.4 collective-permute-start.7
  99.6 2.3 collective-permute-start.11
  101.9 5.0 %collective-permute-done.10.refs_0_ = bf16[16,48,256]{2,1,0:T(8,128)(2,1)S(1)} collective-permute-done((bf16[16,48,256]{2,1,0:T(8,128)(2,1)S(1)}, bf16[16,48,256]{2,1,0:T(8,128)(2,1)S(1)}, u32[]{:S(2)}, u32[]{:S(2)}) %collective-permute-start.10) | collective-permute-done | bytes 393248 | tf_op jit(solution)/shard_map/ppermute | solution.py:404
  106.9 2.4 collective-permute-start.13
  109.3 1.2 collective-permute-start.8
  111.0 5.8 %collective-permute-done.11.refs_1_ = bf16[16,48,256]{2,1,0:T(8,128)(2,1)S(1)} collective-permute-done((bf16[16,48,256]{2,1,0:T(8,128)(2,1)S(1)}, bf16[16,48,256]{2,1,0:T(8,128)(2,1)S(1)}, u32[]{:S(2)}, u32[]{:S(2)}) %collective-permute-start.11) | collective-permute-done | bytes 393248 | tf_op jit(solution)/shard_map/ppermute | solution.py:404
  116.9 2.7 return_blocks.4.refs_3_
  119.6 3.4 %collective-permute-done.8.refs_0_ = bf16[16,48,256]{2,1,0:T(8,128)(2,1)S(1)} collective-permute-done((bf16[16,48,256]{2,1,0:T(8,128)(2,1)S(1)}, bf16[16,48,256]{2,1,0:T(8,128)(2,1)S(1)}, u32[]{:S(2)}, u32[]{:S(2)}) %collective-permute-start.8) | collective-permute-done | bytes 393248 | tf_op jit(solution)/shard_map/ppermute | solution.py:404
  123.1 1.3 return_blocks.5
  124.4 14.1 %all_to_all.59.refs_6_ = bf16[16,48,256]{2,1,0:T(8,128)(2,1)S(1)} all-to-all(bf16[16,48,256]{2,1,0:T(8,128)(2,1)S(1)} %return_blocks.5), channel_id=1, replica_groups=mesh['freq'=16,'panel'=8] {'freq'}, dimensions={0} | all-to-all | bytes 786432 | tf_op jit(solution)/shard_map/all_to_all | solution.py:400
  138.5 1.5 focus_blocks.1
  140.0 12.1 %all_to_all.60.refs_0_ = bf16[16,48,256]{2,1,0:T(8,128)(2,1)S(1)} all-to-all(bf16[16,48,256]{2,1,0:T(8,128)(2,1)S(1)} %focus_blocks.1), channel_id=1, replica_groups=mesh['freq'=16,'panel'=8] {'freq'}, dimensions={0} | all-to-all | bytes 786432 | tf_op jit(solution)/shard_map/all_to_all | solution.py:400
  152.1 1.5 image_blocks.9
  153.6 1.8 collective-permute-start.19
  155.4 2.1 image_blocks.11
  157.5 2.5 collective-permute-start.16
  160.1 1.5 collective-permute-start.15
  161.9 2.1 image_blocks.10
  164.7 2.5 collective-permute-start.20
  167.2 1.0 collective-permute-done.16
  168.3 2.1 collective-permute-start.17
  170.3 2.4 collective-permute-done.15
  173.0 2.1 collective-permute-done.20
  175.0 7.1 %collective-permute-done.17 = bf16[16,48,256]{2,1,0:T(8,128)(2,1)S(1)} collective-permute-done((bf16[16,48,256]{2,1,0:T(8,128)(2,1)S(1)}, bf16[16,48,256]{2,1,0:T(8,128)(2,1)S(1)}, u32[]{:S(2)}, u32[]{:S(2)}) %collective-permute-start.17) | collective-permute-done | bytes 393248 | tf_op jit(solution)/shard_map/ppermute | solution.py:404
  182.4 13.8 %all_to_all.61.refs_5_ = bf16[16,48,256]{2,1,0:T(8,128)(2,1)S(1)} all-to-all(bf16[16,48,256]{2,1,0:T(8,128)(2,1)S(1)} %add_convert_fusion), channel_id=1, replica_groups=mesh['freq'=16,'panel'=8] {'freq'}, dimensions={0} | all-to-all | bytes 786432 | tf_op jit(solution)/shard_map/all_to_all | solution.py:400
  196.2 2.2 upgoing_blocks.3
  198.3 12.1 %all_to_all.62.refs_4_ = bf16[16,48,256]{2,1,0:T(8,128)(2,1)S(1)} all-to-all(bf16[16,48,256]{2,1,0:T(8,128)(2,1)S(1)} %get-tuple-element.54), channel_id=1, replica_groups=mesh['freq'=16,'panel'=8] {'freq'}, dimensions={0} | all-to-all | bytes 786432 | tf_op jit(solution)/shard_map/all_to_all | solution.py:400
  210.4 0.8 collective-permute-start.21
  211.2 2.4 collective-permute-start.23
  213.6 5.1 %all-to-all-start.8 = ((bf16[16,3,32,256]{3,2,1,0:T(8,128)(2,1)}), bf16[16,3,32,256]{3,2,1,0:T(8,128)(2,1)S(1)}, u32[]{:S(2)}, u32[]{:S(2)}) async-start(bf16[16,3,32,256]{3,2,1,0:T(8,128)(2,1)} %get-tuple-element.55), calls=%async_computation.8 | async-start | bytes 1572864 | tf_op jit(solution)/shard_map/all_to_all | solution.py:400
  218.7 1.5 collective-permute-start.26
  220.6 0.8 collective-permute-done.21.refs_0_
  221.4 2.3 collective-permute-start.22
  223.8 1.7 collective-permute-start.25
  225.5 5.6 %collective-permute-done.26.refs_1_ = bf16[16,48,256]{2,1,0:T(8,128)(2,1)S(1)} collective-permute-done((bf16[16,48,256]{2,1,0:T(8,128)(2,1)S(1)}, bf16[16,48,256]{2,1,0:T(8,128)(2,1)S(1)}, u32[]{:S(2)}, u32[]{:S(2)}) %collective-permute-start.26) | collective-permute-done | bytes 393248 | tf_op jit(solution)/shard_map/ppermute | solution.py:404
  231.1 5.6 %return_blocks.6.refs_4_ = f32[8,96,256]{2,1,0:T(8,128)S(1)} custom-call(bf16[16,48,256]{2,1,0:T(8,128)(2,1)S(1)} %collective-permute-done.21.refs_0_, bf16[16,48,256]{2,1,0:T(8,128)(2,1)S(1)} %collective-permute-done.26.refs_1_, bf16[16,48,256]{2,1,0:T(8,128)(2,1)S(1)} %collective-permute-done.27.refs_2_, ...), custom_call_target="tpu_custom_call" | custom-call | flops 1006632960 | bytes 37486592 | tf_op jit(solution)/shard_map/return_blocks/pallas_call | solution.py:139
  236.7 2.9 %fetch_last.1.refs_3_ = bf16[2,8,768,256]{3,2,1,0:T(8,128)(2,1)S(1)} custom-call(bf16[2,8,2048,256]{3,2,1,0:T(8,128)(2,1)} %refl_ref.1, bf16[16,3,32,256]{3,2,1,0:T(8,128)(2,1)S(1)} %all-to-all-done.8._), custom_call_target="tpu_custom_call" | custom-call | bytes 35127296 | tf_op jit(solution)/shard_map/fetch_last/pallas_call | solution.py:139
  239.7 2.8 %return_blocks.7 = bf16[16,48,256]{2,1,0:T(8,128)(2,1)S(1)} custom-call(bf16[16,48,256]{2,1,0:T(8,128)(2,1)S(1)} %collective-permute-done.22.refs_0_, bf16[16,48,256]{2,1,0:T(8,128)(2,1)} %collective-permute-done.24.refs_1_, bf16[16,48,256]{2,1,0:T(8,128)(2,1)} %collective-permute-done.25.refs_2_, bf16[2,8,768,256]{3,2,1,0:T(8,128)(2,1)S(1)} %fetch_last.1.refs_3_, ...), custom_call_target="tpu_custom_call" | custom-call | flops 603979776 | bytes 16515072 | tf_op jit(solution)/shard_map/return_blocks/pallas_call | solution.py:139
  242.5 15.4 %all_to_all.63.refs_3_ = bf16[16,48,256]{2,1,0:T(8,128)(2,1)S(1)} all-to-all(bf16[16,48,256]{2,1,0:T(8,128)(2,1)S(1)} %return_blocks.7), channel_id=1, replica_groups=mesh['freq'=16,'panel'=8] {'freq'}, dimensions={0} | all-to-all | bytes 786432 | tf_op jit(solution)/shard_map/all_to_all | solution.py:400
  258.0 0.7 trace_blocks.1
  258.7 0.9 copy-done.5
  259.6 4.6 %all-to-all-start.10 = ((bf16[16,3,32,256]{3,2,1,0:T(8,128)(2,1)}), bf16[16,3,32,256]{3,2,1,0:T(8,128)(2,1)S(1)}, u32[]{:S(2)}, u32[]{:S(2)}) async-start(bf16[16,3,32,256]{3,2,1,0:T(8,128)(2,1)} %copy-done.5), calls=%async_computation.10 | async-start | bytes 1572864 | tf_op jit(solution)/shard_map/all_to_all | solution.py:400
  264.3 2.1 copy.10
  266.4 10.8 %all-to-all-done.10.samples_ref = bf16[16,3,32,256]{3,2,1,0:T(8,128)(2,1)S(1)} async-done(((bf16[16,3,32,256]{3,2,1,0:T(8,128)(2,1)}), bf16[16,3,32,256]{3,2,1,0:T(8,128)(2,1)S(1)}, u32[]{:S(2)}, u32[]{:S(2)}) %all-to-all-start.10) | async-done | bytes 786464 | tf_op jit(solution)/shard_map/all_to_all | solution.py:400
  277.2 1.4 focus_sum.1
  (46 shorter events, 4.7 us)
Async XLA Ops:
  0.6 21.3 %copy-start.1 = (bf16[256,512]{1,0:T(8,128)(2,1)S(1)}, bf16[256,512]{1,0:T(8,128)(2,1)}, u32[]{:S(2)}) copy-start(bf16[256,512]{1,0:T(8,128)(2,1)} %constant.8.clone.high.refs_2_) | copy-start | bytes 786436
  0.6 21.3 %copy-start.2 = (bf16[256,512]{1,0:T(8,128)(2,1)S(1)}, bf16[256,512]{1,0:T(8,128)(2,1)}, u32[]{:S(2)}) copy-start(bf16[256,512]{1,0:T(8,128)(2,1)} %constant.9.clone.low.refs_3_) | copy-start | bytes 786436
  37.7 16.7 %collective-permute-start.5 = (bf16[16,48,256]{2,1,0:T(8,128)(2,1)S(1)}, bf16[16,48,256]{2,1,0:T(8,128)(2,1)S(1)}, u32[]{:S(2)}, u32[]{:S(2)}) collective-permute-start(bf16[16,48,256]{2,1,0:T(8,128)(2,1)S(1)} %get-tuple-element.41), channel_id=1, source_target_pairs={{0,3},{1,2},{2,1},{3,0},{4,7},{5,6},{6,5},{7,4},{8,11},{9,10},{10,... | collective-permute-start | bytes 1179656 | tf_op jit(solution)/shard_map/ppermute | solution.py:404
  41.5 12.8 %collective-permute-start.4 = (bf16[16,48,256]{2,1,0:T(8,128)(2,1)S(1)}, bf16[16,48,256]{2,1,0:T(8,128)(2,1)S(1)}, u32[]{:S(2)}, u32[]{:S(2)}) collective-permute-start(bf16[16,48,256]{2,1,0:T(8,128)(2,1)S(1)} %get-tuple-element.40), channel_id=1, source_target_pairs={{0,1},{1,0},{2,3},{3,2},{4,5},{5,4},{6,7},{7,6},{8,9},{9,8},{10,11... | collective-permute-start | bytes 1179656 | tf_op jit(solution)/shard_map/ppermute | solution.py:404
  45.6 10.7 %collective-permute-start.2 = (bf16[16,48,256]{2,1,0:T(8,128)(2,1)S(1)}, bf16[16,48,256]{2,1,0:T(8,128)(2,1)S(1)}, u32[]{:S(2)}, u32[]{:S(2)}) collective-permute-start(bf16[16,48,256]{2,1,0:T(8,128)(2,1)S(1)} %get-tuple-element.38), channel_id=1, source_target_pairs={{0,4},{1,5},{2,6},{3,7},{4,0},{5,1},{6,2},{7,3},{8,12},{9,13},{10,... | collective-permute-start | bytes 1179656 | tf_op jit(solution)/shard_map/ppermute | solution.py:404
  48.1 10.1 %collective-permute-start.1 = (bf16[16,48,256]{2,1,0:T(8,128)(2,1)S(1)}, bf16[16,48,256]{2,1,0:T(8,128)(2,1)S(1)}, u32[]{:S(2)}, u32[]{:S(2)}) collective-permute-start(bf16[16,48,256]{2,1,0:T(8,128)(2,1)S(1)} %get-tuple-element.36), channel_id=1, source_target_pairs={{0,3},{1,2},{2,1},{3,0},{4,7},{5,6},{6,5},{7,4},{8,11},{9,10},{10,... | collective-permute-start | bytes 1179656 | tf_op jit(solution)/shard_map/ppermute | solution.py:404
  48.3 11.2 %collective-permute-start = (bf16[16,48,256]{2,1,0:T(8,128)(2,1)S(1)}, bf16[16,48,256]{2,1,0:T(8,128)(2,1)S(1)}, u32[]{:S(2)}, u32[]{:S(2)}) collective-permute-start(bf16[16,48,256]{2,1,0:T(8,128)(2,1)S(1)} %get-tuple-element.35), channel_id=1, source_target_pairs={{0,1},{1,0},{2,3},{3,2},{4,5},{5,4},{6,7},{7,6},{8,9},{9,8},{10,11... | collective-permute-start | bytes 1179656 | tf_op jit(solution)/shard_map/ppermute | solution.py:404
  54.3 28.0 %copy-start.3 = (bf16[512,256]{1,0:T(8,128)(2,1)S(1)}, bf16[512,256]{1,0:T(8,128)(2,1)}, u32[]{:S(2)}) copy-start(bf16[512,256]{1,0:T(8,128)(2,1)} %constant.10.clone.refs_0_) | copy-start | bytes 786436
  54.3 28.0 %copy-start.4 = (bf16[512,256]{1,0:T(8,128)(2,1)S(1)}, bf16[512,256]{1,0:T(8,128)(2,1)}, u32[]{:S(2)}) copy-start(bf16[512,256]{1,0:T(8,128)(2,1)} %constant.11.clone.refs_1_) | copy-start | bytes 786436
  54.3 28.0 %copy-start.6 = (s32[48,256]{1,0:T(8,128)S(1)}, s32[48,256]{1,0:T(8,128)}, u32[]{:S(2)}) copy-start(s32[48,256]{1,0:T(8,128)} %refs_2_.8) | copy-start | bytes 147460
  54.5 9.9 %collective-permute-start.6 = (bf16[16,48,256]{2,1,0:T(8,128)(2,1)S(1)}, bf16[16,48,256]{2,1,0:T(8,128)(2,1)S(1)}, u32[]{:S(2)}, u32[]{:S(2)}) collective-permute-start(bf16[16,48,256]{2,1,0:T(8,128)(2,1)S(1)} %add_convert_fusion.4), channel_id=1, source_target_pairs={{0,4},{1,5},{2,6},{3,7},{4,0},{5,1},{6,2},{7,3},{8,12},{9,13},{10,... | collective-permute-start | bytes 1179656 | tf_op jit(solution)/shard_map/ppermute | solution.py:404
  56.4 11.6 %collective-permute-start.3 = (bf16[16,48,256]{2,1,0:T(8,128)(2,1)S(1)}, bf16[16,48,256]{2,1,0:T(8,128)(2,1)S(1)}, u32[]{:S(2)}, u32[]{:S(2)}) collective-permute-start(bf16[16,48,256]{2,1,0:T(8,128)(2,1)S(1)} %add_convert_fusion.5), channel_id=1, source_target_pairs={{0,2},{1,3},{2,0},{3,1},{4,6},{5,7},{6,4},{7,5},{8,10},{9,11},{10,... | collective-permute-start | bytes 1179656 | tf_op jit(solution)/shard_map/ppermute | solution.py:404
  95.9 11.0 %collective-permute-start.10 = (bf16[16,48,256]{2,1,0:T(8,128)(2,1)S(1)}, bf16[16,48,256]{2,1,0:T(8,128)(2,1)S(1)}, u32[]{:S(2)}, u32[]{:S(2)}) collective-permute-start(bf16[16,48,256]{2,1,0:T(8,128)(2,1)S(1)} %all_to_all.58.refs_4_), channel_id=1, source_target_pairs={{0,2},{1,3},{2,0},{3,1},{4,6},{5,7},{6,4},{7,5},{8,10},{9,11},{10,... | collective-permute-start | bytes 1179656 | tf_op jit(solution)/shard_map/ppermute | solution.py:404
  97.2 12.1 %collective-permute-start.7 = (bf16[16,48,256]{2,1,0:T(8,128)(2,1)S(1)}, bf16[16,48,256]{2,1,0:T(8,128)(2,1)S(1)}, u32[]{:S(2)}, u32[]{:S(2)}) collective-permute-start(bf16[16,48,256]{2,1,0:T(8,128)(2,1)S(1)} %all_to_all.58.refs_4_), channel_id=1, source_target_pairs={{0,4},{1,5},{2,6},{3,7},{4,0},{5,1},{6,2},{7,3},{8,12},{9,13},{10,... | collective-permute-start | bytes 1179656 | tf_op jit(solution)/shard_map/ppermute | solution.py:404
  99.6 17.3 %collective-permute-start.11 = (bf16[16,48,256]{2,1,0:T(8,128)(2,1)S(1)}, bf16[16,48,256]{2,1,0:T(8,128)(2,1)S(1)}, u32[]{:S(2)}, u32[]{:S(2)}) collective-permute-start(bf16[16,48,256]{2,1,0:T(8,128)(2,1)S(1)} %all_to_all.58.refs_4_), channel_id=1, source_target_pairs={{0,3},{1,2},{2,1},{3,0},{4,7},{5,6},{6,5},{7,4},{8,11},{9,10},{10,... | collective-permute-start | bytes 1179656 | tf_op jit(solution)/shard_map/ppermute | solution.py:404
  101.9 15.0 %collective-permute-start.12 = (bf16[16,48,256]{2,1,0:T(8,128)(2,1)S(1)}, bf16[16,48,256]{2,1,0:T(8,128)(2,1)S(1)}, u32[]{:S(2)}, u32[]{:S(2)}) collective-permute-start(bf16[16,48,256]{2,1,0:T(8,128)(2,1)S(1)} %all_to_all.58.refs_4_), channel_id=1, source_target_pairs={{0,1},{1,0},{2,3},{3,2},{4,5},{5,4},{6,7},{7,6},{8,9},{9,8},{10,11... | collective-permute-start | bytes 1179656 | tf_op jit(solution)/shard_map/ppermute | solution.py:404
  106.9 10.0 %collective-permute-start.13 = (bf16[16,48,256]{2,1,0:T(8,128)(2,1)S(1)}, bf16[16,48,256]{2,1,0:T(8,128)(2,1)S(1)}, u32[]{:S(2)}, u32[]{:S(2)}) collective-permute-start(bf16[16,48,256]{2,1,0:T(8,128)(2,1)S(1)} %collective-permute-done.10.refs_0_), channel_id=1, source_target_pairs={{0,4},{1,5},{2,6},{3,7},{4,0},{5,1},{6,2},{7,3},{8,12},{9,13},{10,... | collective-permute-start | bytes 1179656 | tf_op jit(solution)/shard_map/ppermute | solution.py:404
  109.3 13.7 %collective-permute-start.8 = (bf16[16,48,256]{2,1,0:T(8,128)(2,1)S(1)}, bf16[16,48,256]{2,1,0:T(8,128)(2,1)S(1)}, u32[]{:S(2)}, u32[]{:S(2)}) collective-permute-start(bf16[16,48,256]{2,1,0:T(8,128)(2,1)S(1)} %collective-permute-done.7.refs_3_), channel_id=1, source_target_pairs={{0,1},{1,0},{2,3},{3,2},{4,5},{5,4},{6,7},{7,6},{8,9},{9,8},{10,11... | collective-permute-start | bytes 1179656 | tf_op jit(solution)/shard_map/ppermute | solution.py:404
  110.5 12.6 %collective-permute-start.9 = (bf16[16,48,256]{2,1,0:T(8,128)(2,1)S(1)}, bf16[16,48,256]{2,1,0:T(8,128)(2,1)S(1)}, u32[]{:S(2)}, u32[]{:S(2)}) collective-permute-start(bf16[16,48,256]{2,1,0:T(8,128)(2,1)S(1)} %collective-permute-done.7.refs_3_), channel_id=1, source_target_pairs={{0,3},{1,2},{2,1},{3,0},{4,7},{5,6},{6,5},{7,4},{8,11},{9,10},{10,... | collective-permute-start | bytes 1179656 | tf_op jit(solution)/shard_map/ppermute | solution.py:404
  153.6 10.7 %collective-permute-start.19 = (bf16[16,48,256]{2,1,0:T(8,128)(2,1)S(1)}, bf16[16,48,256]{2,1,0:T(8,128)(2,1)S(1)}, u32[]{:S(2)}, u32[]{:S(2)}) collective-permute-start(bf16[16,48,256]{2,1,0:T(8,128)(2,1)S(1)} %get-tuple-element.53), channel_id=1, source_target_pairs={{0,3},{1,2},{2,1},{3,0},{4,7},{5,6},{6,5},{7,4},{8,11},{9,10},{10,... | collective-permute-start | bytes 1179656 | tf_op jit(solution)/shard_map/ppermute | solution.py:404
  155.4 9.2 %collective-permute-start.18 = (bf16[16,48,256]{2,1,0:T(8,128)(2,1)S(1)}, bf16[16,48,256]{2,1,0:T(8,128)(2,1)S(1)}, u32[]{:S(2)}, u32[]{:S(2)}) collective-permute-start(bf16[16,48,256]{2,1,0:T(8,128)(2,1)S(1)} %get-tuple-element.52), channel_id=1, source_target_pairs={{0,1},{1,0},{2,3},{3,2},{4,5},{5,4},{6,7},{7,6},{8,9},{9,8},{10,11... | collective-permute-start | bytes 1179656 | tf_op jit(solution)/shard_map/ppermute | solution.py:404
  157.5 10.7 %collective-permute-start.16 = (bf16[16,48,256]{2,1,0:T(8,128)(2,1)S(1)}, bf16[16,48,256]{2,1,0:T(8,128)(2,1)S(1)}, u32[]{:S(2)}, u32[]{:S(2)}) collective-permute-start(bf16[16,48,256]{2,1,0:T(8,128)(2,1)S(1)} %get-tuple-element.50), channel_id=1, source_target_pairs={{0,4},{1,5},{2,6},{3,7},{4,0},{5,1},{6,2},{7,3},{8,12},{9,13},{10,... | collective-permute-start | bytes 1179656 | tf_op jit(solution)/shard_map/ppermute | solution.py:404
  160.1 12.7 %collective-permute-start.15 = (bf16[16,48,256]{2,1,0:T(8,128)(2,1)S(1)}, bf16[16,48,256]{2,1,0:T(8,128)(2,1)S(1)}, u32[]{:S(2)}, u32[]{:S(2)}) collective-permute-start(bf16[16,48,256]{2,1,0:T(8,128)(2,1)S(1)} %get-tuple-element.48), channel_id=1, source_target_pairs={{0,3},{1,2},{2,1},{3,0},{4,7},{5,6},{6,5},{7,4},{8,11},{9,10},{10,... | collective-permute-start | bytes 1179656 | tf_op jit(solution)/shard_map/ppermute | solution.py:404
  161.6 11.4 %collective-permute-start.14 = (bf16[16,48,256]{2,1,0:T(8,128)(2,1)S(1)}, bf16[16,48,256]{2,1,0:T(8,128)(2,1)S(1)}, u32[]{:S(2)}, u32[]{:S(2)}) collective-permute-start(bf16[16,48,256]{2,1,0:T(8,128)(2,1)S(1)} %get-tuple-element.47), channel_id=1, source_target_pairs={{0,1},{1,0},{2,3},{3,2},{4,5},{5,4},{6,7},{7,6},{8,9},{9,8},{10,11... | collective-permute-start | bytes 1179656 | tf_op jit(solution)/shard_map/ppermute | solution.py:404
  164.7 10.3 %collective-permute-start.20 = (bf16[16,48,256]{2,1,0:T(8,128)(2,1)S(1)}, bf16[16,48,256]{2,1,0:T(8,128)(2,1)S(1)}, u32[]{:S(2)}, u32[]{:S(2)}) collective-permute-start(bf16[16,48,256]{2,1,0:T(8,128)(2,1)S(1)} %add_convert_fusion.1), channel_id=1, source_target_pairs={{0,4},{1,5},{2,6},{3,7},{4,0},{5,1},{6,2},{7,3},{8,12},{9,13},{10,... | collective-permute-start | bytes 1179656 | tf_op jit(solution)/shard_map/ppermute | solution.py:404
  168.3 13.8 %collective-permute-start.17 = (bf16[16,48,256]{2,1,0:T(8,128)(2,1)S(1)}, bf16[16,48,256]{2,1,0:T(8,128)(2,1)S(1)}, u32[]{:S(2)}, u32[]{:S(2)}) collective-permute-start(bf16[16,48,256]{2,1,0:T(8,128)(2,1)S(1)} %add_convert_fusion.2), channel_id=1, source_target_pairs={{0,2},{1,3},{2,0},{3,1},{4,6},{5,7},{6,4},{7,5},{8,10},{9,11},{10,... | collective-permute-start | bytes 1179656 | tf_op jit(solution)/shard_map/ppermute | solution.py:404
  210.4 11.0 %collective-permute-start.21 = (bf16[16,48,256]{2,1,0:T(8,128)(2,1)S(1)}, bf16[16,48,256]{2,1,0:T(8,128)(2,1)S(1)}, u32[]{:S(2)}, u32[]{:S(2)}) collective-permute-start(bf16[16,48,256]{2,1,0:T(8,128)(2,1)S(1)} %all_to_all.62.refs_4_), channel_id=1, source_target_pairs={{0,2},{1,3},{2,0},{3,1},{4,6},{5,7},{6,4},{7,5},{8,10},{9,11},{10,... | collective-permute-start | bytes 1179656 | tf_op jit(solution)/shard_map/ppermute | solution.py:404
  211.2 12.6 %collective-permute-start.23 = (bf16[16,48,256]{2,1,0:T(8,128)(2,1)S(1)}, bf16[16,48,256]{2,1,0:T(8,128)(2,1)}, u32[]{:S(2)}, u32[]{:S(2)}) collective-permute-start(bf16[16,48,256]{2,1,0:T(8,128)(2,1)S(1)} %all_to_all.62.refs_4_), channel_id=1, source_target_pairs={{0,4},{1,5},{2,6},{3,7},{4,0},{5,1},{6,2},{7,3},{8,12},{9,13},{10,... | collective-permute-start | bytes 1179656 | tf_op jit(solution)/shard_map/ppermute | solution.py:404
  213.6 23.1 %all-to-all-start.8 = ((bf16[16,3,32,256]{3,2,1,0:T(8,128)(2,1)}), bf16[16,3,32,256]{3,2,1,0:T(8,128)(2,1)S(1)}, u32[]{:S(2)}, u32[]{:S(2)}) async-start(bf16[16,3,32,256]{3,2,1,0:T(8,128)(2,1)} %get-tuple-element.55), calls=%async_computation.8 | async-start | bytes 1572864 | tf_op jit(solution)/shard_map/all_to_all | solution.py:400
  218.7 12.3 %collective-permute-start.26 = (bf16[16,48,256]{2,1,0:T(8,128)(2,1)S(1)}, bf16[16,48,256]{2,1,0:T(8,128)(2,1)S(1)}, u32[]{:S(2)}, u32[]{:S(2)}) collective-permute-start(bf16[16,48,256]{2,1,0:T(8,128)(2,1)S(1)} %all_to_all.62.refs_4_), channel_id=1, source_target_pairs={{0,3},{1,2},{2,1},{3,0},{4,7},{5,6},{6,5},{7,4},{8,11},{9,10},{10,... | collective-permute-start | bytes 1179656 | tf_op jit(solution)/shard_map/ppermute | solution.py:404
  220.3 10.8 %collective-permute-start.27 = (bf16[16,48,256]{2,1,0:T(8,128)(2,1)S(1)}, bf16[16,48,256]{2,1,0:T(8,128)(2,1)S(1)}, u32[]{:S(2)}, u32[]{:S(2)}) collective-permute-start(bf16[16,48,256]{2,1,0:T(8,128)(2,1)S(1)} %all_to_all.62.refs_4_), channel_id=1, source_target_pairs={{0,1},{1,0},{2,3},{3,2},{4,5},{5,4},{6,7},{7,6},{8,9},{9,8},{10,11... | collective-permute-start | bytes 1179656 | tf_op jit(solution)/shard_map/ppermute | solution.py:404
  221.4 18.2 %collective-permute-start.22 = (bf16[16,48,256]{2,1,0:T(8,128)(2,1)S(1)}, bf16[16,48,256]{2,1,0:T(8,128)(2,1)S(1)}, u32[]{:S(2)}, u32[]{:S(2)}) collective-permute-start(bf16[16,48,256]{2,1,0:T(8,128)(2,1)S(1)} %collective-permute-done.21.refs_0_), channel_id=1, source_target_pairs={{0,4},{1,5},{2,6},{3,7},{4,0},{5,1},{6,2},{7,3},{8,12},{9,13},{10,... | collective-permute-start | bytes 1179656 | tf_op jit(solution)/shard_map/ppermute | solution.py:404
  223.8 15.9 %collective-permute-start.24 = (bf16[16,48,256]{2,1,0:T(8,128)(2,1)}, bf16[16,48,256]{2,1,0:T(8,128)(2,1)}, u32[]{:S(2)}, u32[]{:S(2)}) collective-permute-start(bf16[16,48,256]{2,1,0:T(8,128)(2,1)} %collective-permute-done.23.refs_3_), channel_id=1, source_target_pairs={{0,1},{1,0},{2,3},{3,2},{4,5},{5,4},{6,7},{7,6},{8,9},{9,8},{10,11... | collective-permute-start | bytes 1179656 | tf_op jit(solution)/shard_map/ppermute | solution.py:404
  223.8 15.9 %collective-permute-start.25 = (bf16[16,48,256]{2,1,0:T(8,128)(2,1)}, bf16[16,48,256]{2,1,0:T(8,128)(2,1)}, u32[]{:S(2)}, u32[]{:S(2)}) collective-permute-start(bf16[16,48,256]{2,1,0:T(8,128)(2,1)} %collective-permute-done.23.refs_3_), channel_id=1, source_target_pairs={{0,3},{1,2},{2,1},{3,0},{4,7},{5,6},{6,5},{7,4},{8,11},{9,10},{10,... | collective-permute-start | bytes 1179656 | tf_op jit(solution)/shard_map/ppermute | solution.py:404
  258.0 19.3 %copy-start = (f32[32,48,256]{2,1,0:T(8,128)S(1)}, f32[32,48,256]{2,1,0:T(8,128)}, u32[]{:S(2)}) copy-start(f32[32,48,256]{2,1,0:T(8,128)} %focus_ref.1) | copy-start | bytes 4718596
  258.7 0.9 copy-start.5
  259.6 17.6 %all-to-all-start.10 = ((bf16[16,3,32,256]{3,2,1,0:T(8,128)(2,1)}), bf16[16,3,32,256]{3,2,1,0:T(8,128)(2,1)S(1)}, u32[]{:S(2)}, u32[]{:S(2)}) async-start(bf16[16,3,32,256]{3,2,1,0:T(8,128)(2,1)} %copy-done.5), calls=%async_computation.10 | async-start | bytes 1572864 | tf_op jit(solution)/shard_map/all_to_all | solution.py:400
